TPU v7x, 32 devices: a whole 2x2x4 slice. The times are simulated.
32 devices in a mesh: ctx: 8 (over z, x), ch: 4 (over y, core).
Axes of the slice: x: 2, y: 2, z: 4, core: 2. Of those that a mesh axis runs over, the one named last changes fastest.
Arguments:
- signal: bfloat16 [4096, 1024], P('ctx', 'ch'), may hold values from -6 to 6
- gate_v: bfloat16 [4096, 1024], P('ctx', 'ch'), may hold values from -6 to 6
- taps: float32 [4096, 1024], P('ctx', 'ch'), may hold values from -1 to 1
- skip: float32 [1024], P('ch'), may hold values from -1 to 1
- norm_gain: float32 [1024], replicated, may hold values from 0.5 to 1.5
- router: float32 [1024, 32], replicated, may hold values from -0.1875 to 0.1875
- w_up: bfloat16 [64, 1024, 256], P('ctx'), may hold values from -0.1875 to 0.1875
- w_down: bfloat16 [64, 256, 1024], P('ctx'), may hold values from -0.25 to 0.25
- routes: int32 [4096, 2], P(('ctx', 'ch')), may hold values from 0 to 31, all different within a row; in each aligned block of 128 rows (0 to 127, 128 to 255, ...) at most 16 rows name the same one
Outputs:
- mixed: bfloat16 [4096, 1024], P('ctx', 'ch')
- moe_out: bfloat16 [4096, 1024], P('ctx', 'ch')
Inputs may be any that keep to these rules, and one draw needn't show every extreme that they name: `routes`: each row names two different experts. In each aligned block of 128 rows no expert is named by more than 16 rows.
All inputs are finite; a program needn't handle non-finite values.
Results may differ from a plain program's by a relative error of at most 0.017.
Values may be sent and summed in bfloat16 or wider, within the bound.
No kernel may reach another device: no remote copies, remote signals or barrier semaphores. Data moves between devices by JAX's collectives and lax.ppermute only.
A program may use at most 64 MiB of HBM per device.

v0:
```python
import math

import jax
import jax.numpy as jnp
from jax import lax
from jax.sharding import PartitionSpec as P

CAP = 16


precise = lax.Precision.HIGHEST


def partner(block, axis, distance):
    count = lax.axis_size(axis)
    route = []
    for low in range(count):
        high = low | 1 << distance
        if high != low and high < count:
            route += [(low, high), (high, low)]
    return lax.ppermute(block, axis, route)


def dft_tables(length):
    index = jnp.arange(length, dtype=jnp.int32)
    angle = 2.0 * math.pi / length * (index[:, None] * index[None, :] % length).astype(jnp.float32)
    return (jnp.cos(angle), jnp.sin(angle))


def rotate(real_a, imag_a, real_b, imag_b):
    return (real_a * real_b - imag_a * imag_b, real_a * imag_b + imag_a * real_b)


def local_forward(real_part, imag_part, cosine, sine):
    out_real = jnp.matmul(real_part, cosine, precision=precise) + jnp.matmul(
        imag_part, sine, precision=precise
    )
    out_imag = jnp.matmul(imag_part, cosine, precision=precise) - jnp.matmul(
        real_part, sine, precision=precise
    )
    return (out_real, out_imag)


def local_inverse(real_part, imag_part, cosine, sine):
    count = cosine.shape[0]
    out_real = jnp.matmul(real_part, cosine, precision=precise) - jnp.matmul(
        imag_part, sine, precision=precise
    )
    out_imag = jnp.matmul(imag_part, cosine, precision=precise) + jnp.matmul(
        real_part, sine, precision=precise
    )
    return (out_real / count, out_imag / count)


def forward_pair(own_real, own_imag, far_real, far_imag, upper, tw_real, tw_imag):
    diff_real, diff_imag = rotate(far_real - own_real, far_imag - own_imag, tw_real, tw_imag)
    return (
        jnp.where(upper, diff_real, own_real + far_real),
        jnp.where(upper, diff_imag, own_imag + far_imag),
    )


def inverse_pair(own_real, own_imag, far_real, far_imag, upper, tw_real, tw_imag):
    first_real = jnp.where(upper, far_real, own_real)
    first_imag = jnp.where(upper, far_imag, own_imag)
    second_real = jnp.where(upper, own_real, far_real)
    second_imag = jnp.where(upper, own_imag, far_imag)
    turned_real, turned_imag = rotate(second_real, second_imag, tw_real, tw_imag)
    factor = jnp.where(upper, -0.5, 0.5)
    return (0.5 * first_real + factor * turned_real, 0.5 * first_imag + factor * turned_imag)


def body(signal, gate_v, taps, skip, norm_gain, router, w_up, w_down, routes):
    tok_dev, ch_dev = signal.shape
    shards = lax.axis_size("ctx")
    sections = shards.bit_length() - 1
    device = lax.axis_index("ctx")
    total = shards * tok_dev
    position = jnp.arange(tok_dev, dtype=jnp.int32)
    sig_float = signal.astype(jnp.float32)
    global_pos = (device * tok_dev + position).astype(jnp.float32)
    half_cos = jnp.cos(math.pi * global_pos / total)
    half_sin = jnp.sin(math.pi * global_pos / total)

    def lift(field):
        real_part = jnp.stack([field, field * half_cos], axis=1)
        imag_part = jnp.stack([jnp.zeros_like(field), -field * half_sin], axis=1)
        return (real_part, imag_part)

    sig_real, sig_imag = lift(sig_float.T)
    tap_real, tap_imag = lift(taps.T)
    cosine, sine = dft_tables(tok_dev)
    for level in reversed(range(sections)):
        span = 2**level * tok_dev
        offset = (device % 2**level * tok_dev + position).astype(jnp.float32)
        tw_real = jnp.cos(math.pi * offset / span)
        tw_imag = -jnp.sin(math.pi * offset / span)
        upper = device // 2**level % 2 == 1
        far = partner((sig_real, sig_imag, tap_real, tap_imag), "ctx", level)
        sig_real, sig_imag = forward_pair(
            sig_real, sig_imag, far[0], far[1], upper, tw_real, tw_imag
        )
        tap_real, tap_imag = forward_pair(
            tap_real, tap_imag, far[2], far[3], upper, tw_real, tw_imag
        )
    sig_real, sig_imag = local_forward(sig_real, sig_imag, cosine, sine)
    tap_real, tap_imag = local_forward(tap_real, tap_imag, cosine, sine)
    prod_real, prod_imag = rotate(sig_real, sig_imag, tap_real, tap_imag)
    prod_real, prod_imag = local_inverse(prod_real, prod_imag, cosine, sine)
    for level in range(sections):
        span = 2**level * tok_dev
        offset = (device % 2**level * tok_dev + position).astype(jnp.float32)
        tw_real = jnp.cos(math.pi * offset / span)
        tw_imag = jnp.sin(math.pi * offset / span)
        upper = device // 2**level % 2 == 1
        far = (
            partner(prod_real.astype(jnp.bfloat16), "ctx", level).astype(prod_real.dtype),
            partner(prod_imag.astype(jnp.bfloat16), "ctx", level).astype(prod_imag.dtype),
        )
        prod_real, prod_imag = inverse_pair(
            prod_real, prod_imag, far[0], far[1], upper, tw_real, tw_imag
        )
    low_half = 0.5 * (prod_real[:, 0] + prod_real[:, 1] * half_cos - prod_imag[:, 1] * half_sin)
    conv = low_half.T
    mixed = (gate_v.astype(jnp.float32) * (conv + skip * sig_float)).astype(jnp.bfloat16)
    full_rows = lax.all_to_all(mixed, "ch", split_axis=0, concat_axis=1, tiled=True)
    rows_float = full_rows.astype(jnp.float32)
    scale_row = lax.rsqrt(jnp.mean(rows_float * rows_float, axis=-1, keepdims=True) + 1e-05)
    normed = (rows_float * scale_row * norm_gain).astype(jnp.bfloat16)
    row_count, width = normed.shape
    num_experts = router.shape[1]
    logits = jnp.dot(normed.astype(jnp.float32), router, precision=precise)
    expert_ids = jnp.arange(num_experts, dtype=jnp.int32)
    picked_mask = routes[:, :, None] == expert_ids[None, None, :]
    gates = jax.nn.sigmoid(jnp.sum(jnp.where(picked_mask, logits[:, None, :], 0.0), axis=-1))
    flat_routes = routes.reshape(-1)
    flat_onehot = (flat_routes[:, None] == expert_ids[None, :]).astype(jnp.int32)
    slot_of = jnp.sum((jnp.cumsum(flat_onehot, axis=0) - flat_onehot) * flat_onehot, axis=-1)
    parts_dev = w_up.shape[0]
    part_ids = 2 * flat_routes[:, None] + jnp.arange(2, dtype=jnp.int32)[None, :]
    flat_pos = (
        part_ids // parts_dev * (parts_dev * CAP) + part_ids % parts_dev * CAP + slot_of[:, None]
    )
    flat_pos = flat_pos.reshape(-1)
    source_rows = jnp.repeat(jnp.arange(row_count, dtype=jnp.int32), 4)
    send_rows = (
        jnp.zeros((shards * parts_dev * CAP, width), jnp.bfloat16)
        .at[flat_pos]
        .set(normed[source_rows])
    )
    received = lax.all_to_all(
        send_rows.reshape(shards, parts_dev * CAP, width),
        "ctx",
        split_axis=0,
        concat_axis=0,
        tiled=True,
    )
    grouped = received.reshape(shards, parts_dev, CAP, width)
    hidden = jax.nn.gelu(
        jnp.einsum("spcd,pdh->spch", grouped, w_up, preferred_element_type=jnp.float32),
        approximate=True,
    ).astype(jnp.bfloat16)
    result = jnp.einsum(
        "spch,phd->spcd", hidden, w_down, preferred_element_type=jnp.float32
    ).astype(jnp.bfloat16)
    back = lax.all_to_all(
        result.reshape(shards, parts_dev * CAP, width),
        "ctx",
        split_axis=0,
        concat_axis=0,
        tiled=True,
    )
    picked = back.reshape(-1, width)[flat_pos].astype(jnp.float32).reshape(row_count, 2, 2, width)
    combined = jnp.sum(gates[:, :, None] * jnp.sum(picked, axis=2), axis=1)
    moe_rows = combined.astype(jnp.bfloat16)
    moe_out = lax.all_to_all(moe_rows, "ch", split_axis=1, concat_axis=0, tiled=True)
    return (mixed, moe_out)


def solution(mesh):
    in_specs = (
        P("ctx", "ch"),
        P("ctx", "ch"),
        P("ctx", "ch"),
        P("ch"),
        P(),
        P(),
        P("ctx", None, None),
        P("ctx", None, None),
        P(("ctx", "ch"), None),
    )
    out_specs = (P("ctx", "ch"), P("ctx", "ch"))
    return jax.shard_map(body, mesh=mesh, in_specs=in_specs, out_specs=out_specs, check_vma=False)
```

profile of v0, /device:TPU:0, one launch (start us, length us, event | category | flops | bytes accessed | tf_op | source)
XLA Modules:
  0.0 708.0 jit_solution(15154660657885639393)
XLA Ops:
  14.7 107.9 %collective-permute-done = f32[256,2,512]{2,0,1:T(8,128)} collective-permute-done((f32[256,2,512]{2,0,1:T(8,128)}, f32[256,2,512]{2,0,1:T(8,128)}, u32[]{:S(2)}, u32[]{:S(2)}) %collective-permute-start) | collective-permute-done | bytes 1048608 | tf_op jit(solution)/shard_map/ppermute | solution.py:21
  122.7 22.5 %collective-permute-done.6 = f32[256,2,512]{2,0,1:T(8,128)} collective-permute-done((f32[256,2,512]{2,0,1:T(8,128)}, f32[256,2,512]{2,0,1:T(8,128)}, u32[]{:S(2)}, u32[]{:S(2)}) %collective-permute-start.6) | collective-permute-done | bytes 1048608 | tf_op jit(solution)/shard_map/ppermute | solution.py:21
  145.1 22.5 %collective-permute-done.1 = f32[256,2,512]{2,0,1:T(8,128)} collective-permute-done((f32[256,2,512]{2,0,1:T(8,128)}, f32[256,2,512]{2,0,1:T(8,128)}, u32[]{:S(2)}, u32[]{:S(2)}) %collective-permute-start.1) | collective-permute-done | bytes 1048608 | tf_op jit(solution)/shard_map/ppermute | solution.py:21
  167.6 21.6 %collective-permute-done.7 = f32[256,2,512]{2,0,1:T(8,128)} collective-permute-done((f32[256,2,512]{2,0,1:T(8,128)}, f32[256,2,512]{2,0,1:T(8,128)}, u32[]{:S(2)}, u32[]{:S(2)}) %collective-permute-start.7) | collective-permute-done | bytes 1048608 | tf_op jit(solution)/shard_map/ppermute | solution.py:21
  198.5 22.2 %collective-permute-done.2 = f32[256,2,512]{2,0,1:T(8,128)S(1)} collective-permute-done((f32[256,2,512]{2,0,1:T(8,128)}, f32[256,2,512]{2,0,1:T(8,128)S(1)}, u32[]{:S(2)}, u32[]{:S(2)}) %collective-permute-start.2) | collective-permute-done | bytes 1048608 | tf_op jit(solution)/shard_map/ppermute | solution.py:21
  220.7 22.5 %collective-permute-done.3 = f32[256,2,512]{2,0,1:T(8,128)S(1)} collective-permute-done((f32[256,2,512]{2,0,1:T(8,128)}, f32[256,2,512]{2,0,1:T(8,128)S(1)}, u32[]{:S(2)}, u32[]{:S(2)}) %collective-permute-start.3) | collective-permute-done | bytes 1048608 | tf_op jit(solution)/shard_map/ppermute | solution.py:21
  243.2 22.5 %collective-permute-done.8 = f32[256,2,512]{2,0,1:T(8,128)S(1)} collective-permute-done((f32[256,2,512]{2,0,1:T(8,128)}, f32[256,2,512]{2,0,1:T(8,128)S(1)}, u32[]{:S(2)}, u32[]{:S(2)}) %collective-permute-start.8) | collective-permute-done | bytes 1048608 | tf_op jit(solution)/shard_map/ppermute | solution.py:21
  265.7 20.8 %collective-permute-done.9 = f32[256,2,512]{2,0,1:T(8,128)} collective-permute-done((f32[256,2,512]{2,0,1:T(8,128)}, f32[256,2,512]{2,0,1:T(8,128)}, u32[]{:S(2)}, u32[]{:S(2)}) %collective-permute-start.9) | collective-permute-done | bytes 1048608 | tf_op jit(solution)/shard_map/ppermute | solution.py:21
  296.3 22.1 %collective-permute-done.10 = f32[256,2,512]{2,0,1:T(8,128)} collective-permute-done((f32[256,2,512]{2,0,1:T(8,128)S(1)}, f32[256,2,512]{2,0,1:T(8,128)}, u32[]{:S(2)}, u32[]{:S(2)}) %collective-permute-start.10) | collective-permute-done | bytes 1048608 | tf_op jit(solution)/shard_map/ppermute | solution.py:21
  318.4 22.5 %collective-permute-done.11 = f32[256,2,512]{2,0,1:T(8,128)} collective-permute-done((f32[256,2,512]{2,0,1:T(8,128)S(1)}, f32[256,2,512]{2,0,1:T(8,128)}, u32[]{:S(2)}, u32[]{:S(2)}) %collective-permute-start.11) | collective-permute-done | bytes 1048608 | tf_op jit(solution)/shard_map/ppermute | solution.py:21
  340.9 22.5 %collective-permute-done.4 = f32[256,2,512]{2,0,1:T(8,128)} collective-permute-done((f32[256,2,512]{2,0,1:T(8,128)S(1)}, f32[256,2,512]{2,0,1:T(8,128)}, u32[]{:S(2)}, u32[]{:S(2)}) %collective-permute-start.4) | collective-permute-done | bytes 1048608 | tf_op jit(solution)/shard_map/ppermute | solution.py:21
  363.4 19.8 %collective-permute-done.5 = f32[256,2,512]{2,0,1:T(8,128)} collective-permute-done((f32[256,2,512]{2,0,1:T(8,128)}, f32[256,2,512]{2,0,1:T(8,128)}, u32[]{:S(2)}, u32[]{:S(2)}) %collective-permute-start.5) | collective-permute-done | bytes 1048608 | tf_op jit(solution)/shard_map/ppermute | solution.py:21
  405.9 6.6 fusion.51
  425.2 6.7 convolution_subtract_fusion.1
  431.9 6.5 multiply_subtract_fusion
  451.2 7.0 fusion.190
  459.5 7.0 fusion.189
  472.9 8.2 %collective-permute-done.13 = bf16[256,2,512]{2,0,1:T(8,128)(2,1)} collective-permute-done((bf16[256,2,512]{2,0,1:T(8,128)(2,1)}, bf16[256,2,512]{2,0,1:T(8,128)(2,1)}, u32[]{:S(2)}, u32[]{:S(2)}) %collective-permute-start.13) | collective-permute-done | bytes 524320 | tf_op jit(solution)/shard_map/ppermute | solution.py:21
  486.2 12.6 %collective-permute-done.14 = bf16[256,2,512]{2,0,1:T(8,128)(2,1)S(1)} collective-permute-done((bf16[256,2,512]{2,0,1:T(8,128)(2,1)S(1)}, bf16[256,2,512]{2,0,1:T(8,128)(2,1)S(1)}, u32[]{:S(2)}, u32[]{:S(2)}) %collective-permute-start.14) | collective-permute-done | bytes 524320 | tf_op jit(solution)/shard_map/ppermute | solution.py:21
  498.8 7.8 %collective-permute-done.15 = bf16[256,2,512]{2,0,1:T(8,128)(2,1)S(1)} collective-permute-done((bf16[256,2,512]{2,0,1:T(8,128)(2,1)S(1)}, bf16[256,2,512]{2,0,1:T(8,128)(2,1)S(1)}, u32[]{:S(2)}, u32[]{:S(2)}) %collective-permute-start.15) | collective-permute-done | bytes 524320 | tf_op jit(solution)/shard_map/ppermute | solution.py:21
  513.6 41.4 %collective-permute-done.17 = bf16[256,2,512]{2,0,1:T(8,128)(2,1)} collective-permute-done((bf16[256,2,512]{2,0,1:T(8,128)(2,1)}, bf16[256,2,512]{2,0,1:T(8,128)(2,1)}, u32[]{:S(2)}, u32[]{:S(2)}) %collective-permute-start.17) | collective-permute-done | bytes 524320 | tf_op jit(solution)/shard_map/ppermute | solution.py:21
  569.0 6.8 scatter_custom_fusion
  575.8 53.1 %all_to_all.39 = bf16[8,128,1024]{2,1,0:T(8,128)(2,1)} all-to-all(bf16[8,128,1024]{2,1,0:T(8,128)(2,1)S(1)} %bitcast.176), channel_id=1, replica_groups=mesh['ctx'=8,'ch'=4] {'ctx'}, dimensions={0} | all-to-all | bytes 4194304 | tf_op jit(solution)/shard_map/all_to_all | solution.py:151
  640.8 46.6 %all-to-all-done.2 = bf16[8,128,1024]{2,1,0:T(8,128)(2,1)S(1)} async-done(((bf16[8,128,1024]{2,1,0:T(8,128)(2,1)}), bf16[8,128,1024]{2,1,0:T(8,128)(2,1)S(1)}, u32[]{:S(2)}, u32[]{:S(2)}) %all-to-all-start.2) | async-done | bytes 2097184 | tf_op jit(solution)/shard_map/all_to_all | solution.py:166
  (124 shorter events, 147.0 us)
Async XLA Ops:
  0.6 639.1 %copy-start = (f32[1024,32]{0,1:T(8,128)S(1)}, f32[1024,32]{0,1:T(8,128)}, u32[]{:S(2)}) copy-start(f32[1024,32]{0,1:T(8,128)} %param.14) | copy-start | bytes 393220
  4.4 118.2 %collective-permute-start = (f32[256,2,512]{2,0,1:T(8,128)}, f32[256,2,512]{2,0,1:T(8,128)}, u32[]{:S(2)}, u32[]{:S(2)}) collective-permute-start(f32[256,2,512]{2,0,1:T(8,128)} %pad_maximum_fusion), channel_id=1, source_target_pairs={{0,16},{16,0},{4,20},{20,4},{8,24},{24,8},{12,28},{28,12},{1,17},{... | collective-permute-start | bytes 3145736 | tf_op jit(solution)/shard_map/ppermute | solution.py:21
  9.6 135.6 %collective-permute-start.6 = (f32[256,2,512]{2,0,1:T(8,128)}, f32[256,2,512]{2,0,1:T(8,128)}, u32[]{:S(2)}, u32[]{:S(2)}) collective-permute-start(f32[256,2,512]{2,0,1:T(8,128)} %pad_maximum_fusion.1), channel_id=1, source_target_pairs={{0,16},{16,0},{4,20},{20,4},{8,24},{24,8},{12,28},{28,12},{1,17},{... | collective-permute-start | bytes 3145736 | tf_op jit(solution)/shard_map/ppermute | solution.py:21
  10.7 156.9 %collective-permute-start.1 = (f32[256,2,512]{2,0,1:T(8,128)}, f32[256,2,512]{2,0,1:T(8,128)}, u32[]{:S(2)}, u32[]{:S(2)}) collective-permute-start(f32[256,2,512]{2,0,1:T(8,128)} %stack.34), channel_id=1, source_target_pairs={{0,16},{16,0},{4,20},{20,4},{8,24},{24,8},{12,28},{28,12},{1,17},{... | collective-permute-start | bytes 3145736 | tf_op jit(solution)/shard_map/ppermute | solution.py:21
  14.7 174.5 %collective-permute-start.7 = (f32[256,2,512]{2,0,1:T(8,128)}, f32[256,2,512]{2,0,1:T(8,128)}, u32[]{:S(2)}, u32[]{:S(2)}) collective-permute-start(f32[256,2,512]{2,0,1:T(8,128)} %stack.39), channel_id=1, source_target_pairs={{0,16},{16,0},{4,20},{20,4},{8,24},{24,8},{12,28},{28,12},{1,17},{... | collective-permute-start | bytes 3145736 | tf_op jit(solution)/shard_map/ppermute | solution.py:21
  194.4 26.3 %collective-permute-start.2 = (f32[256,2,512]{2,0,1:T(8,128)}, f32[256,2,512]{2,0,1:T(8,128)S(1)}, u32[]{:S(2)}, u32[]{:S(2)}) collective-permute-start(f32[256,2,512]{2,0,1:T(8,128)} %get-tuple-element.53), channel_id=1, source_target_pairs={{0,8},{8,0},{4,12},{12,4},{16,24},{24,16},{20,28},{28,20},{1,9},{9... | collective-permute-start | bytes 3145736 | tf_op jit(solution)/shard_map/ppermute | solution.py:21
  195.1 48.1 %collective-permute-start.3 = (f32[256,2,512]{2,0,1:T(8,128)}, f32[256,2,512]{2,0,1:T(8,128)S(1)}, u32[]{:S(2)}, u32[]{:S(2)}) collective-permute-start(f32[256,2,512]{2,0,1:T(8,128)} %get-tuple-element.54), channel_id=1, source_target_pairs={{0,8},{8,0},{4,12},{12,4},{16,24},{24,16},{20,28},{28,20},{1,9},{9... | collective-permute-start | bytes 3145736 | tf_op jit(solution)/shard_map/ppermute | solution.py:21
  196.4 69.2 %collective-permute-start.8 = (f32[256,2,512]{2,0,1:T(8,128)}, f32[256,2,512]{2,0,1:T(8,128)S(1)}, u32[]{:S(2)}, u32[]{:S(2)}) collective-permute-start(f32[256,2,512]{2,0,1:T(8,128)} %get-tuple-element.34), channel_id=1, source_target_pairs={{0,8},{8,0},{4,12},{12,4},{16,24},{24,16},{20,28},{28,20},{1,9},{9... | collective-permute-start | bytes 3145736 | tf_op jit(solution)/shard_map/ppermute | solution.py:21
  197.2 89.3 %collective-permute-start.9 = (f32[256,2,512]{2,0,1:T(8,128)}, f32[256,2,512]{2,0,1:T(8,128)}, u32[]{:S(2)}, u32[]{:S(2)}) collective-permute-start(f32[256,2,512]{2,0,1:T(8,128)} %get-tuple-element.35), channel_id=1, source_target_pairs={{0,8},{8,0},{4,12},{12,4},{16,24},{24,16},{20,28},{28,20},{1,9},{9... | collective-permute-start | bytes 3145736 | tf_op jit(solution)/shard_map/ppermute | solution.py:21
  220.7 65.8 %copy-start.3 = (f32[256,2,512]{2,0,1:T(8,128)}, f32[256,2,512]{2,0,1:T(8,128)S(1)}, u32[]{:S(2)}) copy-start(f32[256,2,512]{2,0,1:T(8,128)S(1)} %collective-permute-done.2) | copy-start | bytes 3145732
  292.2 26.2 %collective-permute-start.10 = (f32[256,2,512]{2,0,1:T(8,128)S(1)}, f32[256,2,512]{2,0,1:T(8,128)}, u32[]{:S(2)}, u32[]{:S(2)}) collective-permute-start(f32[256,2,512]{2,0,1:T(8,128)S(1)} %get-tuple-element.26), channel_id=1, source_target_pairs={{0,4},{4,0},{8,12},{12,8},{16,20},{20,16},{24,28},{28,24},{1,5},{5... | collective-permute-start | bytes 3145736 | tf_op jit(solution)/shard_map/ppermute | solution.py:21
  293.5 47.4 %collective-permute-start.11 = (f32[256,2,512]{2,0,1:T(8,128)S(1)}, f32[256,2,512]{2,0,1:T(8,128)}, u32[]{:S(2)}, u32[]{:S(2)}) collective-permute-start(f32[256,2,512]{2,0,1:T(8,128)S(1)} %get-tuple-element.27), channel_id=1, source_target_pairs={{0,4},{4,0},{8,12},{12,8},{16,20},{20,16},{24,28},{28,24},{1,5},{5... | collective-permute-start | bytes 3145736 | tf_op jit(solution)/shard_map/ppermute | solution.py:21
  294.2 69.1 %collective-permute-start.4 = (f32[256,2,512]{2,0,1:T(8,128)S(1)}, f32[256,2,512]{2,0,1:T(8,128)}, u32[]{:S(2)}, u32[]{:S(2)}) collective-permute-start(f32[256,2,512]{2,0,1:T(8,128)S(1)} %get-tuple-element.51), channel_id=1, source_target_pairs={{0,4},{4,0},{8,12},{12,8},{16,20},{20,16},{24,28},{28,24},{1,5},{5... | collective-permute-start | bytes 3145736 | tf_op jit(solution)/shard_map/ppermute | solution.py:21
  295.5 87.7 %collective-permute-start.5 = (f32[256,2,512]{2,0,1:T(8,128)}, f32[256,2,512]{2,0,1:T(8,128)}, u32[]{:S(2)}, u32[]{:S(2)}) collective-permute-start(f32[256,2,512]{2,0,1:T(8,128)} %get-tuple-element.52), channel_id=1, source_target_pairs={{0,4},{4,0},{8,12},{12,8},{16,20},{20,16},{24,28},{28,24},{1,5},{5... | collective-permute-start | bytes 3145736 | tf_op jit(solution)/shard_map/ppermute | solution.py:21
  296.3 90.4 %copy-start.7 = (f32[512]{0:T(512)}, f32[512]{0:T(512)S(1)}, u32[]{:S(2)}) copy-start(f32[512]{0:T(512)S(1)} %get-tuple-element.65) | copy-start | bytes 6148
  458.3 14.6 %collective-permute-start.12 = (bf16[256,2,512]{2,0,1:T(8,128)(2,1)}, bf16[256,2,512]{2,0,1:T(8,128)(2,1)S(1)}, u32[]{:S(2)}, u32[]{:S(2)}) collective-permute-start(bf16[256,2,512]{2,0,1:T(8,128)(2,1)} %get-tuple-element.57), channel_id=1, source_target_pairs={{0,4},{4,0},{8,12},{12,8},{16,20},{20,16},{24,28},{28,24},{1,5},{5... | collective-permute-start | bytes 1572872 | tf_op jit(solution)/shard_map/ppermute | solution.py:21
  466.6 14.5 %collective-permute-start.13 = (bf16[256,2,512]{2,0,1:T(8,128)(2,1)}, bf16[256,2,512]{2,0,1:T(8,128)(2,1)}, u32[]{:S(2)}, u32[]{:S(2)}) collective-permute-start(bf16[256,2,512]{2,0,1:T(8,128)(2,1)} %get-tuple-element.55), channel_id=1, source_target_pairs={{0,4},{4,0},{8,12},{12,8},{16,20},{20,16},{24,28},{28,24},{1,5},{5... | collective-permute-start | bytes 1572872 | tf_op jit(solution)/shard_map/ppermute | solution.py:21
  482.8 16.0 %collective-permute-start.14 = (bf16[256,2,512]{2,0,1:T(8,128)(2,1)S(1)}, bf16[256,2,512]{2,0,1:T(8,128)(2,1)S(1)}, u32[]{:S(2)}, u32[]{:S(2)}) collective-permute-start(bf16[256,2,512]{2,0,1:T(8,128)(2,1)S(1)} %get-tuple-element.20), channel_id=1, source_target_pairs={{0,8},{8,0},{4,12},{12,4},{16,24},{24,16},{20,28},{28,20},{1,9},{9... | collective-permute-start | bytes 1572872 | tf_op jit(solution)/shard_map/ppermute | solution.py:21
  485.9 20.6 %collective-permute-start.15 = (bf16[256,2,512]{2,0,1:T(8,128)(2,1)S(1)}, bf16[256,2,512]{2,0,1:T(8,128)(2,1)S(1)}, u32[]{:S(2)}, u32[]{:S(2)}) collective-permute-start(bf16[256,2,512]{2,0,1:T(8,128)(2,1)S(1)} %get-tuple-element.40), channel_id=1, source_target_pairs={{0,8},{8,0},{4,12},{12,4},{16,24},{24,16},{20,28},{28,20},{1,9},{9... | collective-permute-start | bytes 1572872 | tf_op jit(solution)/shard_map/ppermute | solution.py:21
  508.0 48.1 %collective-permute-start.16 = (bf16[256,2,512]{2,0,1:T(8,128)(2,1)S(1)}, bf16[256,2,512]{2,0,1:T(8,128)(2,1)}, u32[]{:S(2)}, u32[]{:S(2)}) collective-permute-start(bf16[256,2,512]{2,0,1:T(8,128)(2,1)S(1)} %get-tuple-element.16), channel_id=1, source_target_pairs={{0,16},{16,0},{4,20},{20,4},{8,24},{24,8},{12,28},{28,12},{1,17},{... | collective-permute-start | bytes 1572872 | tf_op jit(solution)/shard_map/ppermute | solution.py:21
  512.9 42.1 %collective-permute-start.17 = (bf16[256,2,512]{2,0,1:T(8,128)(2,1)}, bf16[256,2,512]{2,0,1:T(8,128)(2,1)}, u32[]{:S(2)}, u32[]{:S(2)}) collective-permute-start(bf16[256,2,512]{2,0,1:T(8,128)(2,1)} %get-tuple-element.38), channel_id=1, source_target_pairs={{0,16},{16,0},{4,20},{20,4},{8,24},{24,8},{12,28},{28,12},{1,17},{... | collective-permute-start | bytes 1572872 | tf_op jit(solution)/shard_map/ppermute | solution.py:21
  559.0 9.4 %all-to-all-start = ((bf16[4,128,256]{1,2,0:T(8,128)(2,1)}), bf16[4,128,256]{1,2,0:T(8,128)(2,1)S(1)}, u32[]{:S(2)}, u32[]{:S(2)}) async-start(bf16[4,128,256]{1,2,0:T(8,128)(2,1)} %copy_bitcast_fusion), calls=%async_computation | async-start | bytes 524288 | tf_op jit(solution)/shard_map/all_to_all | solution.py:126
  635.9 51.5 %all-to-all-start.2 = ((bf16[8,128,1024]{2,1,0:T(8,128)(2,1)}), bf16[8,128,1024]{2,1,0:T(8,128)(2,1)S(1)}, u32[]{:S(2)}, u32[]{:S(2)}) async-start(bf16[8,128,1024]{2,1,0:T(8,128)(2,1)} %bitcast.175), calls=%async_computation.2 | async-start | bytes 4194304 | tf_op jit(solution)/shard_map/all_to_all | solution.py:166
  697.5 9.4 %all-to-all-start.3 = ((bf16[128,4,256]{0,2,1:T(8,128)(2,1)}), bf16[128,4,256]{0,2,1:T(8,128)(2,1)S(1)}, u32[]{:S(2)}, u32[]{:S(2)}) async-start(bf16[128,4,256]{0,2,1:T(8,128)(2,1)} %bitcast.29), calls=%async_computation.3 | async-start | bytes 524288 | tf_op jit(solution)/shard_map/all_to_all | solution.py:176
  (12 other events, 144.4 us)
where the time goes:
time: 713 us; the launch traced here: 708 us
  waiting for transfers between devices  479 us (67%)
  matrix products  84.3 us (12%)
  blocking collectives  53.1 us (7%)
  starting transfers between devices  35.7 us (5%)
  other arithmetic  31.4 us (4%)
  local copies, waits for them, and re-layouts  23 us (3%)
    ppermute x18, waiting for transfers between devices, partner(): return lax.ppermute(block, axis, route)  421 us
    all_to_all x1, blocking collectives, body(): lax.all_to_all(send_rows.reshape(shards, parts_dev * CAP, width), 'ctx',...  53.1 us
    all_to_all x1, waiting for transfers between devices, body(): lax.all_to_all(result.reshape(shards, parts_dev * CAP, width), 'ctx', spl...  46.6 us
    ppermute x18, starting transfers between devices, partner(): return lax.ppermute(block, axis, route)  25.2 us
    select_n x3, other arithmetic, forward_pair(): jnp.where(upper, diff_real, own_real + far_real)  14.5 us
  transfers between devices with their start and end apart: 21, of which 20 were waited for; matrix products, arithmetic and copies ran while one was open for 3% of the time, Pallas kernels for 0%

commit v1 on v0

v1 whole, which is shorter than its diff:
```python
import functools
import math

import jax
import jax.numpy as jnp
import ml_dtypes
import numpy as np
from jax import lax
from jax.experimental import pallas as pl
from jax.experimental.pallas import tpu as pltpu
from jax.sharding import PartitionSpec as P

CAP = 16
SKIP_ROWS = 16
VMEM_LIMIT = 48 * 1024 * 1024

f32 = jnp.float32
bf16 = jnp.bfloat16


def params(limit=VMEM_LIMIT):
    return pltpu.CompilerParams(vmem_limit_bytes=limit)


def call(kernel, out_shape, scalars, operands, name, scratch=(), cost=None):
    vmem = pl.BlockSpec(memory_space=pltpu.VMEM)
    smem = pl.BlockSpec(memory_space=pltpu.SMEM)
    return pl.pallas_call(
        kernel,
        out_shape=out_shape,
        in_specs=[smem] * len(scalars) + [vmem] * len(operands),
        out_specs=jax.tree.map(lambda _: vmem, out_shape),
        scratch_shapes=scratch,
        compiler_params=params(),
        cost_estimate=cost,
        name=name,
    )(*scalars, *operands)


def cmul(a, w):
    re, im = a
    wr, wi = w.real, w.imag
    if abs(wi) < 1e-12:
        return (re, im) if wr > 0 else (-re, -im)
    if abs(wr) < 1e-12:
        return (-im, re) if wi > 0 else (im, -re)
    return (re * wr - im * wi, re * wi + im * wr)


def fft(values, sign):
    count = len(values)
    if count == 1:
        return values
    even, odd = fft(values[::2], sign), fft(values[1::2], sign)
    low, high = [], []
    for k in range(count // 2):
        angle = sign * 2.0 * math.pi * k / count
        tr, ti = cmul(odd[k], complex(math.cos(angle), math.sin(angle)))
        er, ei = even[k]
        low.append((er + tr, ei + ti))
        high.append((er - tr, ei - ti))
    return low + high


def tables(shards, length):
    index = np.arange(length)
    angle = 2.0 * np.pi / length * (np.outer(index, index) % length)
    turn = 2.0 * np.pi / (shards * length) * np.outer(np.arange(shards) + 0.25, index)
    narrow = ml_dtypes.bfloat16
    return (
        np.cos(angle).astype(narrow),
        np.sin(angle).astype(narrow),
        np.cos(turn).astype(np.float32),
        np.sin(turn).astype(np.float32),
    )


def prep_kernel(groups, blocks, me, sig, gate, taps, skip, spread, *pieces):
    tok, chans = sig.shape
    per = chans // groups
    sig_t = sig[...].astype(f32).T.astype(bf16)
    tap_t = taps[...].T.astype(bf16)
    for g in range(groups):
        spread[g, :per, :] = sig_t[g * per : (g + 1) * per, :]
        spread[g, per:, :] = tap_t[g * per : (g + 1) * per, :]
    rows = tok // blocks
    own = skip[...]
    first = own.astype(bf16)
    own = own - first.astype(f32)
    second = own.astype(bf16)
    third = (own - second.astype(f32)).astype(bf16)
    row = lax.broadcasted_iota(jnp.int32, (SKIP_ROWS, chans), 0)
    wide = jnp.where(
        row == 0,
        first.astype(f32),
        jnp.where(
            row == 1, second.astype(f32), jnp.where(row == 2, third.astype(f32), 0.0)
        ),
    ).astype(bf16)
    for o in range(blocks):
        start = pl.multiple_of((me[0] ^ o) * rows, rows)
        pieces[o][:rows, :] = gate[pl.ds(start, rows), :]
        pieces[o][rows : 2 * rows, :] = sig[pl.ds(start, rows), :]
        pieces[o][2 * rows :, :] = wide


def conv_kernel(blocks, got, cos, sin, turn_cos, turn_sin, out, are, aim, pre, pim):
    shards, twice, tok = got.shape
    per = twice // 2
    rows = tok // blocks
    step = min(per, 16)
    total = shards * tok
    half = shards * per
    twist = [
        complex(math.cos(0.5 * math.pi * j / shards), math.sin(0.5 * math.pi * j / shards))
        for j in range(shards)
    ]
    for which in range(2):
        for r in range(0, per, step):
            for b in range(blocks):
                lanes = slice(b * rows, (b + 1) * rows)
                values = []
                for j in range(shards):
                    x = got[j, which * per + r : which * per + r + step, lanes].astype(f32)
                    values.append((x * twist[j].real, x * -twist[j].imag))
                for k, (re, im) in enumerate(fft(values, -1.0)):
                    c, s = turn_cos[k : k + 1, lanes], turn_sin[k : k + 1, lanes]
                    at = which * half + k * per + r
                    are[at : at + step, lanes] = (re * c + im * s).astype(bf16)
                    aim[at : at + step, lanes] = (im * c - re * s).astype(bf16)

    def dot(a, b):
        return jnp.dot(a, b, preferred_element_type=f32)

    xr = dot(are[...], cos[...]) + dot(aim[...], sin[...])
    xi = dot(aim[...], cos[...]) - dot(are[...], sin[...])
    sr, hr, si, hi = xr[:half], xr[half:], xi[:half], xi[half:]
    prod_re = (sr * hr - si * hi).astype(bf16)
    prod_im = (sr * hi + si * hr).astype(bf16)
    pre[...] = dot(prod_re, cos[...]) - dot(prod_im, sin[...])
    pim[...] = dot(prod_im, cos[...]) + dot(prod_re, sin[...])
    for r in range(0, per, step):
        for b in range(blocks):
            lanes = slice(b * rows, (b + 1) * rows)
            values = []
            for k in range(shards):
                c, s = turn_cos[k : k + 1, lanes], turn_sin[k : k + 1, lanes]
                at = k * per + r
                re, im = pre[at : at + step, lanes], pim[at : at + step, lanes]
                values.append((re * c - im * s, im * c + re * s))
            for j, (re, im) in enumerate(fft(values, 1.0)):
                y = (re * twist[j].real - im * twist[j].imag) * (1.0 / total)
                out[j, b, r : r + step, :] = y.astype(bf16)


def slots(routes_t, experts):
    rows = routes_t.shape[1]
    expert = lax.broadcasted_iota(jnp.int32, (experts, rows), 0)
    named = [routes_t[k : k + 1, :] == expert for k in range(2)]
    either = jnp.where(named[0] | named[1], 1.0, 0.0).astype(bf16)
    before = lax.broadcasted_iota(jnp.int32, (rows, rows), 0)
    after = lax.broadcasted_iota(jnp.int32, (rows, rows), 1)
    ahead = jnp.where(before < after, 1.0, 0.0).astype(bf16)
    rank = jnp.dot(either, ahead, preferred_element_type=f32).astype(jnp.int32)
    slot = lax.broadcasted_iota(jnp.int32, (experts, CAP, rows), 1)
    picks = []
    for k in range(2):
        mine = jnp.where(named[k], rank, -1)
        picks.append(jnp.where(mine[:, None, :] == slot, 1.0, 0.0))
    return picks


def rows_kernel(experts, blocks, me, routes_t, gain, conv, *refs):
    pieces, refs = refs[:blocks], refs[blocks:]
    mixed_out, (send, normed_out, mixed) = refs[:blocks], refs[blocks:]
    shards, _, per, rows = conv.shape
    chans = shards * per
    width = chans * blocks
    square = jnp.zeros((rows, 1), f32)
    for o in range(blocks):
        group = me[0] ^ o
        piece = pieces[o]
        gate = piece[:rows, :].astype(f32)
        sig = piece[rows : 2 * rows, :].astype(f32)
        skip = piece[2 * rows :, :].astype(f32)
        skip = skip[0:1, :] + skip[1:2, :] + skip[2:3, :]
        y = conv[:, group, :, :].astype(f32).reshape(chans, rows).T
        value = (gate * (y + skip * sig)).astype(bf16)
        mixed[group] = value
        mixed_out[o][...] = value
        value = value.astype(f32)
        square = square + jnp.sum(value * value, axis=1, keepdims=True)
    scale = lax.rsqrt(square * (1.0 / width) + 1e-05)
    for h in range(blocks):
        lanes = slice(h * chans, (h + 1) * chans)
        normed_out[:, lanes] = (mixed[h].astype(f32) * scale * gain[:, lanes]).astype(bf16)
    first, second = slots(routes_t[...], experts)
    pick = (first + second).astype(bf16).reshape(experts * CAP, rows)
    sent = jnp.dot(pick, normed_out[...], preferred_element_type=f32).astype(bf16)
    count, size, _ = send.shape
    copies = count * size // (experts * CAP)
    if copies == 1:
        send[...] = sent.reshape(count, size, width)
    else:
        for p in range(count):
            e = p // copies
            send[p] = sent[e * CAP : (e + 1) * CAP, :]


def gates_kernel(normed, router, routes, gates):
    logits = jnp.dot(
        normed[...].astype(f32),
        router[...],
        precision=lax.Precision.HIGHEST,
        preferred_element_type=f32,
    )
    expert = lax.broadcasted_iota(jnp.int32, logits.shape, 1)
    for k in range(2):
        picked = jnp.where(routes[:, k : k + 1] == expert, logits, 0.0)
        value = jnp.sum(picked, axis=1, keepdims=True)
        gates[:, k : k + 1] = jax.nn.sigmoid(value)


def expert_kernel(got, up, down, out):
    shards, size, width = got.shape
    parts = up.shape[0]
    x = got[...].reshape(shards * size, width)
    total = jnp.zeros((shards * size, width), f32)
    for p in range(parts):
        hidden = jnp.dot(x, up[p], preferred_element_type=f32)
        hidden = jax.nn.gelu(hidden, approximate=True).astype(bf16)
        total = total + jnp.dot(hidden, down[p], preferred_element_type=f32)
    out[...] = total.astype(bf16).reshape(shards, size, width)


def combine_kernel(experts, blocks, me, routes_t, gates, back, *out):
    count, size, width = back.shape
    rows = routes_t.shape[1]
    chans = width // blocks
    copies = count * size // (experts * CAP)
    picks = slots(routes_t[...], experts)
    total = jnp.zeros((rows, width), f32)
    for k in range(2):
        pick = picks[k].astype(bf16).reshape(experts * CAP, rows)
        for c in range(copies):
            if copies == 1:
                values = back[...].reshape(experts * CAP, width)
            else:
                values = jnp.concatenate([back[e * copies + c] for e in range(experts)], axis=0)
            chosen = lax.dot_general(
                pick, values, (((0,), (0,)), ((), ())), preferred_element_type=f32
            )
            total = total + gates[:, k : k + 1] * chosen
    total = total.astype(bf16)
    for h in range(blocks):
        out[0][h] = total[:, h * chans : (h + 1) * chans]


def place_kernel(me, *refs):
    pieces, out = refs[:-1], refs[-1]
    rows = pieces[0].shape[0]
    for o, piece in enumerate(pieces):
        start = pl.multiple_of((me[0] ^ o) * rows, rows)
        out[pl.ds(start, rows), :] = piece[...]


def swap(pieces, axis):
    count = len(pieces)
    return [pieces[0]] + [
        lax.ppermute(pieces[o], axis, [(i, i ^ o) for i in range(count)]) for o in range(1, count)
    ]


def body(signal, gate_v, taps, skip, norm_gain, router, w_up, w_down, routes):
    tok, chans = signal.shape
    shards, blocks = lax.axis_size("ctx"), lax.axis_size("ch")
    per, rows, width = chans // shards, tok // blocks, chans * blocks
    experts = router.shape[1]
    parts = w_up.shape[0]
    owned = max(1, parts // 2)
    me = lax.axis_index("ch").astype(jnp.int32).reshape(1)
    shape = jax.ShapeDtypeStruct

    spread, *pieces = call(
        functools.partial(prep_kernel, shards, blocks),
        [shape((shards, 2 * per, tok), bf16)] + [shape((2 * rows + SKIP_ROWS, chans), bf16)] * blocks,
        [me],
        [signal, gate_v, taps, skip.reshape(1, chans)],
        "prep",
    )
    pieces = swap(pieces, "ch")
    got = lax.all_to_all(spread, "ctx", split_axis=0, concat_axis=0, tiled=True)
    conv = call(
        functools.partial(conv_kernel, blocks),
        shape((shards, blocks, per, rows), bf16),
        [],
        [got, *tables(shards, tok)],
        "conv",
        [pltpu.VMEM((2 * shards * per, tok), bf16)] * 2 + [pltpu.VMEM((shards * per, tok), f32)] * 2,
    )
    conv = lax.all_to_all(
        conv.reshape(shards * blocks, per, rows), ("ctx", "ch"), split_axis=0, concat_axis=0, tiled=True
    ).reshape(shards, blocks, per, rows)
    routes_t = routes.T
    *mixed, send, normed = call(
        functools.partial(rows_kernel, experts, blocks),
        [shape((rows, chans), bf16)] * blocks
        + [shape((shards, owned * CAP, width), bf16), shape((rows, width), bf16)],
        [me],
        [routes_t, norm_gain.reshape(1, width), conv, *pieces],
        "rows",
        [pltpu.VMEM((blocks, rows, chans), bf16)],
    )
    mixed = swap(mixed, "ch")
    there = lax.all_to_all(send, "ctx", split_axis=0, concat_axis=0, tiled=True)
    gates = call(gates_kernel, shape((rows, 2), f32), [], [normed, router, routes], "gates")
    mixed = call(place_kernel, shape((tok, chans), bf16), [me], mixed, "place")
    group = min(parts, 2)
    size = owned * CAP
    result = pl.pallas_call(
        expert_kernel,
        grid=(owned,),
        out_shape=shape((shards, size, width), bf16),
        in_specs=[
            pl.BlockSpec((shards, CAP, width), lambda e: (0, e, 0)),
            pl.BlockSpec((group,) + w_up.shape[1:], lambda e: (e, 0, 0)),
            pl.BlockSpec((group,) + w_down.shape[1:], lambda e: (e, 0, 0)),
        ],
        out_specs=pl.BlockSpec((shards, CAP, width), lambda e: (0, e, 0)),
        compiler_params=params(),
        name="experts",
    )(there, w_up, w_down)
    back = lax.all_to_all(result, "ctx", split_axis=0, concat_axis=0, tiled=True)
    (moe_rows,) = call(
        functools.partial(combine_kernel, experts, blocks),
        [shape((blocks, rows, chans), bf16)],
        [me],
        [routes_t, gates, back],
        "combine",
    )
    moe_out = lax.all_to_all(moe_rows, "ch", split_axis=0, concat_axis=0, tiled=True)
    return (mixed, moe_out.reshape(tok, chans))


def solution(mesh):
    in_specs = (
        P("ctx", "ch"),
        P("ctx", "ch"),
        P("ctx", "ch"),
        P("ch"),
        P(),
        P(),
        P("ctx", None, None),
        P("ctx", None, None),
        P(("ctx", "ch"), None),
    )
    out_specs = (P("ctx", "ch"), P("ctx", "ch"))
    return jax.shard_map(body, mesh=mesh, in_specs=in_specs, out_specs=out_specs, check_vma=False)
```

time: 713 us -> 131 us (0.18)
  waiting for transfers between devices: 479 us -> 40.1 us
  matrix products: 84.3 us -> 0 us
  other arithmetic: 31.4 us -> 0 us
  starting transfers between devices: 35.7 us -> 14.8 us
  local copies, waits for them, and re-layouts: 23 us -> 8.16 us
  Pallas kernels: 0 us -> 13.1 us
    ppermute x18 -> x6, waiting for transfers between devices: 421 us -> 15.5 us  [swap(): lax.ppermute(pieces[o], axis, [(i, i ^ o) for i in range(count)])]
    dot_general x14 -> x0, matrix products: 84.3 us -> none  [the longest x2 13.2 us: local_forward(): jnp.matmul(imag_part, cosine, precision=precise)]
    all_to_all x3, waiting for transfers between devices: 57.7 us -> 24.6 us  [the longest x1 24.6 us: body(): lax.all_to_all(result, 'ctx', split_axis=0, concat_axis=0, tiled=True)]
    ppermute x18 -> x6, starting transfers between devices: 25.2 us -> 4.16 us  [swap(): lax.ppermute(pieces[o], axis, [(i, i ^ o) for i in range(count)])]
    select_n x5 -> x0, other arithmetic: 14.5 us -> none  [the longest x3 14.5 us: forward_pair(): jnp.where(upper, diff_real, own_real + far_real)]
    pallas_call x0 -> x7, Pallas kernels: none -> 13.1 us  [the longest x6 7.08 us: call(): pl.pallas_call(kernel, out_shape=out_shape, in_specs=[smem] * len(scalars...]
    all_to_all x1 -> x2, blocking collectives: 53.1 us -> 53.1 us  [the longest x1 31.5 us: body(): there = lax.all_to_all(send, 'ctx', split_axis=0, concat_axis=0, tiled=True)]
  transfers between devices with their start and end apart: 21 -> 9, of which waited for: 20 -> 5; matrix products, arithmetic and copies ran while one was open for 3% -> 0% of each run, Pallas kernels for 0% -> 1%
where the time goes in v1:
time: 131 us; the launch traced here: 130 us
  blocking collectives  53.1 us (41%)
  waiting for transfers between devices  40.1 us (31%)
  starting transfers between devices  14.8 us (11%)
  Pallas kernels  13.1 us (10%)
  local copies, waits for them, and re-layouts  8.16 us (6%)
    all_to_all x1, blocking collectives, body(): there = lax.all_to_all(send, 'ctx', split_axis=0, concat_axis=0, tiled=True)  31.5 us
    all_to_all x1, waiting for transfers between devices, body(): lax.all_to_all(result, 'ctx', split_axis=0, concat_axis=0, tiled=True)  24.6 us
    all_to_all x1, blocking collectives, body(): got = lax.all_to_all(spread, 'ctx', split_axis=0, concat_axis=0, tiled=True)  21.6 us
    ppermute x6, waiting for transfers between devices, swap(): lax.ppermute(pieces[o], axis, [(i, i ^ o) for i in range(count)])  15.5 us
    unnamed x25, local copies, waits for them, and re-layouts  8.16 us
    pallas_call x6, Pallas kernels, call(): pl.pallas_call(kernel, out_shape=out_shape, in_specs=[smem] * len(scalars...  7.08 us
    pallas_call x1, Pallas kernels, body(): pl.pallas_call(expert_kernel, grid=(owned,), out_shape=shape((shards, siz...  6 us
    ppermute x6, starting transfers between devices, swap(): lax.ppermute(pieces[o], axis, [(i, i ^ o) for i in range(count)])  4.16 us
  transfers between devices with their start and end apart: 9, of which 5 were waited for; matrix products, arithmetic and copies ran while one was open for 0% of the time, Pallas kernels for 1%

profile of v1, /device:TPU:0, one launch (start us, length us, event | category | flops | bytes accessed | tf_op | source)
XLA Modules:
  0.0 130.0 jit_solution(8685440527258156714)
XLA Ops:
  0.7 1.0 copy-done.2
  1.7 0.9 copy-done.3
  2.7 0.9 copy-done.4
  4.5 21.6 %all_to_all.25.got = bf16[8,64,512]{2,1,0:T(8,128)(2,1)S(1)} all-to-all(bf16[8,64,512]{2,1,0:T(8,128)(2,1)S(1)} %get-tuple-element.13), channel_id=1, replica_groups=mesh['ctx'=8,'ch'=4] {'ctx'}, dimensions={0} | all-to-all | bytes 1048576 | tf_op jit(solution)/shard_map/all_to_all | solution.py:292
  26.1 1.0 copy-done
  27.1 1.0 copy-done.1
  28.2 0.7 copy-done.5
  28.9 0.7 copy-done.6
  29.6 3.4 %conv.1 = bf16[8,4,32,128]{3,2,1,0:T(8,128)(2,1)} custom-call(bf16[8,64,512]{2,1,0:T(8,128)(2,1)S(1)} %all_to_all.25.got, bf16[512,512]{1,0:T(8,128)(2,1)S(1)} %copy-done, bf16[512,512]{1,0:T(8,128)(2,1)S(1)} %copy-done.1, f32[8,512]{1,0:T(8,128)S(1)} %copy-done.5, f32[8,512]{1,0:T(8,128)S(1)} %copy-done.6), custom_call_target="tpu_custom_call" | custom-call | tf_op jit(solution)/shard_map/conv/pallas_call | solution.py:28
  33.0 3.6 %all-to-all-start.1 = ((bf16[32,32,128]{2,1,0:T(8,128)(2,1)}), bf16[32,32,128]{2,1,0:T(8,128)(2,1)S(1)}, u32[]{:S(2)}, u32[]{:S(2)}) async-start(bf16[32,32,128]{2,1,0:T(8,128)(2,1)} %bitcast.4), calls=%async_computation.1 | async-start | bytes 524288 | tf_op jit(solution)/shard_map/all_to_all | solution.py:301
  36.9 1.7 %collective-permute-start.1 = (bf16[272,256]{1,0:T(8,128)(2,1)S(1)}, bf16[272,256]{1,0:T(8,128)(2,1)S(1)}, u32[]{:S(2)}, u32[]{:S(2)}) collective-permute-start(bf16[272,256]{1,0:T(8,128)(2,1)S(1)} %get-tuple-element.16), channel_id=1, source_target_pairs={{0,2},{1,3},{2,0},{3,1},{4,6},{5,7},{6,4},{7,5},{8,10},{9,11},{10,... | collective-permute-start | bytes 417800 | tf_op jit(solution)/shard_map/ppermute | solution.py:270
  38.6 6.9 %collective-permute-done.1.refs_2_ = bf16[272,256]{1,0:T(8,128)(2,1)S(1)} collective-permute-done((bf16[272,256]{1,0:T(8,128)(2,1)S(1)}, bf16[272,256]{1,0:T(8,128)(2,1)S(1)}, u32[]{:S(2)}, u32[]{:S(2)}) %collective-permute-start.1) | collective-permute-done | bytes 139296 | tf_op jit(solution)/shard_map/ppermute | solution.py:270
  45.6 2.4 %collective-permute-done.2.refs_3_ = bf16[272,256]{1,0:T(8,128)(2,1)S(1)} collective-permute-done((bf16[272,256]{1,0:T(8,128)(2,1)S(1)}, bf16[272,256]{1,0:T(8,128)(2,1)S(1)}, u32[]{:S(2)}, u32[]{:S(2)}) %collective-permute-start.2) | collective-permute-done | bytes 139296 | tf_op jit(solution)/shard_map/ppermute | solution.py:270
  48.0 0.8 rows.1
  48.7 31.5 %all_to_all.26.got = bf16[8,64,1024]{2,1,0:T(8,128)(2,1)S(1)} all-to-all(bf16[8,64,1024]{2,1,0:T(8,128)(2,1)S(1)} %get-tuple-element.23), channel_id=1, replica_groups=mesh['ctx'=8,'ch'=4] {'ctx'}, dimensions={0} | all-to-all | bytes 2097152 | tf_op jit(solution)/shard_map/all_to_all | solution.py:315
  80.3 6.0 %experts.1 = bf16[8,64,1024]{2,1,0:T(8,128)(2,1)} custom-call(bf16[8,64,1024]{2,1,0:T(8,128)(2,1)S(1)} %all_to_all.26.got, bf16[8,1024,256]{2,1,0:T(8,128)(2,1)} %up.1, bf16[8,256,1024]{2,1,0:T(8,128)(2,1)} %down.1), custom_call_target="tpu_custom_call" | custom-call | tf_op jit(solution)/shard_map/experts/pallas_call | solution.py:320
  86.3 3.6 %all-to-all-start.3 = ((bf16[8,64,1024]{2,1,0:T(8,128)(2,1)}), bf16[8,64,1024]{2,1,0:T(8,128)(2,1)S(1)}, u32[]{:S(2)}, u32[]{:S(2)}) async-start(bf16[8,64,1024]{2,1,0:T(8,128)(2,1)} %experts.1), calls=%async_computation.3 | async-start | bytes 2097152 | tf_op jit(solution)/shard_map/all_to_all | solution.py:333
  90.9 24.6 %all-to-all-done.3.back = bf16[8,64,1024]{2,1,0:T(8,128)(2,1)S(1)} async-done(((bf16[8,64,1024]{2,1,0:T(8,128)(2,1)}), bf16[8,64,1024]{2,1,0:T(8,128)(2,1)S(1)}, u32[]{:S(2)}, u32[]{:S(2)}) %all-to-all-start.3) | async-done | bytes 1048608 | tf_op jit(solution)/shard_map/all_to_all | solution.py:333
  115.5 1.3 %combine.1 = bf16[4,128,256]{2,1,0:T(8,128)(2,1)} custom-call(s32[1]{0:T(128)} %bitcast.me, s32[2,128]{1,0:T(2,128)S(1)} %bitcast.9, f32[128,2]{1,0:T(8,128)S(1)} %gates.1, bf16[8,64,1024]{2,1,0:T(8,128)(2,1)S(1)} %all-to-all-done.3.back), custom_call_target="tpu_custom_call" | custom-call | tf_op jit(solution)/shard_map/combine/pallas_call | solution.py:28
  116.9 3.4 %all-to-all-start.4 = ((bf16[4,128,256]{2,1,0:T(8,128)(2,1)}), bf16[4,128,256]{2,1,0:T(8,128)(2,1)S(1)}, u32[]{:S(2)}, u32[]{:S(2)}) async-start(bf16[4,128,256]{2,1,0:T(8,128)(2,1)} %combine.1), calls=%async_computation.4 | async-start | bytes 524288 | tf_op jit(solution)/shard_map/all_to_all | solution.py:341
  120.7 1.7 %collective-permute-start.4 = (bf16[128,256]{1,0:T(8,128)(2,1)S(1)}, bf16[128,256]{1,0:T(8,128)(2,1)S(1)}, u32[]{:S(2)}, u32[]{:S(2)}) collective-permute-start(bf16[128,256]{1,0:T(8,128)(2,1)S(1)} %get-tuple-element.20), channel_id=1, source_target_pairs={{0,2},{1,3},{2,0},{3,1},{4,6},{5,7},{6,4},{7,5},{8,10},{9,11},{10,... | collective-permute-start | bytes 196616 | tf_op jit(solution)/shard_map/ppermute | solution.py:270
  122.4 5.7 %collective-permute-done.4.refs_2_ = bf16[128,256]{1,0:T(8,128)(2,1)S(1)} collective-permute-done((bf16[128,256]{1,0:T(8,128)(2,1)S(1)}, bf16[128,256]{1,0:T(8,128)(2,1)S(1)}, u32[]{:S(2)}, u32[]{:S(2)}) %collective-permute-start.4) | collective-permute-done | bytes 65568 | tf_op jit(solution)/shard_map/ppermute | solution.py:270
  128.6 0.7 place.1
  129.3 0.7 copy.18
  (28 shorter events, 3.1 us)
Async XLA Ops:
  0.6 47.3 %copy-start.7 = (s32[128,2]{0,1:T(2,128)S(1)}, s32[128,2]{0,1:T(2,128)}, u32[]{:S(2)}) copy-start(s32[128,2]{0,1:T(2,128)} %param.21) | copy-start | bytes 3076
  0.6 47.3 %copy-start.8 = (f32[1024]{0:T(1024)S(1)}, f32[1024]{0:T(1024)}, u32[]{:S(2)}) copy-start(f32[1024]{0:T(1024)} %param.17) | copy-start | bytes 12292
  0.7 1.1 copy-start.2
  1.7 0.9 copy-start.3
  2.7 0.9 copy-start.4
  3.6 0.7 copy-start.9
  26.1 1.0 copy-start
  27.1 1.0 copy-start.1
  28.2 0.7 copy-start.5
  28.9 0.7 copy-start.6
  33.0 15.0 %all-to-all-start.1 = ((bf16[32,32,128]{2,1,0:T(8,128)(2,1)}), bf16[32,32,128]{2,1,0:T(8,128)(2,1)S(1)}, u32[]{:S(2)}, u32[]{:S(2)}) async-start(bf16[32,32,128]{2,1,0:T(8,128)(2,1)} %bitcast.4), calls=%async_computation.1 | async-start | bytes 524288 | tf_op jit(solution)/shard_map/all_to_all | solution.py:301
  36.6 2.0 %collective-permute-start = (bf16[272,256]{1,0:T(8,128)(2,1)S(1)}, bf16[272,256]{1,0:T(8,128)(2,1)S(1)}, u32[]{:S(2)}, u32[]{:S(2)}) collective-permute-start(bf16[272,256]{1,0:T(8,128)(2,1)S(1)} %get-tuple-element.15), channel_id=1, source_target_pairs={{0,1},{1,0},{2,3},{3,2},{4,5},{5,4},{6,7},{7,6},{8,9},{9,8},{10,11... | collective-permute-start | bytes 417800 | tf_op jit(solution)/shard_map/ppermute | solution.py:270
  36.9 8.6 %collective-permute-start.1 = (bf16[272,256]{1,0:T(8,128)(2,1)S(1)}, bf16[272,256]{1,0:T(8,128)(2,1)S(1)}, u32[]{:S(2)}, u32[]{:S(2)}) collective-permute-start(bf16[272,256]{1,0:T(8,128)(2,1)S(1)} %get-tuple-element.16), channel_id=1, source_target_pairs={{0,2},{1,3},{2,0},{3,1},{4,6},{5,7},{6,4},{7,5},{8,10},{9,11},{10,... | collective-permute-start | bytes 417800 | tf_op jit(solution)/shard_map/ppermute | solution.py:270
  38.6 9.3 %collective-permute-start.2 = (bf16[272,256]{1,0:T(8,128)(2,1)S(1)}, bf16[272,256]{1,0:T(8,128)(2,1)S(1)}, u32[]{:S(2)}, u32[]{:S(2)}) collective-permute-start(bf16[272,256]{1,0:T(8,128)(2,1)S(1)} %get-tuple-element.17), channel_id=1, source_target_pairs={{0,3},{1,2},{2,1},{3,0},{4,7},{5,6},{6,5},{7,4},{8,11},{9,10},{10,... | collective-permute-start | bytes 417800 | tf_op jit(solution)/shard_map/ppermute | solution.py:270
  80.3 9.8 %copy-start.10 = (f32[1024,32]{0,1:T(8,128)S(1)}, f32[1024,32]{0,1:T(8,128)}, u32[]{:S(2)}) copy-start(f32[1024,32]{0,1:T(8,128)} %param.18) | copy-start | bytes 393220
  86.3 29.2 %all-to-all-start.3 = ((bf16[8,64,1024]{2,1,0:T(8,128)(2,1)}), bf16[8,64,1024]{2,1,0:T(8,128)(2,1)S(1)}, u32[]{:S(2)}, u32[]{:S(2)}) async-start(bf16[8,64,1024]{2,1,0:T(8,128)(2,1)} %experts.1), calls=%async_computation.3 | async-start | bytes 2097152 | tf_op jit(solution)/shard_map/all_to_all | solution.py:333
  116.9 12.5 %all-to-all-start.4 = ((bf16[4,128,256]{2,1,0:T(8,128)(2,1)}), bf16[4,128,256]{2,1,0:T(8,128)(2,1)S(1)}, u32[]{:S(2)}, u32[]{:S(2)}) async-start(bf16[4,128,256]{2,1,0:T(8,128)(2,1)} %combine.1), calls=%async_computation.4 | async-start | bytes 524288 | tf_op jit(solution)/shard_map/all_to_all | solution.py:341
  120.3 2.2 %collective-permute-start.3 = (bf16[128,256]{1,0:T(8,128)(2,1)S(1)}, bf16[128,256]{1,0:T(8,128)(2,1)S(1)}, u32[]{:S(2)}, u32[]{:S(2)}) collective-permute-start(bf16[128,256]{1,0:T(8,128)(2,1)S(1)} %get-tuple-element.19), channel_id=1, source_target_pairs={{0,1},{1,0},{2,3},{3,2},{4,5},{5,4},{6,7},{7,6},{8,9},{9,8},{10,11... | collective-permute-start | bytes 196616 | tf_op jit(solution)/shard_map/ppermute | solution.py:270
  120.7 7.4 %collective-permute-start.4 = (bf16[128,256]{1,0:T(8,128)(2,1)S(1)}, bf16[128,256]{1,0:T(8,128)(2,1)S(1)}, u32[]{:S(2)}, u32[]{:S(2)}) collective-permute-start(bf16[128,256]{1,0:T(8,128)(2,1)S(1)} %get-tuple-element.20), channel_id=1, source_target_pairs={{0,2},{1,3},{2,0},{3,1},{4,6},{5,7},{6,4},{7,5},{8,10},{9,11},{10,... | collective-permute-start | bytes 196616 | tf_op jit(solution)/shard_map/ppermute | solution.py:270
  122.4 6.2 %collective-permute-start.5 = (bf16[128,256]{1,0:T(8,128)(2,1)S(1)}, bf16[128,256]{1,0:T(8,128)(2,1)S(1)}, u32[]{:S(2)}, u32[]{:S(2)}) collective-permute-start(bf16[128,256]{1,0:T(8,128)(2,1)S(1)} %get-tuple-element.21), channel_id=1, source_target_pairs={{0,3},{1,2},{2,1},{3,0},{4,7},{5,6},{6,5},{7,4},{8,11},{9,10},{10,... | collective-permute-start | bytes 196616 | tf_op jit(solution)/shard_map/ppermute | solution.py:270

commit v2 on v1

--- a/solution.py
+++ b/solution.py
@@ -3,8 +3,6 @@
 
 import jax
 import jax.numpy as jnp
-import ml_dtypes
-import numpy as np
 from jax import lax
 from jax.experimental import pallas as pl
 from jax.experimental.pallas import tpu as pltpu
@@ -12,7 +10,8 @@
 
 CAP = 16
 SKIP_ROWS = 16
-VMEM_LIMIT = 48 * 1024 * 1024
+VMEM_LIMIT = 40 * 1024 * 1024
+PREP_LIMIT = 62 * 1024 * 1024
 
 f32 = jnp.float32
 bf16 = jnp.bfloat16
@@ -22,19 +21,29 @@
     return pltpu.CompilerParams(vmem_limit_bytes=limit)
 
 
-def call(kernel, out_shape, scalars, operands, name, scratch=(), cost=None):
+def call(kernel, out_shape, scalars, far, operands, name, scratch=(), limit=VMEM_LIMIT):
     vmem = pl.BlockSpec(memory_space=pltpu.VMEM)
     smem = pl.BlockSpec(memory_space=pltpu.SMEM)
+    hbm = pl.BlockSpec(memory_space=pltpu.HBM)
+    if far:
+        held = [pltpu.VMEM(x.shape, x.dtype) for x in far]
+        scratch = [*scratch, *held, pltpu.SemaphoreType.DMA((len(far),))]
     return pl.pallas_call(
         kernel,
         out_shape=out_shape,
-        in_specs=[smem] * len(scalars) + [vmem] * len(operands),
+        in_specs=[smem] * len(scalars) + [hbm] * len(far) + [vmem] * len(operands),
         out_specs=jax.tree.map(lambda _: vmem, out_shape),
         scratch_shapes=scratch,
-        compiler_params=params(),
-        cost_estimate=cost,
+        compiler_params=params(limit),
         name=name,
-    )(*scalars, *operands)
+    )(*scalars, *far, *operands)
+
+
+def fetch(far, held, sems):
+    copies = [pltpu.make_async_copy(a, b, sems.at[i]) for i, (a, b) in enumerate(zip(far, held))]
+    for copy in copies:
+        copy.start()
+    return copies
 
 
 def cmul(a, w):
@@ -62,27 +71,49 @@
     return low + high
 
 
-def tables(shards, length):
-    index = np.arange(length)
-    angle = 2.0 * np.pi / length * (np.outer(index, index) % length)
-    turn = 2.0 * np.pi / (shards * length) * np.outer(np.arange(shards) + 0.25, index)
-    narrow = ml_dtypes.bfloat16
-    return (
-        np.cos(angle).astype(narrow),
-        np.sin(angle).astype(narrow),
-        np.cos(turn).astype(np.float32),
-        np.sin(turn).astype(np.float32),
-    )
-
-
-def prep_kernel(groups, blocks, me, sig, gate, taps, skip, spread, *pieces):
+def tables_kernel(turn_cos, turn_sin, cos, sin, wide_cos, wide_sin):
+    shards, length = turn_cos.shape
+    shape = (shards, length)
+    shard = lax.broadcasted_iota(jnp.int32, shape, 0).astype(f32) + 0.25
+    lane = lax.broadcasted_iota(jnp.int32, shape, 1).astype(f32)
+    angle = shard * lane * (2.0 * math.pi / (shards * length))
+    turn_cos[...] = jnp.cos(angle)
+    turn_sin[...] = jnp.sin(angle)
+    row = lax.broadcasted_iota(jnp.int32, (8, length), 0)
+    lane = lax.broadcasted_iota(jnp.int32, (8, length), 1)
+    angle = ((row * lane) & (length - 1)).astype(f32) * (2.0 * math.pi / length)
+    wide_cos[0:8, :] = jnp.cos(angle)
+    wide_sin[0:8, :] = jnp.sin(angle)
+    angle = ((lane << (row + 3)) & (length - 1)).astype(f32) * (2.0 * math.pi / length)
+    step_cos, step_sin = jnp.cos(angle), jnp.sin(angle)
+    count = 8
+    for level in range((length // 8).bit_length() - 1):
+        c, s = step_cos[level : level + 1, :], step_sin[level : level + 1, :]
+        have_cos, have_sin = wide_cos[0:count, :], wide_sin[0:count, :]
+        wide_cos[count : 2 * count, :] = have_cos * c - have_sin * s
+        wide_sin[count : 2 * count, :] = have_sin * c + have_cos * s
+        count = 2 * count
+    cos[...] = wide_cos[...].astype(bf16)
+    sin[...] = wide_sin[...].astype(bf16)
+
+
+def prep_kernel(groups, blocks, me, *refs):
+    far, refs = refs[:4], refs[4:]
+    spread, pieces, held, sems = refs[0], refs[1 : 1 + blocks], refs[1 + blocks : -1], refs[-1]
+    copies = fetch(far, held, sems)
+    sig, taps, gate, skip = held
     tok, chans = sig.shape
     per = chans // groups
+    copies[0].wait()
     sig_t = sig[...].astype(f32).T.astype(bf16)
+    for g in range(groups):
+        spread[g, :per, :] = sig_t[g * per : (g + 1) * per, :]
+    copies[1].wait()
     tap_t = taps[...].T.astype(bf16)
     for g in range(groups):
-        spread[g, :per, :] = sig_t[g * per : (g + 1) * per, :]
         spread[g, per:, :] = tap_t[g * per : (g + 1) * per, :]
+    copies[2].wait()
+    copies[3].wait()
     rows = tok // blocks
     own = skip[...]
     first = own.astype(bf16)
@@ -90,13 +121,10 @@
     second = own.astype(bf16)
     third = (own - second.astype(f32)).astype(bf16)
     row = lax.broadcasted_iota(jnp.int32, (SKIP_ROWS, chans), 0)
-    wide = jnp.where(
-        row == 0,
-        first.astype(f32),
-        jnp.where(
-            row == 1, second.astype(f32), jnp.where(row == 2, third.astype(f32), 0.0)
-        ),
-    ).astype(bf16)
+    wide = jnp.zeros((SKIP_ROWS, chans), f32)
+    for i, term in enumerate((first, second, third)):
+        wide = jnp.where(row == i, term.astype(f32), wide)
+    wide = wide.astype(bf16)
     for o in range(blocks):
         start = pl.multiple_of((me[0] ^ o) * rows, rows)
         pieces[o][:rows, :] = gate[pl.ds(start, rows), :]
@@ -104,7 +132,7 @@
         pieces[o][2 * rows :, :] = wide
 
 
-def conv_kernel(blocks, got, cos, sin, turn_cos, turn_sin, out, are, aim, pre, pim):
+def conv_kernel(blocks, got, turn_cos, turn_sin, cos, sin, out, are, aim, pre, pim):
     shards, twice, tok = got.shape
     per = twice // 2
     rows = tok // blocks
@@ -170,9 +198,10 @@
     return picks
 
 
-def rows_kernel(experts, blocks, me, routes_t, gain, conv, *refs):
+def rows_kernel(experts, blocks, me, at, routes_t, gain, conv, *refs):
     pieces, refs = refs[:blocks], refs[blocks:]
-    mixed_out, (send, normed_out, mixed) = refs[:blocks], refs[blocks:]
+    mixed_out, refs = refs[:blocks], refs[blocks:]
+    send, (normed_out, mixed, sent) = refs[:-3], refs[-3:]
     shards, _, per, rows = conv.shape
     chans = shards * per
     width = chans * blocks
@@ -196,15 +225,20 @@
         normed_out[:, lanes] = (mixed[h].astype(f32) * scale * gain[:, lanes]).astype(bf16)
     first, second = slots(routes_t[...], experts)
     pick = (first + second).astype(bf16).reshape(experts * CAP, rows)
-    sent = jnp.dot(pick, normed_out[...], preferred_element_type=f32).astype(bf16)
-    count, size, _ = send.shape
-    copies = count * size // (experts * CAP)
+    values = jnp.dot(pick, normed_out[...], preferred_element_type=f32).astype(bf16)
+    _, size, _ = sent.shape
+    copies = shards * size // (experts * CAP)
     if copies == 1:
-        send[...] = sent.reshape(count, size, width)
-    else:
-        for p in range(count):
+        sent[...] = values.reshape(shards, size, width)
+    else:
+        for p in range(shards):
             e = p // copies
-            send[p] = sent[e * CAP : (e + 1) * CAP, :]
+            sent[p] = values[e * CAP : (e + 1) * CAP, :]
+    if len(send) == 1:
+        send[0][...] = sent[...]
+    else:
+        for o in range(shards):
+            send[o][...] = sent[at[0] ^ o]
 
 
 def gates_kernel(normed, router, routes, gates):
@@ -221,39 +255,73 @@
         gates[:, k : k + 1] = jax.nn.sigmoid(value)
 
 
-def expert_kernel(got, up, down, out):
-    shards, size, width = got.shape
-    parts = up.shape[0]
-    x = got[...].reshape(shards * size, width)
-    total = jnp.zeros((shards * size, width), f32)
-    for p in range(parts):
+def expert_kernel(count, *refs):
+    got, (up, down), out = refs[:count], refs[count : count + 2], refs[count + 2 :]
+    width = up.shape[1]
+    rows = math.prod(got[0].shape[:-1])
+    x = jnp.concatenate([piece[...].reshape(rows, width) for piece in got], axis=0)
+    total = jnp.zeros(x.shape, f32)
+    for p in range(up.shape[0]):
         hidden = jnp.dot(x, up[p], preferred_element_type=f32)
         hidden = jax.nn.gelu(hidden, approximate=True).astype(bf16)
         total = total + jnp.dot(hidden, down[p], preferred_element_type=f32)
-    out[...] = total.astype(bf16).reshape(shards, size, width)
-
-
-def combine_kernel(experts, blocks, me, routes_t, gates, back, *out):
-    count, size, width = back.shape
+    total = total.astype(bf16)
+    for i, piece in enumerate(out):
+        piece[...] = total[i * rows : (i + 1) * rows].reshape(piece.shape)
+
+
+def run_experts(got, w_up, w_down, owned, group):
+    width = got[0].shape[-1]
+    if got[0].ndim == 2:
+        slot = pl.BlockSpec((CAP, width), lambda e: (e, 0))
+    else:
+        slot = pl.BlockSpec((got[0].shape[0], CAP, width), lambda e: (0, e, 0))
+    return pl.pallas_call(
+        functools.partial(expert_kernel, len(got)),
+        grid=(owned,),
+        out_shape=[jax.ShapeDtypeStruct(x.shape, x.dtype) for x in got],
+        in_specs=[slot] * len(got)
+        + [
+            pl.BlockSpec((group,) + w_up.shape[1:], lambda e: (e, 0, 0)),
+            pl.BlockSpec((group,) + w_down.shape[1:], lambda e: (e, 0, 0)),
+        ],
+        out_specs=[slot] * len(got),
+        compiler_params=params(),
+        name="experts",
+    )(*got, w_up, w_down)
+
+
+def combine_kernel(experts, blocks, shards, me, at, routes_t, gates, *refs):
+    back, out, home = refs[: -blocks - 1], refs[-blocks - 1 : -1], refs[-1]
+    _, size, width = home.shape
     rows = routes_t.shape[1]
     chans = width // blocks
-    copies = count * size // (experts * CAP)
+    copies = shards * size // (experts * CAP)
+    if len(back) == 1:
+        home[...] = back[0][...]
+    else:
+        for o in range(shards):
+            home[at[0] ^ o] = back[o][...]
     picks = slots(routes_t[...], experts)
     total = jnp.zeros((rows, width), f32)
     for k in range(2):
         pick = picks[k].astype(bf16).reshape(experts * CAP, rows)
         for c in range(copies):
             if copies == 1:
-                values = back[...].reshape(experts * CAP, width)
+                values = home[...].reshape(experts * CAP, width)
             else:
-                values = jnp.concatenate([back[e * copies + c] for e in range(experts)], axis=0)
+                values = jnp.concatenate([home[e * copies + c] for e in range(experts)], axis=0)
             chosen = lax.dot_general(
                 pick, values, (((0,), (0,)), ((), ())), preferred_element_type=f32
             )
             total = total + gates[:, k : k + 1] * chosen
     total = total.astype(bf16)
-    for h in range(blocks):
-        out[0][h] = total[:, h * chans : (h + 1) * chans]
+    parts = [total[:, h * chans : (h + 1) * chans] for h in range(blocks)]
+    for o in range(blocks):
+        value = parts[0]
+        for h in range(1, blocks):
+            value = jnp.where((me[0] ^ o) == h, parts[h], value)
+        out[o][...] = value
 
 
 def place_kernel(me, *refs):
@@ -264,11 +332,15 @@
         out[pl.ds(start, rows), :] = piece[...]
 
 
-def swap(pieces, axis):
-    count = len(pieces)
-    return [pieces[0]] + [
-        lax.ppermute(pieces[o], axis, [(i, i ^ o) for i in range(count)]) for o in range(1, count)
+def swap(pieces, axis, offsets, total):
+    return [
+        piece if o == 0 else lax.ppermute(piece, axis, [(i, i ^ o) for i in range(total)])
+        for o, piece in zip(offsets, pieces)
     ]
+
+
+def spread_out(block, axis):
+    return lax.all_to_all(block, axis, split_axis=0, concat_axis=0, tiled=True)
 
 
 def body(signal, gate_v, taps, skip, norm_gain, router, w_up, w_down, routes):
@@ -278,68 +350,94 @@
     experts = router.shape[1]
     parts = w_up.shape[0]
     owned = max(1, parts // 2)
+    group = min(parts, 2)
+    size = owned * CAP
+    direct = 4 <= shards <= 8
     me = lax.axis_index("ch").astype(jnp.int32).reshape(1)
+    at = lax.axis_index("ctx").astype(jnp.int32).reshape(1)
     shape = jax.ShapeDtypeStruct
+    around = list(range(blocks))
 
     spread, *pieces = call(
         functools.partial(prep_kernel, shards, blocks),
         [shape((shards, 2 * per, tok), bf16)] + [shape((2 * rows + SKIP_ROWS, chans), bf16)] * blocks,
         [me],
-        [signal, gate_v, taps, skip.reshape(1, chans)],
+        [signal, taps, gate_v, skip.reshape(1, chans)],
+        [],
         "prep",
-    )
-    pieces = swap(pieces, "ch")
-    got = lax.all_to_all(spread, "ctx", split_axis=0, concat_axis=0, tiled=True)
+        limit=PREP_LIMIT,
+    )
+    turns = call(
+        tables_kernel,
+        [shape((shards, tok), f32)] * 2 + [shape((tok, tok), bf16)] * 2,
+        [],
+        [],
+        [],
+        "tables",
+        [pltpu.VMEM((tok, tok), f32)] * 2,
+    )
+    got = spread_out(spread, "ctx")
+    pieces = swap(pieces, "ch", around, blocks)
+    got, pieces = lax.optimization_barrier((got, pieces))
     conv = call(
         functools.partial(conv_kernel, blocks),
         shape((shards, blocks, per, rows), bf16),
         [],
-        [got, *tables(shards, tok)],
+        [],
+        [got, *turns],
         "conv",
         [pltpu.VMEM((2 * shards * per, tok), bf16)] * 2 + [pltpu.VMEM((shards * per, tok), f32)] * 2,
     )
-    conv = lax.all_to_all(
-        conv.reshape(shards * blocks, per, rows), ("ctx", "ch"), split_axis=0, concat_axis=0, tiled=True
-    ).reshape(shards, blocks, per, rows)
+    conv = spread_out(conv.reshape(shards * blocks, per, rows), ("ctx", "ch"))
+    conv = conv.reshape(shards, blocks, per, rows)
     routes_t = routes.T
-    *mixed, send, normed = call(
+    if direct:
+        send_shape = [shape((size, width), bf16)] * shards
+    else:
+        send_shape = [shape((shards, size, width), bf16)]
+    mixed_and_send = call(
         functools.partial(rows_kernel, experts, blocks),
-        [shape((rows, chans), bf16)] * blocks
-        + [shape((shards, owned * CAP, width), bf16), shape((rows, width), bf16)],
-        [me],
+        [shape((rows, chans), bf16)] * blocks + send_shape + [shape((rows, width), bf16)],
+        [me, at],
+        [],
         [routes_t, norm_gain.reshape(1, width), conv, *pieces],
         "rows",
-        [pltpu.VMEM((blocks, rows, chans), bf16)],
-    )
-    mixed = swap(mixed, "ch")
-    there = lax.all_to_all(send, "ctx", split_axis=0, concat_axis=0, tiled=True)
-    gates = call(gates_kernel, shape((rows, 2), f32), [], [normed, router, routes], "gates")
-    mixed = call(place_kernel, shape((tok, chans), bf16), [me], mixed, "place")
-    group = min(parts, 2)
-    size = owned * CAP
-    result = pl.pallas_call(
-        expert_kernel,
-        grid=(owned,),
-        out_shape=shape((shards, size, width), bf16),
-        in_specs=[
-            pl.BlockSpec((shards, CAP, width), lambda e: (0, e, 0)),
-            pl.BlockSpec((group,) + w_up.shape[1:], lambda e: (e, 0, 0)),
-            pl.BlockSpec((group,) + w_down.shape[1:], lambda e: (e, 0, 0)),
-        ],
-        out_specs=pl.BlockSpec((shards, CAP, width), lambda e: (0, e, 0)),
-        compiler_params=params(),
-        name="experts",
-    )(there, w_up, w_down)
-    back = lax.all_to_all(result, "ctx", split_axis=0, concat_axis=0, tiled=True)
-    (moe_rows,) = call(
-        functools.partial(combine_kernel, experts, blocks),
-        [shape((blocks, rows, chans), bf16)],
-        [me],
-        [routes_t, gates, back],
+        [pltpu.VMEM((blocks, rows, chans), bf16), pltpu.VMEM((shards, size, width), bf16)],
+    )
+    mixed, send, normed = mixed_and_send[:blocks], mixed_and_send[blocks:-1], mixed_and_send[-1]
+    gates = call(gates_kernel, shape((rows, 2), f32), [], [], [normed, router, routes], "gates")
+    if direct:
+        half = shards // 2
+        split = half + half // 2
+        early = [0, *range(half, split), *range(1, half)]
+        late = list(range(split, shards))
+        there = swap([send[o] for o in early], "ctx", early, shards)
+        there_late = swap([send[o] for o in late], "ctx", late, shards)
+        mixed = swap(mixed, "ch", around, blocks)
+        result = run_experts(there, w_up, w_down, owned, group)
+        home = dict(zip(early, swap(result, "ctx", early, shards)))
+        there_late, mixed = lax.optimization_barrier((there_late, mixed))
+        result = run_experts(there_late, w_up, w_down, owned, group)
+        home.update(zip(late, swap(result, "ctx", late, shards)))
+        back = [home[o] for o in range(shards)]
+    else:
+        there = spread_out(send[0], "ctx")
+        mixed = swap(mixed, "ch", around, blocks)
+        (result,) = run_experts([there], w_up, w_down, owned, group)
+        back = [spread_out(result, "ctx")]
+    mixed = call(place_kernel, shape((tok, chans), bf16), [me], [], mixed, "place")
+    moe = call(
+        functools.partial(combine_kernel, experts, blocks, shards),
+        [shape((rows, chans), bf16)] * blocks,
+        [me, at],
+        [],
+        [routes_t, gates, *back],
         "combine",
-    )
-    moe_out = lax.all_to_all(moe_rows, "ch", split_axis=0, concat_axis=0, tiled=True)
-    return (mixed, moe_out.reshape(tok, chans))
+        [pltpu.VMEM((shards, size, width), bf16)],
+    )
+    moe = swap(moe, "ch", around, blocks)
+    moe_out = call(place_kernel, shape((tok, chans), bf16), [me], [], moe, "place")
+    return (mixed, moe_out)
 
 
 def solution(mesh):

time: 131 us -> 102 us (0.78)
  blocking collectives: 53.1 us -> 0 us
  starting transfers between devices: 14.8 us -> 37.6 us
  waiting for transfers between devices: 40.1 us -> 43.3 us
  local copies, waits for them, and re-layouts: 8.16 us -> 5.6 us
  Pallas kernels: 13.1 us -> 14.5 us
    all_to_all x2 -> x0, blocking collectives: 53.1 us -> none  [the longest x1 31.5 us: body(): there = lax.all_to_all(send, 'ctx', split_axis=0, concat_axis=0, tiled=True)]
    ppermute x6 -> x23, starting transfers between devices: 4.16 us -> 26.7 us  [swap(): lax.ppermute(piece, axis, [(i, i ^ o) for i in range(total)])]
    ppermute x6 -> x23, waiting for transfers between devices: 15.5 us -> 27 us  [swap(): lax.ppermute(piece, axis, [(i, i ^ o) for i in range(total)])]
    all_to_all x3 -> x2, waiting for transfers between devices: 24.6 us -> 16.3 us  [spread_out(): return lax.all_to_all(block, axis, split_axis=0, concat_axis=0, tiled=True)]
    pallas_call x6 -> x8, Pallas kernels: 7.08 us -> 9.87 us  [call(): pl.pallas_call(kernel, out_shape=out_shape, in_specs=[smem] * len(scalars...]
    unnamed x25 -> x16, local copies, waits for them, and re-layouts: 8.16 us -> 5.6 us
    pallas_call x1 -> x2, Pallas kernels: 6 us -> 4.59 us  [run_experts(): pl.pallas_call(functools.partial(expert_kernel, len(got)), grid=(owned,),...]
    all_to_all x3 -> x2, starting transfers between devices: 10.7 us -> 10.9 us  [spread_out(): return lax.all_to_all(block, axis, split_axis=0, concat_axis=0, tiled=True)]
  transfers between devices with their start and end apart: 9 -> 25, of which waited for: 5 -> 11; matrix products, arithmetic and copies ran while one was open for 0% -> 0% of each run, Pallas kernels for 1% -> 6%
where the time goes in v2:
time: 102 us
  waiting for transfers between devices  43.3 us (42%)
  starting transfers between devices  37.6 us (37%)
  Pallas kernels  14.5 us (14%)
  local copies, waits for them, and re-layouts  5.6 us (5%)
    ppermute x23, waiting for transfers between devices, swap(): lax.ppermute(piece, axis, [(i, i ^ o) for i in range(total)])  27 us
    ppermute x23, starting transfers between devices, swap(): lax.ppermute(piece, axis, [(i, i ^ o) for i in range(total)])  26.7 us
    all_to_all x2, waiting for transfers between devices, spread_out(): return lax.all_to_all(block, axis, split_axis=0, concat_axis=0, tiled=True)  16.3 us
    all_to_all x2, starting transfers between devices, spread_out(): return lax.all_to_all(block, axis, split_axis=0, concat_axis=0, tiled=True)  10.9 us
    pallas_call x8, Pallas kernels, call(): pl.pallas_call(kernel, out_shape=out_shape, in_specs=[smem] * len(scalars...  9.87 us
    unnamed x16, local copies, waits for them, and re-layouts  5.6 us
    pallas_call x2, Pallas kernels, run_experts(): pl.pallas_call(functools.partial(expert_kernel, len(got)), grid=(owned,),...  4.59 us
  transfers between devices with their start and end apart: 25, of which 11 were waited for; matrix products, arithmetic and copies ran while one was open for 0% of the time, Pallas kernels for 6%

profile of v2, /device:TPU:0, one launch (start us, length us, event | category | flops | bytes accessed | tf_op | source)
XLA Modules:
  0.0 101.8 jit_solution(9562737912483892313)
XLA Ops:
  0.7 2.3 %prep.1 = (bf16[8,64,512]{2,1,0:T(8,128)(2,1)}, bf16[272,256]{1,0:T(8,128)(2,1)}, bf16[272,256]{1,0:T(8,128)(2,1)}, bf16[272,256]{1,0:T(8,128)(2,1)}, bf16[272,256]{1,0:T(8,128)(2,1)}) custom-call(s32[1]{0:T(128)} %bitcast.me, bf16[512,256]{1,0:T(8,128)(2,1)} %refs_0_.1, f32[512,256]{1,0:T(8,128)} %refs_1_.1, bf16[512,256]{1,0:T(8,128)(2,1)} %refs_2_.2, ...), custom_call_target="tpu_custom_call" | custom-call | tf_op jit(solution)/shard_map/prep/pallas_call | solution.py:31
  3.0 7.3 %all-to-all-start = ((bf16[8,64,512]{2,1,0:T(8,128)(2,1)}), bf16[8,64,512]{2,1,0:T(8,128)(2,1)S(1)}, u32[]{:S(2)}, u32[]{:S(2)}) async-start(bf16[8,64,512]{2,1,0:T(8,128)(2,1)} %get-tuple-element.47), calls=%async_computation | async-start | bytes 1048576 | tf_op jit(solution)/shard_map/all_to_all | solution.py:343
  12.6 4.4 %collective-permute-done.1.refs_2_ = bf16[272,256]{1,0:T(8,128)(2,1)S(1)} collective-permute-done((bf16[272,256]{1,0:T(8,128)(2,1)}, bf16[272,256]{1,0:T(8,128)(2,1)S(1)}, u32[]{:S(2)}, u32[]{:S(2)}) %collective-permute-start.1) | collective-permute-done | bytes 139296 | tf_op jit(solution)/shard_map/ppermute | solution.py:337
  17.0 2.0 %collective-permute-done.2.refs_3_ = bf16[272,256]{1,0:T(8,128)(2,1)S(1)} collective-permute-done((bf16[272,256]{1,0:T(8,128)(2,1)}, bf16[272,256]{1,0:T(8,128)(2,1)S(1)}, u32[]{:S(2)}, u32[]{:S(2)}) %collective-permute-start.2) | collective-permute-done | bytes 139296 | tf_op jit(solution)/shard_map/ppermute | solution.py:337
  19.1 5.7 %all-to-all-done.got = bf16[8,64,512]{2,1,0:T(8,128)(2,1)S(1)} async-done(((bf16[8,64,512]{2,1,0:T(8,128)(2,1)}), bf16[8,64,512]{2,1,0:T(8,128)(2,1)S(1)}, u32[]{:S(2)}, u32[]{:S(2)}) %all-to-all-start) | async-done | bytes 524320 | tf_op jit(solution)/shard_map/all_to_all | solution.py:343
  24.7 3.5 %conv.1 = bf16[8,4,32,128]{3,2,1,0:T(8,128)(2,1)} custom-call(bf16[8,64,512]{2,1,0:T(8,128)(2,1)S(1)} %all-to-all-done.got, f32[8,512]{1,0:T(8,128)S(1)} %get-tuple-element.53.turn_cos, f32[8,512]{1,0:T(8,128)S(1)} %get-tuple-element.54.turn_sin, bf16[512,512]{1,0:T(8,128)(2,1)S(1)} %get-tuple-element.55.cos, bf16[512,512]{1,0:T(8,128)(2,1)S(1)} %get-tuple-element.56.sin), custom_call_target="tpu_custom_call" | custom-call | tf_op jit(solution)/shard_map/conv/pallas_call | solution.py:31
  28.2 3.7 %all-to-all-start.1 = ((bf16[32,32,128]{2,1,0:T(8,128)(2,1)}), bf16[32,32,128]{2,1,0:T(8,128)(2,1)S(1)}, u32[]{:S(2)}, u32[]{:S(2)}) async-start(bf16[32,32,128]{2,1,0:T(8,128)(2,1)} %bitcast.5), calls=%async_computation.1 | async-start | bytes 524288 | tf_op jit(solution)/shard_map/all_to_all | solution.py:343
  31.9 10.6 %all-to-all-done.1 = bf16[32,32,128]{2,1,0:T(8,128)(2,1)S(1)} async-done(((bf16[32,32,128]{2,1,0:T(8,128)(2,1)}), bf16[32,32,128]{2,1,0:T(8,128)(2,1)S(1)}, u32[]{:S(2)}, u32[]{:S(2)}) %all-to-all-start.1) | async-done | bytes 262176 | tf_op jit(solution)/shard_map/all_to_all | solution.py:343
  46.4 3.0 %collective-permute-start.4 = (bf16[64,1024]{1,0:T(8,128)(2,1)S(1)}, bf16[64,1024]{1,0:T(8,128)(2,1)S(1)}, u32[]{:S(2)}, u32[]{:S(2)}) collective-permute-start(bf16[64,1024]{1,0:T(8,128)(2,1)S(1)} %get-tuple-element.62), channel_id=1, source_target_pairs={{0,28},{4,24},{8,20},{12,16},{16,12},{20,8},{24,4},{28,0},{1,29},{... | collective-permute-start | bytes 393224 | tf_op jit(solution)/shard_map/ppermute | solution.py:337
  50.7 4.0 %collective-permute-done.7.refs_3_ = bf16[128,256]{1,0:T(8,128)(2,1)S(1)} collective-permute-done((bf16[128,256]{1,0:T(8,128)(2,1)S(1)}, bf16[128,256]{1,0:T(8,128)(2,1)S(1)}, u32[]{:S(2)}, u32[]{:S(2)}) %collective-permute-start.7) | collective-permute-done | bytes 65568 | tf_op jit(solution)/shard_map/ppermute | solution.py:337
  54.8 2.3 %collective-permute-start.12 = (bf16[64,1024]{1,0:T(8,128)(2,1)S(1)}, bf16[64,1024]{1,0:T(8,128)(2,1)S(1)}, u32[]{:S(2)}, u32[]{:S(2)}) collective-permute-start(bf16[64,1024]{1,0:T(8,128)(2,1)S(1)} %get-tuple-element.77), channel_id=1, source_target_pairs={{0,12},{4,8},{8,4},{12,0},{16,28},{20,24},{24,20},{28,16},{1,13},{... | collective-permute-start | bytes 393224 | tf_op jit(solution)/shard_map/ppermute | solution.py:337
  57.7 3.6 %collective-permute-start.9 = (bf16[64,1024]{1,0:T(8,128)(2,1)S(1)}, bf16[64,1024]{1,0:T(8,128)(2,1)S(1)}, u32[]{:S(2)}, u32[]{:S(2)}) collective-permute-start(bf16[64,1024]{1,0:T(8,128)(2,1)S(1)} %get-tuple-element.74), channel_id=1, source_target_pairs={{0,20},{4,16},{8,28},{12,24},{16,4},{20,0},{24,12},{28,8},{1,21},{... | collective-permute-start | bytes 393224 | tf_op jit(solution)/shard_map/ppermute | solution.py:337
  61.4 2.2 %copy-done = bf16[8,1024,256]{2,1,0:T(8,128)(2,1)S(1)} copy-done((bf16[8,1024,256]{2,1,0:T(8,128)(2,1)S(1)}, bf16[8,1024,256]{2,1,0:T(8,128)(2,1)}, u32[]{:S(2)}) %copy-start) | copy-done | bytes 4194328
  63.6 2.2 %copy-done.2 = bf16[8,256,1024]{2,1,0:T(8,128)(2,1)S(1)} copy-done((bf16[8,256,1024]{2,1,0:T(8,128)(2,1)S(1)}, bf16[8,256,1024]{2,1,0:T(8,128)(2,1)}, u32[]{:S(2)}) %copy-start.2) | copy-done | bytes 4194328
  65.7 2.2 %experts.3 = (bf16[64,1024]{1,0:T(8,128)(2,1)S(1)}, bf16[64,1024]{1,0:T(8,128)(2,1)S(1)}) custom-call(bf16[64,1024]{1,0:T(8,128)(2,1)S(1)} %collective-permute-done.3.refs_0_, bf16[64,1024]{1,0:T(8,128)(2,1)S(1)} %collective-permute-done.4.refs_1_, bf16[8,1024,256]{2,1,0:T(8,128)(2,1)S(1)} %copy-done, bf16[8,256,1024]{2,1,0:T(8,128)(2,1)S(1)} %copy-done.2), custom_call_target="tpu_custom_call" | custom-call | tf_op jit(solution)/shard_map/experts/pallas_call | solution.py:279
  69.6 1.7 %collective-permute-start.19 = (bf16[64,1024]{1,0:T(8,128)(2,1)S(1)}, bf16[64,1024]{1,0:T(8,128)(2,1)S(1)}, u32[]{:S(2)}, u32[]{:S(2)}) collective-permute-start(bf16[64,1024]{1,0:T(8,128)(2,1)S(1)} %get-tuple-element.87), channel_id=1, source_target_pairs={{0,28},{4,24},{8,20},{12,16},{16,12},{20,8},{24,4},{28,0},{1,29},{... | collective-permute-start | bytes 393224 | tf_op jit(solution)/shard_map/ppermute | solution.py:337
  71.4 7.3 %collective-permute-done.9.refs_2_ = bf16[64,1024]{1,0:T(8,128)(2,1)S(1)} collective-permute-done((bf16[64,1024]{1,0:T(8,128)(2,1)S(1)}, bf16[64,1024]{1,0:T(8,128)(2,1)S(1)}, u32[]{:S(2)}, u32[]{:S(2)}) %collective-permute-start.9) | collective-permute-done | bytes 131104 | tf_op jit(solution)/shard_map/ppermute | solution.py:337
  78.6 2.4 %experts.2 = (bf16[64,1024]{1,0:T(8,128)(2,1)S(1)}, bf16[64,1024]{1,0:T(8,128)(2,1)S(1)}, bf16[64,1024]{1,0:T(8,128)(2,1)S(1)}, bf16[64,1024]{1,0:T(8,128)(2,1)S...) custom-call(bf16[64,1024]{1,0:T(8,128)(2,1)S(1)} %get-tuple-element.72.refs_0_, ...), custom_call_target="tpu_custom_call" | custom-call | tf_op jit(solution)/shard_map/experts/pallas_call | solution.py:279
  81.6 3.0 %collective-permute-start.15 = (bf16[64,1024]{1,0:T(8,128)(2,1)S(1)}, bf16[64,1024]{1,0:T(8,128)(2,1)S(1)}, u32[]{:S(2)}, u32[]{:S(2)}) collective-permute-start(bf16[64,1024]{1,0:T(8,128)(2,1)S(1)} %get-tuple-element.81), channel_id=1, source_target_pairs={{0,12},{4,8},{8,4},{12,0},{16,28},{20,24},{24,20},{28,16},{1,13},{... | collective-permute-start | bytes 393224 | tf_op jit(solution)/shard_map/ppermute | solution.py:337
  84.8 2.7 %collective-permute-start.17 = (bf16[64,1024]{1,0:T(8,128)(2,1)S(1)}, bf16[64,1024]{1,0:T(8,128)(2,1)S(1)}, u32[]{:S(2)}, u32[]{:S(2)}) collective-permute-start(bf16[64,1024]{1,0:T(8,128)(2,1)S(1)} %get-tuple-element.83), channel_id=1, source_target_pairs={{0,20},{4,16},{8,28},{12,24},{16,4},{20,0},{24,12},{28,8},{1,21},{... | collective-permute-start | bytes 393224 | tf_op jit(solution)/shard_map/ppermute | solution.py:337
  88.5 2.6 %collective-permute-done.15.refs_3_ = bf16[64,1024]{1,0:T(8,128)(2,1)S(1)} collective-permute-done((bf16[64,1024]{1,0:T(8,128)(2,1)S(1)}, bf16[64,1024]{1,0:T(8,128)(2,1)S(1)}, u32[]{:S(2)}, u32[]{:S(2)}) %collective-permute-start.15) | collective-permute-done | bytes 131104 | tf_op jit(solution)/shard_map/ppermute | solution.py:337
  91.1 2.2 %collective-permute-done.16.refs_4_ = bf16[64,1024]{1,0:T(8,128)(2,1)S(1)} collective-permute-done((bf16[64,1024]{1,0:T(8,128)(2,1)S(1)}, bf16[64,1024]{1,0:T(8,128)(2,1)S(1)}, u32[]{:S(2)}, u32[]{:S(2)}) %collective-permute-start.16) | collective-permute-done | bytes 131104 | tf_op jit(solution)/shard_map/ppermute | solution.py:337
  95.7 1.8 %collective-permute-start.22 = (bf16[128,256]{1,0:T(8,128)(2,1)S(1)}, bf16[128,256]{1,0:T(8,128)(2,1)S(1)}, u32[]{:S(2)}, u32[]{:S(2)}) collective-permute-start(bf16[128,256]{1,0:T(8,128)(2,1)S(1)} %get-tuple-element.91), channel_id=1, source_target_pairs={{0,3},{1,2},{2,1},{3,0},{4,7},{5,6},{6,5},{7,4},{8,11},{9,10},{10,... | collective-permute-start | bytes 196616 | tf_op jit(solution)/shard_map/ppermute | solution.py:337
  98.2 2.4 %collective-permute-done.21.refs_2_ = bf16[128,256]{1,0:T(8,128)(2,1)S(1)} collective-permute-done((bf16[128,256]{1,0:T(8,128)(2,1)S(1)}, bf16[128,256]{1,0:T(8,128)(2,1)S(1)}, u32[]{:S(2)}, u32[]{:S(2)}) %collective-permute-start.21) | collective-permute-done | bytes 65568 | tf_op jit(solution)/shard_map/ppermute | solution.py:337
  (52 shorter events, 16.0 us)
Async XLA Ops:
  3.0 21.8 %all-to-all-start = ((bf16[8,64,512]{2,1,0:T(8,128)(2,1)}), bf16[8,64,512]{2,1,0:T(8,128)(2,1)S(1)}, u32[]{:S(2)}, u32[]{:S(2)}) async-start(bf16[8,64,512]{2,1,0:T(8,128)(2,1)} %get-tuple-element.47), calls=%async_computation | async-start | bytes 1048576 | tf_op jit(solution)/shard_map/all_to_all | solution.py:343
  10.2 6.8 %collective-permute-start.1 = (bf16[272,256]{1,0:T(8,128)(2,1)}, bf16[272,256]{1,0:T(8,128)(2,1)S(1)}, u32[]{:S(2)}, u32[]{:S(2)}) collective-permute-start(bf16[272,256]{1,0:T(8,128)(2,1)} %get-tuple-element.50), channel_id=1, source_target_pairs={{0,2},{1,3},{2,0},{3,1},{4,6},{5,7},{6,4},{7,5},{8,10},{9,11},{10,... | collective-permute-start | bytes 417800 | tf_op jit(solution)/shard_map/ppermute | solution.py:337
  11.8 7.2 %collective-permute-start.2 = (bf16[272,256]{1,0:T(8,128)(2,1)}, bf16[272,256]{1,0:T(8,128)(2,1)S(1)}, u32[]{:S(2)}, u32[]{:S(2)}) collective-permute-start(bf16[272,256]{1,0:T(8,128)(2,1)} %get-tuple-element.51), channel_id=1, source_target_pairs={{0,3},{1,2},{2,1},{3,0},{4,7},{5,6},{6,5},{7,4},{8,11},{9,10},{10,... | collective-permute-start | bytes 417800 | tf_op jit(solution)/shard_map/ppermute | solution.py:337
  28.2 14.3 %all-to-all-start.1 = ((bf16[32,32,128]{2,1,0:T(8,128)(2,1)}), bf16[32,32,128]{2,1,0:T(8,128)(2,1)S(1)}, u32[]{:S(2)}, u32[]{:S(2)}) async-start(bf16[32,32,128]{2,1,0:T(8,128)(2,1)} %bitcast.5), calls=%async_computation.1 | async-start | bytes 524288 | tf_op jit(solution)/shard_map/all_to_all | solution.py:343
  44.3 6.2 %collective-permute-start.5 = (bf16[128,256]{1,0:T(8,128)(2,1)S(1)}, bf16[128,256]{1,0:T(8,128)(2,1)S(1)}, u32[]{:S(2)}, u32[]{:S(2)}) collective-permute-start(bf16[128,256]{1,0:T(8,128)(2,1)S(1)} %get-tuple-element.64), channel_id=1, source_target_pairs={{0,1},{1,0},{2,3},{3,2},{4,5},{5,4},{6,7},{7,6},{8,9},{9,8},{10,11... | collective-permute-start | bytes 196616 | tf_op jit(solution)/shard_map/ppermute | solution.py:337
  44.3 6.1 %collective-permute-start.6 = (bf16[128,256]{1,0:T(8,128)(2,1)S(1)}, bf16[128,256]{1,0:T(8,128)(2,1)S(1)}, u32[]{:S(2)}, u32[]{:S(2)}) collective-permute-start(bf16[128,256]{1,0:T(8,128)(2,1)S(1)} %get-tuple-element.65), channel_id=1, source_target_pairs={{0,2},{1,3},{2,0},{3,1},{4,6},{5,7},{6,4},{7,5},{8,10},{9,11},{10,... | collective-permute-start | bytes 196616 | tf_op jit(solution)/shard_map/ppermute | solution.py:337
  45.2 11.9 %collective-permute-start.3 = (bf16[64,1024]{1,0:T(8,128)(2,1)S(1)}, bf16[64,1024]{1,0:T(8,128)(2,1)S(1)}, u32[]{:S(2)}, u32[]{:S(2)}) collective-permute-start(bf16[64,1024]{1,0:T(8,128)(2,1)S(1)} %get-tuple-element.61), channel_id=1, source_target_pairs={{0,24},{4,28},{8,16},{12,20},{16,8},{20,12},{24,0},{28,4},{1,25},{... | collective-permute-start | bytes 393224 | tf_op jit(solution)/shard_map/ppermute | solution.py:337
  46.4 11.3 %collective-permute-start.4 = (bf16[64,1024]{1,0:T(8,128)(2,1)S(1)}, bf16[64,1024]{1,0:T(8,128)(2,1)S(1)}, u32[]{:S(2)}, u32[]{:S(2)}) collective-permute-start(bf16[64,1024]{1,0:T(8,128)(2,1)S(1)} %get-tuple-element.62), channel_id=1, source_target_pairs={{0,28},{4,24},{8,20},{12,16},{16,12},{20,8},{24,4},{28,0},{1,29},{... | collective-permute-start | bytes 393224 | tf_op jit(solution)/shard_map/ppermute | solution.py:337
  49.4 18.5 %collective-permute-start.10 = (bf16[64,1024]{1,0:T(8,128)(2,1)S(1)}, bf16[64,1024]{1,0:T(8,128)(2,1)S(1)}, u32[]{:S(2)}, u32[]{:S(2)}) collective-permute-start(bf16[64,1024]{1,0:T(8,128)(2,1)S(1)} %get-tuple-element.75), channel_id=1, source_target_pairs={{0,4},{4,0},{8,12},{12,8},{16,20},{20,16},{24,28},{28,24},{1,5},{5... | collective-permute-start | bytes 393224 | tf_op jit(solution)/shard_map/ppermute | solution.py:337
  50.4 19.2 %collective-permute-start.11 = (bf16[64,1024]{1,0:T(8,128)(2,1)S(1)}, bf16[64,1024]{1,0:T(8,128)(2,1)S(1)}, u32[]{:S(2)}, u32[]{:S(2)}) collective-permute-start(bf16[64,1024]{1,0:T(8,128)(2,1)S(1)} %get-tuple-element.76), channel_id=1, source_target_pairs={{0,8},{4,12},{8,0},{12,4},{16,24},{20,28},{24,16},{28,20},{1,9},{5... | collective-permute-start | bytes 393224 | tf_op jit(solution)/shard_map/ppermute | solution.py:337
  50.5 4.3 %collective-permute-start.7 = (bf16[128,256]{1,0:T(8,128)(2,1)S(1)}, bf16[128,256]{1,0:T(8,128)(2,1)S(1)}, u32[]{:S(2)}, u32[]{:S(2)}) collective-permute-start(bf16[128,256]{1,0:T(8,128)(2,1)S(1)} %get-tuple-element.66), channel_id=1, source_target_pairs={{0,3},{1,2},{2,1},{3,0},{4,7},{5,6},{6,5},{7,4},{8,11},{9,10},{10,... | collective-permute-start | bytes 196616 | tf_op jit(solution)/shard_map/ppermute | solution.py:337
  54.8 16.6 %collective-permute-start.12 = (bf16[64,1024]{1,0:T(8,128)(2,1)S(1)}, bf16[64,1024]{1,0:T(8,128)(2,1)S(1)}, u32[]{:S(2)}, u32[]{:S(2)}) collective-permute-start(bf16[64,1024]{1,0:T(8,128)(2,1)S(1)} %get-tuple-element.77), channel_id=1, source_target_pairs={{0,12},{4,8},{8,4},{12,0},{16,28},{20,24},{24,20},{28,16},{1,13},{... | collective-permute-start | bytes 393224 | tf_op jit(solution)/shard_map/ppermute | solution.py:337
  57.0 14.3 %collective-permute-start.8 = (bf16[64,1024]{1,0:T(8,128)(2,1)S(1)}, bf16[64,1024]{1,0:T(8,128)(2,1)S(1)}, u32[]{:S(2)}, u32[]{:S(2)}) collective-permute-start(bf16[64,1024]{1,0:T(8,128)(2,1)S(1)} %get-tuple-element.73), channel_id=1, source_target_pairs={{0,16},{4,20},{8,24},{12,28},{16,0},{20,4},{24,8},{28,12},{1,17},{... | collective-permute-start | bytes 393224 | tf_op jit(solution)/shard_map/ppermute | solution.py:337
  57.7 20.9 %collective-permute-start.9 = (bf16[64,1024]{1,0:T(8,128)(2,1)S(1)}, bf16[64,1024]{1,0:T(8,128)(2,1)S(1)}, u32[]{:S(2)}, u32[]{:S(2)}) collective-permute-start(bf16[64,1024]{1,0:T(8,128)(2,1)S(1)} %get-tuple-element.74), channel_id=1, source_target_pairs={{0,20},{4,16},{8,28},{12,24},{16,4},{20,0},{24,12},{28,8},{1,21},{... | collective-permute-start | bytes 393224 | tf_op jit(solution)/shard_map/ppermute | solution.py:337
  68.0 16.6 %collective-permute-start.18 = (bf16[64,1024]{1,0:T(8,128)(2,1)S(1)}, bf16[64,1024]{1,0:T(8,128)(2,1)S(1)}, u32[]{:S(2)}, u32[]{:S(2)}) collective-permute-start(bf16[64,1024]{1,0:T(8,128)(2,1)S(1)} %get-tuple-element.86), channel_id=1, source_target_pairs={{0,24},{4,28},{8,16},{12,20},{16,8},{20,12},{24,0},{28,4},{1,25},{... | collective-permute-start | bytes 393224 | tf_op jit(solution)/shard_map/ppermute | solution.py:337
  69.6 15.2 %collective-permute-start.19 = (bf16[64,1024]{1,0:T(8,128)(2,1)S(1)}, bf16[64,1024]{1,0:T(8,128)(2,1)S(1)}, u32[]{:S(2)}, u32[]{:S(2)}) collective-permute-start(bf16[64,1024]{1,0:T(8,128)(2,1)S(1)} %get-tuple-element.87), channel_id=1, source_target_pairs={{0,28},{4,24},{8,20},{12,16},{16,12},{20,8},{24,4},{28,0},{1,29},{... | collective-permute-start | bytes 393224 | tf_op jit(solution)/shard_map/ppermute | solution.py:337
  81.0 7.5 %collective-permute-start.13 = (bf16[64,1024]{1,0:T(8,128)(2,1)S(1)}, bf16[64,1024]{1,0:T(8,128)(2,1)S(1)}, u32[]{:S(2)}, u32[]{:S(2)}) collective-permute-start(bf16[64,1024]{1,0:T(8,128)(2,1)S(1)} %get-tuple-element.79), channel_id=1, source_target_pairs={{0,4},{4,0},{8,12},{12,8},{16,20},{20,16},{24,28},{28,24},{1,5},{5... | collective-permute-start | bytes 393224 | tf_op jit(solution)/shard_map/ppermute | solution.py:337
  81.6 6.9 %collective-permute-start.14 = (bf16[64,1024]{1,0:T(8,128)(2,1)S(1)}, bf16[64,1024]{1,0:T(8,128)(2,1)S(1)}, u32[]{:S(2)}, u32[]{:S(2)}) collective-permute-start(bf16[64,1024]{1,0:T(8,128)(2,1)S(1)} %get-tuple-element.80), channel_id=1, source_target_pairs={{0,8},{4,12},{8,0},{12,4},{16,24},{20,28},{24,16},{28,20},{1,9},{5... | collective-permute-start | bytes 393224 | tf_op jit(solution)/shard_map/ppermute | solution.py:337
  81.6 9.5 %collective-permute-start.15 = (bf16[64,1024]{1,0:T(8,128)(2,1)S(1)}, bf16[64,1024]{1,0:T(8,128)(2,1)S(1)}, u32[]{:S(2)}, u32[]{:S(2)}) collective-permute-start(bf16[64,1024]{1,0:T(8,128)(2,1)S(1)} %get-tuple-element.81), channel_id=1, source_target_pairs={{0,12},{4,8},{8,4},{12,0},{16,28},{20,24},{24,20},{28,16},{1,13},{... | collective-permute-start | bytes 393224 | tf_op jit(solution)/shard_map/ppermute | solution.py:337
  84.6 8.7 %collective-permute-start.16 = (bf16[64,1024]{1,0:T(8,128)(2,1)S(1)}, bf16[64,1024]{1,0:T(8,128)(2,1)S(1)}, u32[]{:S(2)}, u32[]{:S(2)}) collective-permute-start(bf16[64,1024]{1,0:T(8,128)(2,1)S(1)} %get-tuple-element.82), channel_id=1, source_target_pairs={{0,16},{4,20},{8,24},{12,28},{16,0},{20,4},{24,8},{28,12},{1,17},{... | collective-permute-start | bytes 393224 | tf_op jit(solution)/shard_map/ppermute | solution.py:337
  84.8 10.0 %collective-permute-start.17 = (bf16[64,1024]{1,0:T(8,128)(2,1)S(1)}, bf16[64,1024]{1,0:T(8,128)(2,1)S(1)}, u32[]{:S(2)}, u32[]{:S(2)}) collective-permute-start(bf16[64,1024]{1,0:T(8,128)(2,1)S(1)} %get-tuple-element.83), channel_id=1, source_target_pairs={{0,20},{4,16},{8,28},{12,24},{16,4},{20,0},{24,12},{28,8},{1,21},{... | collective-permute-start | bytes 393224 | tf_op jit(solution)/shard_map/ppermute | solution.py:337
  95.5 2.7 %collective-permute-start.20 = (bf16[128,256]{1,0:T(8,128)(2,1)S(1)}, bf16[128,256]{1,0:T(8,128)(2,1)S(1)}, u32[]{:S(2)}, u32[]{:S(2)}) collective-permute-start(bf16[128,256]{1,0:T(8,128)(2,1)S(1)} %get-tuple-element.89), channel_id=1, source_target_pairs={{0,1},{1,0},{2,3},{3,2},{4,5},{5,4},{6,7},{7,6},{8,9},{9,8},{10,11... | collective-permute-start | bytes 196616 | tf_op jit(solution)/shard_map/ppermute | solution.py:337
  95.6 5.0 %collective-permute-start.21 = (bf16[128,256]{1,0:T(8,128)(2,1)S(1)}, bf16[128,256]{1,0:T(8,128)(2,1)S(1)}, u32[]{:S(2)}, u32[]{:S(2)}) collective-permute-start(bf16[128,256]{1,0:T(8,128)(2,1)S(1)} %get-tuple-element.90), channel_id=1, source_target_pairs={{0,2},{1,3},{2,0},{3,1},{4,6},{5,7},{6,4},{7,5},{8,10},{9,11},{10,... | collective-permute-start | bytes 196616 | tf_op jit(solution)/shard_map/ppermute | solution.py:337
  95.7 5.4 %collective-permute-start.22 = (bf16[128,256]{1,0:T(8,128)(2,1)S(1)}, bf16[128,256]{1,0:T(8,128)(2,1)S(1)}, u32[]{:S(2)}, u32[]{:S(2)}) collective-permute-start(bf16[128,256]{1,0:T(8,128)(2,1)S(1)} %get-tuple-element.91), channel_id=1, source_target_pairs={{0,3},{1,2},{2,1},{3,0},{4,7},{5,6},{6,5},{7,4},{8,11},{9,10},{10,... | collective-permute-start | bytes 196616 | tf_op jit(solution)/shard_map/ppermute | solution.py:337
  (8 other events, 113.2 us)

commit v3 on v2

--- a/solution.py
+++ b/solution.py
@@ -9,9 +9,8 @@
 from jax.sharding import PartitionSpec as P
 
 CAP = 16
-SKIP_ROWS = 16
-VMEM_LIMIT = 40 * 1024 * 1024
-PREP_LIMIT = 62 * 1024 * 1024
+VMEM_LIMIT = 16 * 1024 * 1024
+FULL_LIMIT = 62 * 1024 * 1024
 
 f32 = jnp.float32
 bf16 = jnp.bfloat16
@@ -21,7 +20,7 @@
     return pltpu.CompilerParams(vmem_limit_bytes=limit)
 
 
-def call(kernel, out_shape, scalars, far, operands, name, scratch=(), limit=VMEM_LIMIT):
+def call(kernel, out_shape, scalars, far, operands, name, scratch=(), limit=VMEM_LIMIT, cost=None):
     vmem = pl.BlockSpec(memory_space=pltpu.VMEM)
     smem = pl.BlockSpec(memory_space=pltpu.SMEM)
     hbm = pl.BlockSpec(memory_space=pltpu.HBM)
@@ -35,6 +34,7 @@
         out_specs=jax.tree.map(lambda _: vmem, out_shape),
         scratch_shapes=scratch,
         compiler_params=params(limit),
+        cost_estimate=cost,
         name=name,
     )(*scalars, *far, *operands)
 
@@ -97,11 +97,10 @@
     sin[...] = wide_sin[...].astype(bf16)
 
 
-def prep_kernel(groups, blocks, me, *refs):
-    far, refs = refs[:4], refs[4:]
-    spread, pieces, held, sems = refs[0], refs[1 : 1 + blocks], refs[1 + blocks : -1], refs[-1]
-    copies = fetch(far, held, sems)
-    sig, taps, gate, skip = held
+def prep_kernel(groups, at, *refs):
+    far, refs = refs[:2], refs[2:]
+    skip, spread, sig, taps, sems = refs
+    copies = fetch(far, (sig, taps), sems)
     tok, chans = sig.shape
     per = chans // groups
     copies[0].wait()
@@ -109,27 +108,23 @@
     for g in range(groups):
         spread[g, :per, :] = sig_t[g * per : (g + 1) * per, :]
     copies[1].wait()
+    taps[0:1, :] = taps[0:1, :] + jnp.where(at[0] == 0, skip[...], 0.0)
     tap_t = taps[...].T.astype(bf16)
     for g in range(groups):
         spread[g, per:, :] = tap_t[g * per : (g + 1) * per, :]
-    copies[2].wait()
-    copies[3].wait()
-    rows = tok // blocks
-    own = skip[...]
-    first = own.astype(bf16)
-    own = own - first.astype(f32)
-    second = own.astype(bf16)
-    third = (own - second.astype(f32)).astype(bf16)
-    row = lax.broadcasted_iota(jnp.int32, (SKIP_ROWS, chans), 0)
-    wide = jnp.zeros((SKIP_ROWS, chans), f32)
-    for i, term in enumerate((first, second, third)):
-        wide = jnp.where(row == i, term.astype(f32), wide)
-    wide = wide.astype(bf16)
-    for o in range(blocks):
+
+
+def split_kernel(me, whole, *refs):
+    pieces, sems = refs[:-1], refs[-1]
+    rows = pieces[0].shape[0]
+    copies = []
+    for o, piece in enumerate(pieces):
         start = pl.multiple_of((me[0] ^ o) * rows, rows)
-        pieces[o][:rows, :] = gate[pl.ds(start, rows), :]
-        pieces[o][rows : 2 * rows, :] = sig[pl.ds(start, rows), :]
-        pieces[o][2 * rows :, :] = wide
+        copies.append(pltpu.make_async_copy(whole.at[pl.ds(start, rows), :], piece, sems.at[o]))
+    for copy in copies:
+        copy.start()
+    for copy in copies:
+        copy.wait()
 
 
 def conv_kernel(blocks, got, turn_cos, turn_sin, cos, sin, out, are, aim, pre, pim):
@@ -208,13 +203,8 @@
     square = jnp.zeros((rows, 1), f32)
     for o in range(blocks):
         group = me[0] ^ o
-        piece = pieces[o]
-        gate = piece[:rows, :].astype(f32)
-        sig = piece[rows : 2 * rows, :].astype(f32)
-        skip = piece[2 * rows :, :].astype(f32)
-        skip = skip[0:1, :] + skip[1:2, :] + skip[2:3, :]
         y = conv[:, group, :, :].astype(f32).reshape(chans, rows).T
-        value = (gate * (y + skip * sig)).astype(bf16)
+        value = (pieces[o][...].astype(f32) * y).astype(bf16)
         mixed[group] = value
         mixed_out[o][...] = value
         value = value.astype(f32)
@@ -255,40 +245,51 @@
         gates[:, k : k + 1] = jax.nn.sigmoid(value)
 
 
-def expert_kernel(count, *refs):
-    got, (up, down), out = refs[:count], refs[count : count + 2], refs[count + 2 :]
+def expert_kernel(count, owned, up, down, *refs):
+    got, out, token, x = refs[:count], refs[-2 - count : -2], refs[-2], refs[-1]
+    group = up.shape[0] // owned
     width = up.shape[1]
-    rows = math.prod(got[0].shape[:-1])
-    x = jnp.concatenate([piece[...].reshape(rows, width) for piece in got], axis=0)
-    total = jnp.zeros(x.shape, f32)
-    for p in range(up.shape[0]):
-        hidden = jnp.dot(x, up[p], preferred_element_type=f32)
-        hidden = jax.nn.gelu(hidden, approximate=True).astype(bf16)
-        total = total + jnp.dot(hidden, down[p], preferred_element_type=f32)
-    total = total.astype(bf16)
-    for i, piece in enumerate(out):
-        piece[...] = total[i * rows : (i + 1) * rows].reshape(piece.shape)
-
-
-def run_experts(got, w_up, w_down, owned, group):
+    for e in range(owned):
+        pieces = []
+        for piece in got:
+            if len(piece.shape) == 2:
+                pieces.append(piece[e * CAP : (e + 1) * CAP, :])
+            else:
+                slots = piece[:, e * CAP : (e + 1) * CAP, :]
+                pieces.append(slots.reshape(piece.shape[0] * CAP, width))
+        x[...] = jnp.concatenate(pieces, axis=0)
+        total = jnp.zeros(x.shape, f32)
+        for p in range(e * group, (e + 1) * group):
+            hidden = jnp.dot(x[...], up[p], preferred_element_type=f32)
+            hidden = jax.nn.gelu(hidden, approximate=True).astype(bf16)
+            total = total + jnp.dot(hidden, down[p], preferred_element_type=f32)
+        total = total.astype(bf16)
+        rows = total.shape[0] // count
+        for i, piece in enumerate(out):
+            part = total[i * rows : (i + 1) * rows]
+            if len(piece.shape) == 2:
+                piece[e * CAP : (e + 1) * CAP, :] = part
+            else:
+                piece[:, e * CAP : (e + 1) * CAP, :] = part.reshape(piece.shape[0], CAP, width)
+    token[...] = jnp.zeros(token.shape, f32)
+
+
+def run_experts(got, w_up, w_down, owned, after):
     width = got[0].shape[-1]
-    if got[0].ndim == 2:
-        slot = pl.BlockSpec((CAP, width), lambda e: (e, 0))
-    else:
-        slot = pl.BlockSpec((got[0].shape[0], CAP, width), lambda e: (0, e, 0))
-    return pl.pallas_call(
-        functools.partial(expert_kernel, len(got)),
-        grid=(owned,),
-        out_shape=[jax.ShapeDtypeStruct(x.shape, x.dtype) for x in got],
-        in_specs=[slot] * len(got)
-        + [
-            pl.BlockSpec((group,) + w_up.shape[1:], lambda e: (e, 0, 0)),
-            pl.BlockSpec((group,) + w_down.shape[1:], lambda e: (e, 0, 0)),
-        ],
-        out_specs=[slot] * len(got),
+    slots = sum(math.prod(x.shape[:-1]) for x in got) // owned
+    vmem = pl.BlockSpec(memory_space=pltpu.VMEM)
+    *result, token = pl.pallas_call(
+        functools.partial(expert_kernel, len(got), owned),
+        out_shape=[jax.ShapeDtypeStruct(x.shape, x.dtype) for x in got]
+        + [jax.ShapeDtypeStruct((8, 128), f32)],
+        in_specs=[vmem] * (2 + len(got) + len(after)),
+        out_specs=[vmem] * (len(got) + 1),
+        scratch_shapes=[pltpu.VMEM((slots, width), bf16)],
         compiler_params=params(),
+        cost_estimate=pl.CostEstimate(flops=1, bytes_accessed=1, transcendentals=0),
         name="experts",
-    )(*got, w_up, w_down)
+    )(w_up, w_down, *got, *after)
+    return result, [token]
 
 
 def combine_kernel(experts, blocks, shards, me, at, routes_t, gates, *refs):
@@ -325,11 +326,43 @@
 
 
 def place_kernel(me, *refs):
-    pieces, out = refs[:-1], refs[-1]
+    pieces, out, sems = refs[:-2], refs[-2], refs[-1]
     rows = pieces[0].shape[0]
+    copies = []
     for o, piece in enumerate(pieces):
         start = pl.multiple_of((me[0] ^ o) * rows, rows)
-        out[pl.ds(start, rows), :] = piece[...]
+        copies.append(pltpu.make_async_copy(piece, out.at[pl.ds(start, rows), :], sems.at[o]))
+    for copy in copies:
+        copy.start()
+    for copy in copies:
+        copy.wait()
+
+
+def split(whole, me, count):
+    shape = (whole.shape[0] // count, whole.shape[1])
+    return pl.pallas_call(
+        split_kernel,
+        out_shape=[jax.ShapeDtypeStruct(shape, whole.dtype)] * count,
+        in_specs=[pl.BlockSpec(memory_space=pltpu.SMEM), pl.BlockSpec(memory_space=pltpu.HBM)],
+        out_specs=[pl.BlockSpec(memory_space=pltpu.VMEM)] * count,
+        scratch_shapes=[pltpu.SemaphoreType.DMA((count,))],
+        compiler_params=params(),
+        name="split",
+    )(me, whole)
+
+
+def place(pieces, me):
+    count, (rows, width) = len(pieces), pieces[0].shape
+    return pl.pallas_call(
+        place_kernel,
+        out_shape=jax.ShapeDtypeStruct((count * rows, width), pieces[0].dtype),
+        in_specs=[pl.BlockSpec(memory_space=pltpu.SMEM)]
+        + [pl.BlockSpec(memory_space=pltpu.VMEM)] * count,
+        out_specs=pl.BlockSpec(memory_space=pltpu.HBM),
+        scratch_shapes=[pltpu.SemaphoreType.DMA((count,))],
+        compiler_params=params(),
+        name="place",
+    )(me, *pieces)
 
 
 def swap(pieces, axis, offsets, total):
@@ -350,7 +383,6 @@
     experts = router.shape[1]
     parts = w_up.shape[0]
     owned = max(1, parts // 2)
-    group = min(parts, 2)
     size = owned * CAP
     direct = 4 <= shards <= 8
     me = lax.axis_index("ch").astype(jnp.int32).reshape(1)
@@ -358,15 +390,16 @@
     shape = jax.ShapeDtypeStruct
     around = list(range(blocks))
 
-    spread, *pieces = call(
-        functools.partial(prep_kernel, shards, blocks),
-        [shape((shards, 2 * per, tok), bf16)] + [shape((2 * rows + SKIP_ROWS, chans), bf16)] * blocks,
-        [me],
-        [signal, taps, gate_v, skip.reshape(1, chans)],
-        [],
+    spread = call(
+        functools.partial(prep_kernel, shards),
+        shape((shards, 2 * per, tok), bf16),
+        [at],
+        [signal, taps],
+        [skip.reshape(1, chans)],
         "prep",
-        limit=PREP_LIMIT,
-    )
+        limit=FULL_LIMIT,
+    )
+    pieces = split(gate_v, me, blocks)
     turns = call(
         tables_kernel,
         [shape((shards, tok), f32)] * 2 + [shape((tok, tok), bf16)] * 2,
@@ -377,8 +410,9 @@
         [pltpu.VMEM((tok, tok), f32)] * 2,
     )
     got = spread_out(spread, "ctx")
-    pieces = swap(pieces, "ch", around, blocks)
+    own, *pieces = swap(pieces, "ch", around, blocks)
     got, pieces = lax.optimization_barrier((got, pieces))
+    pieces = [own, *pieces]
     conv = call(
         functools.partial(conv_kernel, blocks),
         shape((shards, blocks, per, rows), bf16),
@@ -407,25 +441,23 @@
     mixed, send, normed = mixed_and_send[:blocks], mixed_and_send[blocks:-1], mixed_and_send[-1]
     gates = call(gates_kernel, shape((rows, 2), f32), [], [], [normed, router, routes], "gates")
     if direct:
+        (own,), done = run_experts(send[:1], w_up, w_down, owned, [])
+        home = {0: own}
         half = shards // 2
-        split = half + half // 2
-        early = [0, *range(half, split), *range(1, half)]
-        late = list(range(split, shards))
-        there = swap([send[o] for o in early], "ctx", early, shards)
-        there_late = swap([send[o] for o in late], "ctx", late, shards)
+        cut = half + half // 2
+        groups = [[*range(half, cut), *range(1, half)], list(range(cut, shards))]
+        there = [swap([send[o] for o in group], "ctx", group, shards) for group in groups]
+        for i, group in enumerate(groups):
+            result, done = run_experts(there[i], w_up, w_down, owned, done)
+            home.update(zip(group, swap(result, "ctx", group, shards)))
+        back = [home[o] for o in range(shards)]
         mixed = swap(mixed, "ch", around, blocks)
-        result = run_experts(there, w_up, w_down, owned, group)
-        home = dict(zip(early, swap(result, "ctx", early, shards)))
-        there_late, mixed = lax.optimization_barrier((there_late, mixed))
-        result = run_experts(there_late, w_up, w_down, owned, group)
-        home.update(zip(late, swap(result, "ctx", late, shards)))
-        back = [home[o] for o in range(shards)]
     else:
         there = spread_out(send[0], "ctx")
         mixed = swap(mixed, "ch", around, blocks)
-        (result,) = run_experts([there], w_up, w_down, owned, group)
+        (result,), _ = run_experts([there], w_up, w_down, owned, [])
         back = [spread_out(result, "ctx")]
-    mixed = call(place_kernel, shape((tok, chans), bf16), [me], [], mixed, "place")
+    mixed = place(mixed, me)
     moe = call(
         functools.partial(combine_kernel, experts, blocks, shards),
         [shape((rows, chans), bf16)] * blocks,
@@ -436,8 +468,7 @@
         [pltpu.VMEM((shards, size, width), bf16)],
     )
     moe = swap(moe, "ch", around, blocks)
-    moe_out = call(place_kernel, shape((tok, chans), bf16), [me], [], moe, "place")
-    return (mixed, moe_out)
+    return (mixed, place(moe, me))
 
 
 def solution(mesh):

time: 102 us -> 96.4 us (0.945)
  waiting for transfers between devices: 43.3 us -> 18.9 us
  blocking collectives: 0 us -> 14.1 us
  starting transfers between devices: 37.6 us -> 40.8 us
  Pallas kernels: 14.5 us -> 15.9 us
    ppermute x23, waiting for transfers between devices: 27 us -> 11.4 us  [swap(): lax.ppermute(piece, axis, [(i, i ^ o) for i in range(total)])]
    all_to_all x0 -> x1, blocking collectives: none -> 14.1 us  [spread_out(): return lax.all_to_all(block, axis, split_axis=0, concat_axis=0, tiled=True)]
    all_to_all x2 -> x1, waiting for transfers between devices: 16.3 us -> 7.47 us  [spread_out(): return lax.all_to_all(block, axis, split_axis=0, concat_axis=0, tiled=True)]
    ppermute x23, starting transfers between devices: 26.7 us -> 33.5 us  [swap(): lax.ppermute(piece, axis, [(i, i ^ o) for i in range(total)])]
    all_to_all x2 -> x1, starting transfers between devices: 10.9 us -> 7.26 us  [spread_out(): return lax.all_to_all(block, axis, split_axis=0, concat_axis=0, tiled=True)]
    pallas_call x2 -> x6, Pallas kernels: 4.59 us -> 7.78 us  [the longest x3 5.99 us: run_experts(): pl.pallas_call(functools.partial(expert_kernel, len(got), owned), out_sha...]
    pallas_call x8 -> x6, Pallas kernels: 9.87 us -> 8.11 us  [call(): pl.pallas_call(kernel, out_shape=out_shape, in_specs=[smem] * len(scalars...]
    unnamed x16 -> x18, local copies, waits for them, and re-layouts: 5.6 us -> 5.65 us
  transfers between devices with their start and end apart: 25 -> 24, of which waited for: 11 -> 9; matrix products, arithmetic and copies ran while one was open for 0% -> 0% of each run, Pallas kernels for 6% -> 9%
where the time goes in v3:
time: 96.4 us; the launch traced here: 96 us
  starting transfers between devices  40.8 us (42%)
  waiting for transfers between devices  18.9 us (20%)
  Pallas kernels  15.9 us (16%)
  blocking collectives  14.1 us (15%)
  local copies, waits for them, and re-layouts  5.65 us (6%)
    ppermute x23, starting transfers between devices, swap(): lax.ppermute(piece, axis, [(i, i ^ o) for i in range(total)])  33.5 us
    all_to_all x1, blocking collectives, spread_out(): return lax.all_to_all(block, axis, split_axis=0, concat_axis=0, tiled=True)  14.1 us
    ppermute x23, waiting for transfers between devices, swap(): lax.ppermute(piece, axis, [(i, i ^ o) for i in range(total)])  11.4 us
    pallas_call x6, Pallas kernels, call(): pl.pallas_call(kernel, out_shape=out_shape, in_specs=[smem] * len(scalars...  8.11 us
    all_to_all x1, waiting for transfers between devices, spread_out(): return lax.all_to_all(block, axis, split_axis=0, concat_axis=0, tiled=True)  7.47 us
    all_to_all x1, starting transfers between devices, spread_out(): return lax.all_to_all(block, axis, split_axis=0, concat_axis=0, tiled=True)  7.26 us
    pallas_call x3, Pallas kernels, run_experts(): pl.pallas_call(functools.partial(expert_kernel, len(got), owned), out_sha...  5.99 us
    unnamed x18, local copies, waits for them, and re-layouts  5.65 us
  transfers between devices with their start and end apart: 24, of which 9 were waited for; matrix products, arithmetic and copies ran while one was open for 0% of the time, Pallas kernels for 9%

profile of v3, /device:TPU:0, one launch (start us, length us, event | category | flops | bytes accessed | tf_op | source)
XLA Modules:
  0.0 96.0 jit_solution(9408347933641788054)
XLA Ops:
  0.7 2.8 %prep.1 = bf16[8,64,512]{2,1,0:T(8,128)(2,1)} custom-call(s32[1]{0:T(128)} %bitcast.1.at, bf16[512,256]{1,0:T(8,128)(2,1)} %refs_0_.1, f32[512,256]{1,0:T(8,128)} %refs_1_.1, f32[1,256]{1,0:T(1,128)} %bitcast.12), custom_call_target="tpu_custom_call" | custom-call | tf_op jit(solution)/shard_map/prep/pallas_call | solution.py:30
  3.4 7.3 %all-to-all-start = ((bf16[8,64,512]{2,1,0:T(8,128)(2,1)}), bf16[8,64,512]{2,1,0:T(8,128)(2,1)S(1)}, u32[]{:S(2)}, u32[]{:S(2)}) async-start(bf16[8,64,512]{2,1,0:T(8,128)(2,1)} %prep.1), calls=%async_computation | async-start | bytes 1048576 | tf_op jit(solution)/shard_map/all_to_all | solution.py:376
  12.1 1.6 %collective-permute-start.1 = (bf16[128,256]{1,0:T(8,128)(2,1)S(1)}, bf16[128,256]{1,0:T(8,128)(2,1)S(1)}, u32[]{:S(2)}, u32[]{:S(2)}) collective-permute-start(bf16[128,256]{1,0:T(8,128)(2,1)S(1)} %get-tuple-element.42), channel_id=1, source_target_pairs={{0,2},{1,3},{2,0},{3,1},{4,6},{5,7},{6,4},{7,5},{8,10},{9,11},{10,... | collective-permute-start | bytes 196616 | tf_op jit(solution)/shard_map/ppermute | solution.py:370
  14.4 2.2 %collective-permute-done.1.refs_2_ = bf16[128,256]{1,0:T(8,128)(2,1)S(1)} collective-permute-done((bf16[128,256]{1,0:T(8,128)(2,1)S(1)}, bf16[128,256]{1,0:T(8,128)(2,1)S(1)}, u32[]{:S(2)}, u32[]{:S(2)}) %collective-permute-start.1) | collective-permute-done | bytes 65568 | tf_op jit(solution)/shard_map/ppermute | solution.py:370
  17.7 7.5 %all-to-all-done.got = bf16[8,64,512]{2,1,0:T(8,128)(2,1)S(1)} async-done(((bf16[8,64,512]{2,1,0:T(8,128)(2,1)}), bf16[8,64,512]{2,1,0:T(8,128)(2,1)S(1)}, u32[]{:S(2)}, u32[]{:S(2)}) %all-to-all-start) | async-done | bytes 524320 | tf_op jit(solution)/shard_map/all_to_all | solution.py:376
  25.2 2.7 %conv.1 = bf16[8,4,32,128]{3,2,1,0:T(8,128)(2,1)S(1)} custom-call(bf16[8,64,512]{2,1,0:T(8,128)(2,1)S(1)} %all-to-all-done.got, f32[8,512]{1,0:T(8,128)S(1)} %get-tuple-element.45.turn_cos, f32[8,512]{1,0:T(8,128)S(1)} %get-tuple-element.46.turn_sin, bf16[512,512]{1,0:T(8,128)(2,1)S(1)} %get-tuple-element.47.cos, bf16[512,512]{1,0:T(8,128)(2,1)S(1)} %get-tuple-element.48.sin), custom_call_target="tpu_custom_call" | custom-call | tf_op jit(solution)/shard_map/conv/pallas_call | solution.py:30
  27.9 14.1 %all_to_all.10 = bf16[32,32,128]{2,1,0:T(8,128)(2,1)S(1)} all-to-all(bf16[32,32,128]{2,1,0:T(8,128)(2,1)S(1)} %bitcast.7), channel_id=1, replica_groups=mesh['ctx'=8,'ch'=4] {'ctx','ch'}, dimensions={0} | all-to-all | bytes 524288 | tf_op jit(solution)/shard_map/all_to_all | solution.py:376
  43.2 3.0 %collective-permute-start.7 = (bf16[64,1024]{1,0:T(8,128)(2,1)S(1)}, bf16[64,1024]{1,0:T(8,128)(2,1)S(1)}, u32[]{:S(2)}, u32[]{:S(2)}) collective-permute-start(bf16[64,1024]{1,0:T(8,128)(2,1)S(1)} %get-tuple-element.61), channel_id=1, source_target_pairs={{0,20},{4,16},{8,28},{12,24},{16,4},{20,0},{24,12},{28,8},{1,21},{... | collective-permute-start | bytes 393224 | tf_op jit(solution)/shard_map/ppermute | solution.py:370
  48.2 1.4 %collective-permute-start.10 = (bf16[64,1024]{1,0:T(8,128)(2,1)S(1)}, bf16[64,1024]{1,0:T(8,128)(2,1)S(1)}, u32[]{:S(2)}, u32[]{:S(2)}) collective-permute-start(bf16[64,1024]{1,0:T(8,128)(2,1)S(1)} %get-tuple-element.64), channel_id=1, source_target_pairs={{0,12},{4,8},{8,4},{12,0},{16,28},{20,24},{24,20},{28,16},{1,13},{... | collective-permute-start | bytes 393224 | tf_op jit(solution)/shard_map/ppermute | solution.py:370
  49.6 2.2 %copy-done = bf16[8,1024,256]{2,1,0:T(8,128)(2,1)S(1)} copy-done((bf16[8,1024,256]{2,1,0:T(8,128)(2,1)S(1)}, bf16[8,1024,256]{2,1,0:T(8,128)(2,1)}, u32[]{:S(2)}) %copy-start) | copy-done | bytes 4194328
  51.8 2.2 %copy-done.2 = bf16[8,256,1024]{2,1,0:T(8,128)(2,1)S(1)} copy-done((bf16[8,256,1024]{2,1,0:T(8,128)(2,1)S(1)}, bf16[8,256,1024]{2,1,0:T(8,128)(2,1)}, u32[]{:S(2)}) %copy-start.2) | copy-done | bytes 4194328
  54.0 1.6 %experts.3 = (bf16[64,1024]{1,0:T(8,128)(2,1)S(1)}, f32[8,128]{1,0:T(8,128)S(1)}) custom-call(bf16[8,1024,256]{2,1,0:T(8,128)(2,1)S(1)} %copy-done, bf16[8,256,1024]{2,1,0:T(8,128)(2,1)S(1)} %copy-done.2, bf16[64,1024]{1,0:T(8,128)(2,1)S(1)} %get-tuple-element.58.refs_0_), custom_call_target="tpu_custom_call" | custom-call | flops 1 | bytes 1 | tf_op jit(solution)/shard_map/experts/pallas_call | solution.py:281
  55.6 1.2 %collective-permute-start.16 = (bf16[64,1024]{1,0:T(8,128)(2,1)S(1)}, bf16[64,1024]{1,0:T(8,128)(2,1)S(1)}, u32[]{:S(2)}, u32[]{:S(2)}) collective-permute-start(bf16[64,1024]{1,0:T(8,128)(2,1)S(1)} %get-tuple-element.71), channel_id=1, source_target_pairs={{0,24},{4,28},{8,16},{12,20},{16,8},{20,12},{24,0},{28,4},{1,25},{... | collective-permute-start | bytes 393224 | tf_op jit(solution)/shard_map/ppermute | solution.py:370
  57.2 3.1 %collective-permute-start.17 = (bf16[64,1024]{1,0:T(8,128)(2,1)S(1)}, bf16[64,1024]{1,0:T(8,128)(2,1)S(1)}, u32[]{:S(2)}, u32[]{:S(2)}) collective-permute-start(bf16[64,1024]{1,0:T(8,128)(2,1)S(1)} %get-tuple-element.72), channel_id=1, source_target_pairs={{0,28},{4,24},{8,20},{12,16},{16,12},{20,8},{24,4},{28,0},{1,29},{... | collective-permute-start | bytes 393224 | tf_op jit(solution)/shard_map/ppermute | solution.py:370
  60.3 2.1 %experts.4 = (bf16[64,1024]{1,0:T(8,128)(2,1)S(1)}, bf16[64,1024]{1,0:T(8,128)(2,1)S(1)}, bf16[64,1024]{1,0:T(8,128)(2,1)S(1)}, bf16[64,1024]{1,0:T(8,128)(2,1)S...) custom-call(bf16[8,1024,256]{2,1,0:T(8,128)(2,1)S(1)} %copy-done.1, bf16[8,256,1024]{2,1,0:T(8,128)(2,1)S(1)} %copy-done.3, ...), custom_call_target="tpu_custom_call" | custom-call | flops 1 | bytes 1 | tf_op jit(solution)/shard_map/experts/pallas_call | solution.py:281
  62.3 7.0 %collective-permute-start.11 = (bf16[64,1024]{1,0:T(8,128)(2,1)S(1)}, bf16[64,1024]{1,0:T(8,128)(2,1)S(1)}, u32[]{:S(2)}, u32[]{:S(2)}) collective-permute-start(bf16[64,1024]{1,0:T(8,128)(2,1)S(1)} %get-tuple-element.66), channel_id=1, source_target_pairs={{0,4},{4,0},{8,12},{12,8},{16,20},{20,16},{24,28},{28,24},{1,5},{5... | collective-permute-start | bytes 393224 | tf_op jit(solution)/shard_map/ppermute | solution.py:370
  69.3 1.5 %collective-permute-start.13 = (bf16[64,1024]{1,0:T(8,128)(2,1)S(1)}, bf16[64,1024]{1,0:T(8,128)(2,1)S(1)}, u32[]{:S(2)}, u32[]{:S(2)}) collective-permute-start(bf16[64,1024]{1,0:T(8,128)(2,1)S(1)} %get-tuple-element.68), channel_id=1, source_target_pairs={{0,12},{4,8},{8,4},{12,0},{16,28},{20,24},{24,20},{28,16},{1,13},{... | collective-permute-start | bytes 393224 | tf_op jit(solution)/shard_map/ppermute | solution.py:370
  70.9 4.3 %collective-permute-start.15 = (bf16[64,1024]{1,0:T(8,128)(2,1)S(1)}, bf16[64,1024]{1,0:T(8,128)(2,1)S(1)}, u32[]{:S(2)}, u32[]{:S(2)}) collective-permute-start(bf16[64,1024]{1,0:T(8,128)(2,1)S(1)} %get-tuple-element.70), channel_id=1, source_target_pairs={{0,20},{4,16},{8,28},{12,24},{16,4},{20,0},{24,12},{28,8},{1,21},{... | collective-permute-start | bytes 393224 | tf_op jit(solution)/shard_map/ppermute | solution.py:370
  75.2 2.3 %experts.5 = (bf16[64,1024]{1,0:T(8,128)(2,1)S(1)}, bf16[64,1024]{1,0:T(8,128)(2,1)S(1)}, f32[8,128]{1,0:T(8,128)}) custom-call(bf16[8,1024,256]{2,1,0:T(8,128)(2,1)S(1)} %copy-done.1, bf16[8,256,1024]{2,1,0:T(8,128)(2,1)S(1)} %copy-done.3, bf16[64,1024]{1,0:T(8,128)(2,1)S(1)} %collective-permute-done.16.refs_0_, ...), custom_call_target="tpu_custom_call" | custom-call | flops 1 | bytes 1 | tf_op jit(solution)/shard_map/experts/pallas_call | solution.py:281
  77.5 3.3 %collective-permute-start.19 = (bf16[64,1024]{1,0:T(8,128)(2,1)S(1)}, bf16[64,1024]{1,0:T(8,128)(2,1)S(1)}, u32[]{:S(2)}, u32[]{:S(2)}) collective-permute-start(bf16[64,1024]{1,0:T(8,128)(2,1)S(1)} %get-tuple-element.75), channel_id=1, source_target_pairs={{0,28},{4,24},{8,20},{12,16},{16,12},{20,8},{24,4},{28,0},{1,29},{... | collective-permute-start | bytes 393224 | tf_op jit(solution)/shard_map/ppermute | solution.py:370
  81.9 4.7 %collective-permute-done.14.refs_4_ = bf16[64,1024]{1,0:T(8,128)(2,1)S(1)} collective-permute-done((bf16[64,1024]{1,0:T(8,128)(2,1)S(1)}, bf16[64,1024]{1,0:T(8,128)(2,1)S(1)}, u32[]{:S(2)}, u32[]{:S(2)}) %collective-permute-start.14) | collective-permute-done | bytes 131104 | tf_op jit(solution)/shard_map/ppermute | solution.py:370
  86.6 1.4 %collective-permute-start.4 = (bf16[128,256]{1,0:T(8,128)(2,1)S(1)}, bf16[128,256]{1,0:T(8,128)(2,1)S(1)}, u32[]{:S(2)}, u32[]{:S(2)}) collective-permute-start(bf16[128,256]{1,0:T(8,128)(2,1)S(1)} %get-tuple-element.55), channel_id=1, source_target_pairs={{0,2},{1,3},{2,0},{3,1},{4,6},{5,7},{6,4},{7,5},{8,10},{9,11},{10,... | collective-permute-start | bytes 196616 | tf_op jit(solution)/shard_map/ppermute | solution.py:370
  88.7 1.5 %collective-permute-start.20 = (bf16[128,256]{1,0:T(8,128)(2,1)S(1)}, bf16[128,256]{1,0:T(8,128)(2,1)S(1)}, u32[]{:S(2)}, u32[]{:S(2)}) collective-permute-start(bf16[128,256]{1,0:T(8,128)(2,1)S(1)} %get-tuple-element.77), channel_id=1, source_target_pairs={{0,1},{1,0},{2,3},{3,2},{4,5},{5,4},{6,7},{7,6},{8,9},{9,8},{10,11... | collective-permute-start | bytes 196616 | tf_op jit(solution)/shard_map/ppermute | solution.py:370
  93.0 2.0 %collective-permute-done.21.refs_2_ = bf16[128,256]{1,0:T(8,128)(2,1)S(1)} collective-permute-done((bf16[128,256]{1,0:T(8,128)(2,1)S(1)}, bf16[128,256]{1,0:T(8,128)(2,1)S(1)}, u32[]{:S(2)}, u32[]{:S(2)}) %collective-permute-start.21) | collective-permute-done | bytes 65568 | tf_op jit(solution)/shard_map/ppermute | solution.py:370
  (55 shorter events, 12.4 us)
Async XLA Ops:
  3.4 21.8 %all-to-all-start = ((bf16[8,64,512]{2,1,0:T(8,128)(2,1)}), bf16[8,64,512]{2,1,0:T(8,128)(2,1)S(1)}, u32[]{:S(2)}, u32[]{:S(2)}) async-start(bf16[8,64,512]{2,1,0:T(8,128)(2,1)} %prep.1), calls=%async_computation | async-start | bytes 1048576 | tf_op jit(solution)/shard_map/all_to_all | solution.py:376
  12.0 2.4 %collective-permute-start = (bf16[128,256]{1,0:T(8,128)(2,1)S(1)}, bf16[128,256]{1,0:T(8,128)(2,1)S(1)}, u32[]{:S(2)}, u32[]{:S(2)}) collective-permute-start(bf16[128,256]{1,0:T(8,128)(2,1)S(1)} %get-tuple-element.41), channel_id=1, source_target_pairs={{0,1},{1,0},{2,3},{3,2},{4,5},{5,4},{6,7},{7,6},{8,9},{9,8},{10,11... | collective-permute-start | bytes 196616 | tf_op jit(solution)/shard_map/ppermute | solution.py:370
  12.1 4.5 %collective-permute-start.1 = (bf16[128,256]{1,0:T(8,128)(2,1)S(1)}, bf16[128,256]{1,0:T(8,128)(2,1)S(1)}, u32[]{:S(2)}, u32[]{:S(2)}) collective-permute-start(bf16[128,256]{1,0:T(8,128)(2,1)S(1)} %get-tuple-element.42), channel_id=1, source_target_pairs={{0,2},{1,3},{2,0},{3,1},{4,6},{5,7},{6,4},{7,5},{8,10},{9,11},{10,... | collective-permute-start | bytes 196616 | tf_op jit(solution)/shard_map/ppermute | solution.py:370
  13.7 4.0 %collective-permute-start.2 = (bf16[128,256]{1,0:T(8,128)(2,1)S(1)}, bf16[128,256]{1,0:T(8,128)(2,1)S(1)}, u32[]{:S(2)}, u32[]{:S(2)}) collective-permute-start(bf16[128,256]{1,0:T(8,128)(2,1)S(1)} %get-tuple-element.43), channel_id=1, source_target_pairs={{0,3},{1,2},{2,1},{3,0},{4,7},{5,6},{6,5},{7,4},{8,11},{9,10},{10,... | collective-permute-start | bytes 196616 | tf_op jit(solution)/shard_map/ppermute | solution.py:370
  42.8 12.8 %collective-permute-start.6 = (bf16[64,1024]{1,0:T(8,128)(2,1)S(1)}, bf16[64,1024]{1,0:T(8,128)(2,1)S(1)}, u32[]{:S(2)}, u32[]{:S(2)}) collective-permute-start(bf16[64,1024]{1,0:T(8,128)(2,1)S(1)} %get-tuple-element.60), channel_id=1, source_target_pairs={{0,16},{4,20},{8,24},{12,28},{16,0},{20,4},{24,8},{28,12},{1,17},{... | collective-permute-start | bytes 393224 | tf_op jit(solution)/shard_map/ppermute | solution.py:370
  43.2 14.0 %collective-permute-start.7 = (bf16[64,1024]{1,0:T(8,128)(2,1)S(1)}, bf16[64,1024]{1,0:T(8,128)(2,1)S(1)}, u32[]{:S(2)}, u32[]{:S(2)}) collective-permute-start(bf16[64,1024]{1,0:T(8,128)(2,1)S(1)} %get-tuple-element.61), channel_id=1, source_target_pairs={{0,20},{4,16},{8,28},{12,24},{16,4},{20,0},{24,12},{28,8},{1,21},{... | collective-permute-start | bytes 393224 | tf_op jit(solution)/shard_map/ppermute | solution.py:370
  46.2 14.1 %collective-permute-start.8 = (bf16[64,1024]{1,0:T(8,128)(2,1)S(1)}, bf16[64,1024]{1,0:T(8,128)(2,1)S(1)}, u32[]{:S(2)}, u32[]{:S(2)}) collective-permute-start(bf16[64,1024]{1,0:T(8,128)(2,1)S(1)} %get-tuple-element.62), channel_id=1, source_target_pairs={{0,4},{4,0},{8,12},{12,8},{16,20},{20,16},{24,28},{28,24},{1,5},{5... | collective-permute-start | bytes 393224 | tf_op jit(solution)/shard_map/ppermute | solution.py:370
  47.3 13.0 %collective-permute-start.9 = (bf16[64,1024]{1,0:T(8,128)(2,1)S(1)}, bf16[64,1024]{1,0:T(8,128)(2,1)S(1)}, u32[]{:S(2)}, u32[]{:S(2)}) collective-permute-start(bf16[64,1024]{1,0:T(8,128)(2,1)S(1)} %get-tuple-element.63), channel_id=1, source_target_pairs={{0,8},{4,12},{8,0},{12,4},{16,24},{20,28},{24,16},{28,20},{1,9},{5... | collective-permute-start | bytes 393224 | tf_op jit(solution)/shard_map/ppermute | solution.py:370
  48.2 12.1 %collective-permute-start.10 = (bf16[64,1024]{1,0:T(8,128)(2,1)S(1)}, bf16[64,1024]{1,0:T(8,128)(2,1)S(1)}, u32[]{:S(2)}, u32[]{:S(2)}) collective-permute-start(bf16[64,1024]{1,0:T(8,128)(2,1)S(1)} %get-tuple-element.64), channel_id=1, source_target_pairs={{0,12},{4,8},{8,4},{12,0},{16,28},{20,24},{24,20},{28,16},{1,13},{... | collective-permute-start | bytes 393224 | tf_op jit(solution)/shard_map/ppermute | solution.py:370
  55.6 15.2 %collective-permute-start.16 = (bf16[64,1024]{1,0:T(8,128)(2,1)S(1)}, bf16[64,1024]{1,0:T(8,128)(2,1)S(1)}, u32[]{:S(2)}, u32[]{:S(2)}) collective-permute-start(bf16[64,1024]{1,0:T(8,128)(2,1)S(1)} %get-tuple-element.71), channel_id=1, source_target_pairs={{0,24},{4,28},{8,16},{12,20},{16,8},{20,12},{24,0},{28,4},{1,25},{... | collective-permute-start | bytes 393224 | tf_op jit(solution)/shard_map/ppermute | solution.py:370
  57.2 13.7 %collective-permute-start.17 = (bf16[64,1024]{1,0:T(8,128)(2,1)S(1)}, bf16[64,1024]{1,0:T(8,128)(2,1)S(1)}, u32[]{:S(2)}, u32[]{:S(2)}) collective-permute-start(bf16[64,1024]{1,0:T(8,128)(2,1)S(1)} %get-tuple-element.72), channel_id=1, source_target_pairs={{0,28},{4,24},{8,20},{12,16},{16,12},{20,8},{24,4},{28,0},{1,29},{... | collective-permute-start | bytes 393224 | tf_op jit(solution)/shard_map/ppermute | solution.py:370
  62.3 15.2 %collective-permute-start.11 = (bf16[64,1024]{1,0:T(8,128)(2,1)S(1)}, bf16[64,1024]{1,0:T(8,128)(2,1)S(1)}, u32[]{:S(2)}, u32[]{:S(2)}) collective-permute-start(bf16[64,1024]{1,0:T(8,128)(2,1)S(1)} %get-tuple-element.66), channel_id=1, source_target_pairs={{0,4},{4,0},{8,12},{12,8},{16,20},{20,16},{24,28},{28,24},{1,5},{5... | collective-permute-start | bytes 393224 | tf_op jit(solution)/shard_map/ppermute | solution.py:370
  69.3 8.2 %collective-permute-start.12 = (bf16[64,1024]{1,0:T(8,128)(2,1)S(1)}, bf16[64,1024]{1,0:T(8,128)(2,1)S(1)}, u32[]{:S(2)}, u32[]{:S(2)}) collective-permute-start(bf16[64,1024]{1,0:T(8,128)(2,1)S(1)} %get-tuple-element.67), channel_id=1, source_target_pairs={{0,8},{4,12},{8,0},{12,4},{16,24},{20,28},{24,16},{28,20},{1,9},{5... | collective-permute-start | bytes 393224 | tf_op jit(solution)/shard_map/ppermute | solution.py:370
  69.3 11.6 %collective-permute-start.13 = (bf16[64,1024]{1,0:T(8,128)(2,1)S(1)}, bf16[64,1024]{1,0:T(8,128)(2,1)S(1)}, u32[]{:S(2)}, u32[]{:S(2)}) collective-permute-start(bf16[64,1024]{1,0:T(8,128)(2,1)S(1)} %get-tuple-element.68), channel_id=1, source_target_pairs={{0,12},{4,8},{8,4},{12,0},{16,28},{20,24},{24,20},{28,16},{1,13},{... | collective-permute-start | bytes 393224 | tf_op jit(solution)/shard_map/ppermute | solution.py:370
  70.9 15.7 %collective-permute-start.14 = (bf16[64,1024]{1,0:T(8,128)(2,1)S(1)}, bf16[64,1024]{1,0:T(8,128)(2,1)S(1)}, u32[]{:S(2)}, u32[]{:S(2)}) collective-permute-start(bf16[64,1024]{1,0:T(8,128)(2,1)S(1)} %get-tuple-element.69), channel_id=1, source_target_pairs={{0,16},{4,20},{8,24},{12,28},{16,0},{20,4},{24,8},{28,12},{1,17},{... | collective-permute-start | bytes 393224 | tf_op jit(solution)/shard_map/ppermute | solution.py:370
  70.9 17.2 %collective-permute-start.15 = (bf16[64,1024]{1,0:T(8,128)(2,1)S(1)}, bf16[64,1024]{1,0:T(8,128)(2,1)S(1)}, u32[]{:S(2)}, u32[]{:S(2)}) collective-permute-start(bf16[64,1024]{1,0:T(8,128)(2,1)S(1)} %get-tuple-element.70), channel_id=1, source_target_pairs={{0,20},{4,16},{8,28},{12,24},{16,4},{20,0},{24,12},{28,8},{1,21},{... | collective-permute-start | bytes 393224 | tf_op jit(solution)/shard_map/ppermute | solution.py:370
  77.5 10.5 %collective-permute-start.18 = (bf16[64,1024]{1,0:T(8,128)(2,1)S(1)}, bf16[64,1024]{1,0:T(8,128)(2,1)S(1)}, u32[]{:S(2)}, u32[]{:S(2)}) collective-permute-start(bf16[64,1024]{1,0:T(8,128)(2,1)S(1)} %get-tuple-element.74), channel_id=1, source_target_pairs={{0,24},{4,28},{8,16},{12,20},{16,8},{20,12},{24,0},{28,4},{1,25},{... | collective-permute-start | bytes 393224 | tf_op jit(solution)/shard_map/ppermute | solution.py:370
  77.5 10.5 %collective-permute-start.19 = (bf16[64,1024]{1,0:T(8,128)(2,1)S(1)}, bf16[64,1024]{1,0:T(8,128)(2,1)S(1)}, u32[]{:S(2)}, u32[]{:S(2)}) collective-permute-start(bf16[64,1024]{1,0:T(8,128)(2,1)S(1)} %get-tuple-element.75), channel_id=1, source_target_pairs={{0,28},{4,24},{8,20},{12,16},{16,12},{20,8},{24,4},{28,0},{1,29},{... | collective-permute-start | bytes 393224 | tf_op jit(solution)/shard_map/ppermute | solution.py:370
  80.9 10.0 %collective-permute-start.3 = (bf16[128,256]{1,0:T(8,128)(2,1)S(1)}, bf16[128,256]{1,0:T(8,128)(2,1)S(1)}, u32[]{:S(2)}, u32[]{:S(2)}) collective-permute-start(bf16[128,256]{1,0:T(8,128)(2,1)S(1)} %get-tuple-element.54), channel_id=1, source_target_pairs={{0,1},{1,0},{2,3},{3,2},{4,5},{5,4},{6,7},{7,6},{8,9},{9,8},{10,11... | collective-permute-start | bytes 196616 | tf_op jit(solution)/shard_map/ppermute | solution.py:370
  86.6 5.0 %collective-permute-start.4 = (bf16[128,256]{1,0:T(8,128)(2,1)S(1)}, bf16[128,256]{1,0:T(8,128)(2,1)S(1)}, u32[]{:S(2)}, u32[]{:S(2)}) collective-permute-start(bf16[128,256]{1,0:T(8,128)(2,1)S(1)} %get-tuple-element.55), channel_id=1, source_target_pairs={{0,2},{1,3},{2,0},{3,1},{4,6},{5,7},{6,4},{7,5},{8,10},{9,11},{10,... | collective-permute-start | bytes 196616 | tf_op jit(solution)/shard_map/ppermute | solution.py:370
  88.0 4.2 %collective-permute-start.5 = (bf16[128,256]{1,0:T(8,128)(2,1)S(1)}, bf16[128,256]{1,0:T(8,128)(2,1)S(1)}, u32[]{:S(2)}, u32[]{:S(2)}) collective-permute-start(bf16[128,256]{1,0:T(8,128)(2,1)S(1)} %get-tuple-element.56), channel_id=1, source_target_pairs={{0,3},{1,2},{2,1},{3,0},{4,7},{5,6},{6,5},{7,4},{8,11},{9,10},{10,... | collective-permute-start | bytes 196616 | tf_op jit(solution)/shard_map/ppermute | solution.py:370
  88.7 4.3 %collective-permute-start.20 = (bf16[128,256]{1,0:T(8,128)(2,1)S(1)}, bf16[128,256]{1,0:T(8,128)(2,1)S(1)}, u32[]{:S(2)}, u32[]{:S(2)}) collective-permute-start(bf16[128,256]{1,0:T(8,128)(2,1)S(1)} %get-tuple-element.77), channel_id=1, source_target_pairs={{0,1},{1,0},{2,3},{3,2},{4,5},{5,4},{6,7},{7,6},{8,9},{9,8},{10,11... | collective-permute-start | bytes 196616 | tf_op jit(solution)/shard_map/ppermute | solution.py:370
  90.2 4.8 %collective-permute-start.21 = (bf16[128,256]{1,0:T(8,128)(2,1)S(1)}, bf16[128,256]{1,0:T(8,128)(2,1)S(1)}, u32[]{:S(2)}, u32[]{:S(2)}) collective-permute-start(bf16[128,256]{1,0:T(8,128)(2,1)S(1)} %get-tuple-element.78), channel_id=1, source_target_pairs={{0,2},{1,3},{2,0},{3,1},{4,6},{5,7},{6,4},{7,5},{8,10},{9,11},{10,... | collective-permute-start | bytes 196616 | tf_op jit(solution)/shard_map/ppermute | solution.py:370
  90.9 4.4 %collective-permute-start.22 = (bf16[128,256]{1,0:T(8,128)(2,1)S(1)}, bf16[128,256]{1,0:T(8,128)(2,1)S(1)}, u32[]{:S(2)}, u32[]{:S(2)}) collective-permute-start(bf16[128,256]{1,0:T(8,128)(2,1)S(1)} %get-tuple-element.79), channel_id=1, source_target_pairs={{0,3},{1,2},{2,1},{3,0},{4,7},{5,6},{6,5},{7,4},{8,11},{9,10},{10,... | collective-permute-start | bytes 196616 | tf_op jit(solution)/shard_map/ppermute | solution.py:370
  (8 other events, 106.4 us)

commit v4 on v3

--- a/solution.py
+++ b/solution.py
@@ -9,6 +9,7 @@
 from jax.sharding import PartitionSpec as P
 
 CAP = 16
+LANES = 128
 VMEM_LIMIT = 16 * 1024 * 1024
 FULL_LIMIT = 62 * 1024 * 1024
 
@@ -20,30 +21,18 @@
     return pltpu.CompilerParams(vmem_limit_bytes=limit)
 
 
-def call(kernel, out_shape, scalars, far, operands, name, scratch=(), limit=VMEM_LIMIT, cost=None):
+def call(kernel, out_shape, scalars, operands, name, scratch=()):
     vmem = pl.BlockSpec(memory_space=pltpu.VMEM)
     smem = pl.BlockSpec(memory_space=pltpu.SMEM)
-    hbm = pl.BlockSpec(memory_space=pltpu.HBM)
-    if far:
-        held = [pltpu.VMEM(x.shape, x.dtype) for x in far]
-        scratch = [*scratch, *held, pltpu.SemaphoreType.DMA((len(far),))]
     return pl.pallas_call(
         kernel,
         out_shape=out_shape,
-        in_specs=[smem] * len(scalars) + [hbm] * len(far) + [vmem] * len(operands),
+        in_specs=[smem] * len(scalars) + [vmem] * len(operands),
         out_specs=jax.tree.map(lambda _: vmem, out_shape),
         scratch_shapes=scratch,
-        compiler_params=params(limit),
-        cost_estimate=cost,
+        compiler_params=params(),
         name=name,
-    )(*scalars, *far, *operands)
-
-
-def fetch(far, held, sems):
-    copies = [pltpu.make_async_copy(a, b, sems.at[i]) for i, (a, b) in enumerate(zip(far, held))]
-    for copy in copies:
-        copy.start()
-    return copies
+    )(*scalars, *operands)
 
 
 def cmul(a, w):
@@ -97,21 +86,43 @@
     sin[...] = wide_sin[...].astype(bf16)
 
 
-def prep_kernel(groups, at, *refs):
-    far, refs = refs[:2], refs[2:]
-    skip, spread, sig, taps, sems = refs
-    copies = fetch(far, (sig, taps), sems)
+def prep_kernel(groups, at, far_sig, far_taps, far_skip, spread, sig, taps, skip, stage, arrive, leave):
     tok, chans = sig.shape
     per = chans // groups
-    copies[0].wait()
-    sig_t = sig[...].astype(f32).T.astype(bf16)
-    for g in range(groups):
-        spread[g, :per, :] = sig_t[g * per : (g + 1) * per, :]
-    copies[1].wait()
-    taps[0:1, :] = taps[0:1, :] + jnp.where(at[0] == 0, skip[...], 0.0)
-    tap_t = taps[...].T.astype(bf16)
-    for g in range(groups):
-        spread[g, per:, :] = tap_t[g * per : (g + 1) * per, :]
+    wide = LANES if chans % LANES == 0 and LANES % per == 0 else chans
+    count = chans // wide
+    some = groups // count
+    coming = []
+    early = pltpu.make_async_copy(far_skip, skip, arrive.at[2 * count])
+    early.start()
+    for i in range(count):
+        lanes = pl.ds(i * wide, wide)
+        for k, (far, held) in enumerate(((far_sig, sig), (far_taps, taps))):
+            copy = pltpu.make_async_copy(
+                far.at[:, lanes], held.at[:, lanes], arrive.at[2 * i + k]
+            )
+            copy.start()
+            coming.append(copy)
+    going = []
+    for i in range(count):
+        lanes = slice(i * wide, (i + 1) * wide)
+        coming[2 * i].wait()
+        sig_t = sig[:, lanes].astype(f32).T.astype(bf16)
+        for g in range(some):
+            stage[i * some + g, :per, :] = sig_t[g * per : (g + 1) * per, :]
+        coming[2 * i + 1].wait()
+        if i == 0:
+            early.wait()
+        taps[0:1, lanes] = taps[0:1, lanes] + jnp.where(at[0] == 0, skip[:, lanes], 0.0)
+        tap_t = taps[:, lanes].T.astype(bf16)
+        for g in range(some):
+            stage[i * some + g, per:, :] = tap_t[g * per : (g + 1) * per, :]
+        bundle = pl.ds(i * some, some)
+        copy = pltpu.make_async_copy(stage.at[bundle], spread.at[bundle], leave.at[i])
+        copy.start()
+        going.append(copy)
+    for copy in going:
+        copy.wait()
 
 
 def split_kernel(me, whole, *refs):
@@ -246,7 +257,7 @@
 
 
 def expert_kernel(count, owned, up, down, *refs):
-    got, out, token, x = refs[:count], refs[-2 - count : -2], refs[-2], refs[-1]
+    got, out, x = refs[:count], refs[-1 - count : -1], refs[-1]
     group = up.shape[0] // owned
     width = up.shape[1]
     for e in range(owned):
@@ -271,25 +282,22 @@
                 piece[e * CAP : (e + 1) * CAP, :] = part
             else:
                 piece[:, e * CAP : (e + 1) * CAP, :] = part.reshape(piece.shape[0], CAP, width)
-    token[...] = jnp.zeros(token.shape, f32)
 
 
 def run_experts(got, w_up, w_down, owned, after):
     width = got[0].shape[-1]
     slots = sum(math.prod(x.shape[:-1]) for x in got) // owned
     vmem = pl.BlockSpec(memory_space=pltpu.VMEM)
-    *result, token = pl.pallas_call(
+    return pl.pallas_call(
         functools.partial(expert_kernel, len(got), owned),
-        out_shape=[jax.ShapeDtypeStruct(x.shape, x.dtype) for x in got]
-        + [jax.ShapeDtypeStruct((8, 128), f32)],
+        out_shape=[jax.ShapeDtypeStruct(x.shape, x.dtype) for x in got],
         in_specs=[vmem] * (2 + len(got) + len(after)),
-        out_specs=[vmem] * (len(got) + 1),
+        out_specs=[vmem] * len(got),
         scratch_shapes=[pltpu.VMEM((slots, width), bf16)],
         compiler_params=params(),
         cost_estimate=pl.CostEstimate(flops=1, bytes_accessed=1, transcendentals=0),
         name="experts",
     )(w_up, w_down, *got, *after)
-    return result, [token]
 
 
 def combine_kernel(experts, blocks, shards, me, at, routes_t, gates, *refs):
@@ -390,20 +398,28 @@
     shape = jax.ShapeDtypeStruct
     around = list(range(blocks))
 
-    spread = call(
+    hbm = pl.BlockSpec(memory_space=pltpu.HBM)
+    steps = max(1, chans // LANES)
+    spread = pl.pallas_call(
         functools.partial(prep_kernel, shards),
-        shape((shards, 2 * per, tok), bf16),
-        [at],
-        [signal, taps],
-        [skip.reshape(1, chans)],
-        "prep",
-        limit=FULL_LIMIT,
-    )
+        out_shape=shape((shards, 2 * per, tok), bf16),
+        in_specs=[pl.BlockSpec(memory_space=pltpu.SMEM), hbm, hbm, hbm],
+        out_specs=hbm,
+        scratch_shapes=[
+            pltpu.VMEM(signal.shape, signal.dtype),
+            pltpu.VMEM(taps.shape, taps.dtype),
+            pltpu.VMEM((1, chans), skip.dtype),
+            pltpu.VMEM((shards, 2 * per, tok), bf16),
+            pltpu.SemaphoreType.DMA((2 * steps + 1,)),
+            pltpu.SemaphoreType.DMA((steps,)),
+        ],
+        compiler_params=params(FULL_LIMIT),
+        name="prep",
+    )(at, signal, taps, skip.reshape(1, chans))
     pieces = split(gate_v, me, blocks)
     turns = call(
         tables_kernel,
         [shape((shards, tok), f32)] * 2 + [shape((tok, tok), bf16)] * 2,
-        [],
         [],
         [],
         "tables",
@@ -416,7 +432,6 @@
     conv = call(
         functools.partial(conv_kernel, blocks),
         shape((shards, blocks, per, rows), bf16),
-        [],
         [],
         [got, *turns],
         "conv",
@@ -433,36 +448,34 @@
         functools.partial(rows_kernel, experts, blocks),
         [shape((rows, chans), bf16)] * blocks + send_shape + [shape((rows, width), bf16)],
         [me, at],
-        [],
         [routes_t, norm_gain.reshape(1, width), conv, *pieces],
         "rows",
         [pltpu.VMEM((blocks, rows, chans), bf16), pltpu.VMEM((shards, size, width), bf16)],
     )
     mixed, send, normed = mixed_and_send[:blocks], mixed_and_send[blocks:-1], mixed_and_send[-1]
-    gates = call(gates_kernel, shape((rows, 2), f32), [], [], [normed, router, routes], "gates")
+    gates = call(gates_kernel, shape((rows, 2), f32), [], [normed, router, routes], "gates")
     if direct:
-        (own,), done = run_experts(send[:1], w_up, w_down, owned, [])
-        home = {0: own}
+        done = run_experts(send[:1], w_up, w_down, owned, [])
+        home = {0: done[0]}
         half = shards // 2
         cut = half + half // 2
-        groups = [[*range(half, cut), *range(1, half)], list(range(cut, shards))]
+        groups = [[*range(half, cut), *reversed(range(1, half))], list(range(cut, shards))]
         there = [swap([send[o] for o in group], "ctx", group, shards) for group in groups]
         for i, group in enumerate(groups):
-            result, done = run_experts(there[i], w_up, w_down, owned, done)
-            home.update(zip(group, swap(result, "ctx", group, shards)))
+            done = run_experts(there[i], w_up, w_down, owned, done[:1])
+            home.update(zip(group, swap(done, "ctx", group, shards)))
         back = [home[o] for o in range(shards)]
         mixed = swap(mixed, "ch", around, blocks)
     else:
         there = spread_out(send[0], "ctx")
         mixed = swap(mixed, "ch", around, blocks)
-        (result,), _ = run_experts([there], w_up, w_down, owned, [])
+        (result,) = run_experts([there], w_up, w_down, owned, [])
         back = [spread_out(result, "ctx")]
     mixed = place(mixed, me)
     moe = call(
         functools.partial(combine_kernel, experts, blocks, shards),
         [shape((rows, chans), bf16)] * blocks,
         [me, at],
-        [],
         [routes_t, gates, *back],
         "combine",
         [pltpu.VMEM((shards, size, width), bf16)],

time: 96.4 us -> 95.5 us (level)
  starting transfers between devices: 40.8 us -> 37.6 us
  waiting for transfers between devices: 18.9 us -> 21.8 us
  Pallas kernels: 15.9 us -> 14.8 us
    ppermute x23, starting transfers between devices: 33.5 us -> 30.3 us  [swap(): lax.ppermute(piece, axis, [(i, i ^ o) for i in range(total)])]
    ppermute x23, waiting for transfers between devices: 11.4 us -> 14.3 us  [swap(): lax.ppermute(piece, axis, [(i, i ^ o) for i in range(total)])]
    pallas_call x6 -> x5, Pallas kernels: 8.11 us -> 5.35 us  [call(): pl.pallas_call(kernel, out_shape=out_shape, in_specs=[smem] * len(scalars...]
    pallas_call x0 -> x1, Pallas kernels: none -> 2.13 us  [body(): pl.pallas_call(functools.partial(prep_kernel, shards), out_shape=shape((s...]
where the time goes in v4:
time: 95.5 us; the launch traced here: 94.7 us
  starting transfers between devices  37.6 us (39%)
  waiting for transfers between devices  21.8 us (23%)
  Pallas kernels  14.8 us (15%)
  blocking collectives  14.1 us (15%)
  local copies, waits for them, and re-layouts  5.65 us (6%)
    ppermute x23, starting transfers between devices, swap(): lax.ppermute(piece, axis, [(i, i ^ o) for i in range(total)])  30.3 us
    ppermute x23, waiting for transfers between devices, swap(): lax.ppermute(piece, axis, [(i, i ^ o) for i in range(total)])  14.3 us
    all_to_all x1, blocking collectives, spread_out(): return lax.all_to_all(block, axis, split_axis=0, concat_axis=0, tiled=True)  14.1 us
    all_to_all x1, waiting for transfers between devices, spread_out(): return lax.all_to_all(block, axis, split_axis=0, concat_axis=0, tiled=True)  7.47 us
    all_to_all x1, starting transfers between devices, spread_out(): return lax.all_to_all(block, axis, split_axis=0, concat_axis=0, tiled=True)  7.26 us
    unnamed x18, local copies, waits for them, and re-layouts  5.65 us
    pallas_call x3, Pallas kernels, run_experts(): pl.pallas_call(functools.partial(expert_kernel, len(got), owned), out_sha...  5.51 us
    pallas_call x5, Pallas kernels, call(): pl.pallas_call(kernel, out_shape=out_shape, in_specs=[smem] * len(scalars...  5.35 us
  transfers between devices with their start and end apart: 24, of which 9 were waited for; matrix products, arithmetic and copies ran while one was open for 0% of the time, Pallas kernels for 9%

profile of v4, /device:TPU:0, one launch (start us, length us, event | category | flops | bytes accessed | tf_op | source)
XLA Modules:
  0.0 94.7 jit_solution(10682973078061411697)
XLA Ops:
  0.7 2.1 %prep.1 = bf16[8,64,512]{2,1,0:T(8,128)(2,1)} custom-call(s32[1]{0:T(128)} %bitcast.1.at, bf16[512,256]{1,0:T(8,128)(2,1)} %far_sig.1, f32[512,256]{1,0:T(8,128)} %far_taps.1, f32[1,256]{1,0:T(1,128)} %bitcast.12), custom_call_target="tpu_custom_call" | custom-call | tf_op jit(solution)/shard_map/prep/pallas_call | solution.py:403
  2.8 7.3 %all-to-all-start = ((bf16[8,64,512]{2,1,0:T(8,128)(2,1)}), bf16[8,64,512]{2,1,0:T(8,128)(2,1)S(1)}, u32[]{:S(2)}, u32[]{:S(2)}) async-start(bf16[8,64,512]{2,1,0:T(8,128)(2,1)} %prep.1), calls=%async_computation | async-start | bytes 1048576 | tf_op jit(solution)/shard_map/all_to_all | solution.py:384
  11.4 1.6 %collective-permute-start.1 = (bf16[128,256]{1,0:T(8,128)(2,1)S(1)}, bf16[128,256]{1,0:T(8,128)(2,1)S(1)}, u32[]{:S(2)}, u32[]{:S(2)}) collective-permute-start(bf16[128,256]{1,0:T(8,128)(2,1)S(1)} %get-tuple-element.39), channel_id=1, source_target_pairs={{0,2},{1,3},{2,0},{3,1},{4,6},{5,7},{6,4},{7,5},{8,10},{9,11},{10,... | collective-permute-start | bytes 196616 | tf_op jit(solution)/shard_map/ppermute | solution.py:378
  13.8 2.2 %collective-permute-done.1.refs_2_ = bf16[128,256]{1,0:T(8,128)(2,1)S(1)} collective-permute-done((bf16[128,256]{1,0:T(8,128)(2,1)S(1)}, bf16[128,256]{1,0:T(8,128)(2,1)S(1)}, u32[]{:S(2)}, u32[]{:S(2)}) %collective-permute-start.1) | collective-permute-done | bytes 65568 | tf_op jit(solution)/shard_map/ppermute | solution.py:378
  17.1 7.5 %all-to-all-done.got = bf16[8,64,512]{2,1,0:T(8,128)(2,1)S(1)} async-done(((bf16[8,64,512]{2,1,0:T(8,128)(2,1)}), bf16[8,64,512]{2,1,0:T(8,128)(2,1)S(1)}, u32[]{:S(2)}, u32[]{:S(2)}) %all-to-all-start) | async-done | bytes 524320 | tf_op jit(solution)/shard_map/all_to_all | solution.py:384
  24.5 2.7 %conv.1 = bf16[8,4,32,128]{3,2,1,0:T(8,128)(2,1)S(1)} custom-call(bf16[8,64,512]{2,1,0:T(8,128)(2,1)S(1)} %all-to-all-done.got, f32[8,512]{1,0:T(8,128)S(1)} %get-tuple-element.42.turn_cos, f32[8,512]{1,0:T(8,128)S(1)} %get-tuple-element.43.turn_sin, bf16[512,512]{1,0:T(8,128)(2,1)S(1)} %get-tuple-element.44.cos, bf16[512,512]{1,0:T(8,128)(2,1)S(1)} %get-tuple-element.45.sin), custom_call_target="tpu_custom_call" | custom-call | tf_op jit(solution)/shard_map/conv/pallas_call | solution.py:27
  27.3 14.1 %all_to_all.10 = bf16[32,32,128]{2,1,0:T(8,128)(2,1)S(1)} all-to-all(bf16[32,32,128]{2,1,0:T(8,128)(2,1)S(1)} %bitcast.7), channel_id=1, replica_groups=mesh['ctx'=8,'ch'=4] {'ctx','ch'}, dimensions={0} | all-to-all | bytes 524288 | tf_op jit(solution)/shard_map/all_to_all | solution.py:384
  42.6 3.0 %collective-permute-start.7 = (bf16[64,1024]{1,0:T(8,128)(2,1)S(1)}, bf16[64,1024]{1,0:T(8,128)(2,1)S(1)}, u32[]{:S(2)}, u32[]{:S(2)}) collective-permute-start(bf16[64,1024]{1,0:T(8,128)(2,1)S(1)} %get-tuple-element.57), channel_id=1, source_target_pairs={{0,20},{4,16},{8,28},{12,24},{16,4},{20,0},{24,12},{28,8},{1,21},{... | collective-permute-start | bytes 393224 | tf_op jit(solution)/shard_map/ppermute | solution.py:378
  45.5 1.5 %collective-permute-start.8 = (bf16[64,1024]{1,0:T(8,128)(2,1)S(1)}, bf16[64,1024]{1,0:T(8,128)(2,1)S(1)}, u32[]{:S(2)}, u32[]{:S(2)}) collective-permute-start(bf16[64,1024]{1,0:T(8,128)(2,1)S(1)} %get-tuple-element.58), channel_id=1, source_target_pairs={{0,12},{4,8},{8,4},{12,0},{16,28},{20,24},{24,20},{28,16},{1,13},{... | collective-permute-start | bytes 393224 | tf_op jit(solution)/shard_map/ppermute | solution.py:378
  49.0 2.2 %copy-done = bf16[8,1024,256]{2,1,0:T(8,128)(2,1)S(1)} copy-done((bf16[8,1024,256]{2,1,0:T(8,128)(2,1)S(1)}, bf16[8,1024,256]{2,1,0:T(8,128)(2,1)}, u32[]{:S(2)}) %copy-start) | copy-done | bytes 4194328
  51.2 2.2 %copy-done.2 = bf16[8,256,1024]{2,1,0:T(8,128)(2,1)S(1)} copy-done((bf16[8,256,1024]{2,1,0:T(8,128)(2,1)S(1)}, bf16[8,256,1024]{2,1,0:T(8,128)(2,1)}, u32[]{:S(2)}) %copy-start.2) | copy-done | bytes 4194328
  53.4 1.6 %experts.3.refs_5_.refs_0_ = bf16[64,1024]{1,0:T(8,128)(2,1)S(1)} custom-call(bf16[8,1024,256]{2,1,0:T(8,128)(2,1)S(1)} %copy-done, bf16[8,256,1024]{2,1,0:T(8,128)(2,1)S(1)} %copy-done.2, bf16[64,1024]{1,0:T(8,128)(2,1)S(1)} %get-tuple-element.55.refs_0_), custom_call_target="tpu_custom_call" | custom-call | flops 1 | bytes 1 | tf_op jit(solution)/shard_map/experts/pallas_call | solution.py:291
  55.0 1.2 %collective-permute-start.16 = (bf16[64,1024]{1,0:T(8,128)(2,1)S(1)}, bf16[64,1024]{1,0:T(8,128)(2,1)S(1)}, u32[]{:S(2)}, u32[]{:S(2)}) collective-permute-start(bf16[64,1024]{1,0:T(8,128)(2,1)S(1)} %get-tuple-element.66), channel_id=1, source_target_pairs={{0,24},{4,28},{8,16},{12,20},{16,8},{20,12},{24,0},{28,4},{1,25},{... | collective-permute-start | bytes 393224 | tf_op jit(solution)/shard_map/ppermute | solution.py:378
  56.6 2.9 %collective-permute-start.17 = (bf16[64,1024]{1,0:T(8,128)(2,1)S(1)}, bf16[64,1024]{1,0:T(8,128)(2,1)S(1)}, u32[]{:S(2)}, u32[]{:S(2)}) collective-permute-start(bf16[64,1024]{1,0:T(8,128)(2,1)S(1)} %get-tuple-element.67), channel_id=1, source_target_pairs={{0,28},{4,24},{8,20},{12,16},{16,12},{20,8},{24,4},{28,0},{1,29},{... | collective-permute-start | bytes 393224 | tf_op jit(solution)/shard_map/ppermute | solution.py:378
  60.5 2.1 %experts.4 = (bf16[64,1024]{1,0:T(8,128)(2,1)S(1)}, bf16[64,1024]{1,0:T(8,128)(2,1)S(1)}, bf16[64,1024]{1,0:T(8,128)(2,1)S(1)}, bf16[64,1024]{1,0:T(8,128)(2,1)S(1)}, bf16[64,1024]{1,0:T(8,128)(2,1)S(1)}) custom-call(bf16[8,1024,256]{2,1,0:T(8,128)(2,1)S(1)} %copy-done.1, bf16[8,256,1024]{2,1,0:T(8,128)(2,1)S(1)} %copy-done.3, ...), custom_call_target="tpu_custom_call" | custom-call | flops 1 | bytes 1 | tf_op jit(solution)/shard_map/experts/pallas_call | solution.py:291
  62.7 3.4 %collective-permute-start.13 = (bf16[64,1024]{1,0:T(8,128)(2,1)S(1)}, bf16[64,1024]{1,0:T(8,128)(2,1)S(1)}, u32[]{:S(2)}, u32[]{:S(2)}) collective-permute-start(bf16[64,1024]{1,0:T(8,128)(2,1)S(1)} %get-tuple-element.63), channel_id=1, source_target_pairs={{0,12},{4,8},{8,4},{12,0},{16,28},{20,24},{24,20},{28,16},{1,13},{... | collective-permute-start | bytes 393224 | tf_op jit(solution)/shard_map/ppermute | solution.py:378
  67.0 3.2 %collective-permute-start.15 = (bf16[64,1024]{1,0:T(8,128)(2,1)S(1)}, bf16[64,1024]{1,0:T(8,128)(2,1)S(1)}, u32[]{:S(2)}, u32[]{:S(2)}) collective-permute-start(bf16[64,1024]{1,0:T(8,128)(2,1)S(1)} %get-tuple-element.65), channel_id=1, source_target_pairs={{0,20},{4,16},{8,28},{12,24},{16,4},{20,0},{24,12},{28,8},{1,21},{... | collective-permute-start | bytes 393224 | tf_op jit(solution)/shard_map/ppermute | solution.py:378
  70.1 1.9 %experts.5 = (bf16[64,1024]{1,0:T(8,128)(2,1)S(1)}, bf16[64,1024]{1,0:T(8,128)(2,1)S(1)}) custom-call(bf16[8,1024,256]{2,1,0:T(8,128)(2,1)S(1)} %copy-done.1, bf16[8,256,1024]{2,1,0:T(8,128)(2,1)S(1)} %copy-done.3, bf16[64,1024]{1,0:T(8,128)(2,1)S(1)} %collective-permute-done.16.refs_0_, bf16[64,1024]{1,0:T(8,128)(2,1)S(1)} %collective-permute-done.17.refs_1_, ...), custom_call_target="tpu_custom_call" | custom-call | flops 1 | bytes 1 | tf_op jit(solution)/shard_map/experts/pallas_call | solution.py:291
  72.0 2.8 %collective-permute-start.18 = (bf16[64,1024]{1,0:T(8,128)(2,1)S(1)}, bf16[64,1024]{1,0:T(8,128)(2,1)S(1)}, u32[]{:S(2)}, u32[]{:S(2)}) collective-permute-start(bf16[64,1024]{1,0:T(8,128)(2,1)S(1)} %get-tuple-element.68), channel_id=1, source_target_pairs={{0,24},{4,28},{8,16},{12,20},{16,8},{20,12},{24,0},{28,4},{1,25},{... | collective-permute-start | bytes 393224 | tf_op jit(solution)/shard_map/ppermute | solution.py:378
  74.8 2.6 %collective-permute-start.19 = (bf16[64,1024]{1,0:T(8,128)(2,1)S(1)}, bf16[64,1024]{1,0:T(8,128)(2,1)S(1)}, u32[]{:S(2)}, u32[]{:S(2)}) collective-permute-start(bf16[64,1024]{1,0:T(8,128)(2,1)S(1)} %get-tuple-element.69), channel_id=1, source_target_pairs={{0,28},{4,24},{8,20},{12,16},{16,12},{20,8},{24,4},{28,0},{1,29},{... | collective-permute-start | bytes 393224 | tf_op jit(solution)/shard_map/ppermute | solution.py:378
  78.4 5.7 %collective-permute-done.14.refs_4_ = bf16[64,1024]{1,0:T(8,128)(2,1)S(1)} collective-permute-done((bf16[64,1024]{1,0:T(8,128)(2,1)S(1)}, bf16[64,1024]{1,0:T(8,128)(2,1)S(1)}, u32[]{:S(2)}, u32[]{:S(2)}) %collective-permute-start.14) | collective-permute-done | bytes 131104 | tf_op jit(solution)/shard_map/ppermute | solution.py:378
  84.2 1.3 %collective-permute-start.4 = (bf16[128,256]{1,0:T(8,128)(2,1)S(1)}, bf16[128,256]{1,0:T(8,128)(2,1)S(1)}, u32[]{:S(2)}, u32[]{:S(2)}) collective-permute-start(bf16[128,256]{1,0:T(8,128)(2,1)S(1)} %get-tuple-element.52), channel_id=1, source_target_pairs={{0,2},{1,3},{2,0},{3,1},{4,6},{5,7},{6,4},{7,5},{8,10},{9,11},{10,... | collective-permute-start | bytes 196616 | tf_op jit(solution)/shard_map/ppermute | solution.py:378
  87.4 1.8 %collective-permute-start.20 = (bf16[128,256]{1,0:T(8,128)(2,1)S(1)}, bf16[128,256]{1,0:T(8,128)(2,1)S(1)}, u32[]{:S(2)}, u32[]{:S(2)}) collective-permute-start(bf16[128,256]{1,0:T(8,128)(2,1)S(1)} %get-tuple-element.71), channel_id=1, source_target_pairs={{0,1},{1,0},{2,3},{3,2},{4,5},{5,4},{6,7},{7,6},{8,9},{9,8},{10,11... | collective-permute-start | bytes 196616 | tf_op jit(solution)/shard_map/ppermute | solution.py:378
  91.7 2.3 %collective-permute-done.21.refs_2_ = bf16[128,256]{1,0:T(8,128)(2,1)S(1)} collective-permute-done((bf16[128,256]{1,0:T(8,128)(2,1)S(1)}, bf16[128,256]{1,0:T(8,128)(2,1)S(1)}, u32[]{:S(2)}, u32[]{:S(2)}) %collective-permute-start.21) | collective-permute-done | bytes 65568 | tf_op jit(solution)/shard_map/ppermute | solution.py:378
  (55 shorter events, 14.9 us)
Async XLA Ops:
  2.8 21.8 %all-to-all-start = ((bf16[8,64,512]{2,1,0:T(8,128)(2,1)}), bf16[8,64,512]{2,1,0:T(8,128)(2,1)S(1)}, u32[]{:S(2)}, u32[]{:S(2)}) async-start(bf16[8,64,512]{2,1,0:T(8,128)(2,1)} %prep.1), calls=%async_computation | async-start | bytes 1048576 | tf_op jit(solution)/shard_map/all_to_all | solution.py:384
  11.4 2.4 %collective-permute-start = (bf16[128,256]{1,0:T(8,128)(2,1)S(1)}, bf16[128,256]{1,0:T(8,128)(2,1)S(1)}, u32[]{:S(2)}, u32[]{:S(2)}) collective-permute-start(bf16[128,256]{1,0:T(8,128)(2,1)S(1)} %get-tuple-element.38), channel_id=1, source_target_pairs={{0,1},{1,0},{2,3},{3,2},{4,5},{5,4},{6,7},{7,6},{8,9},{9,8},{10,11... | collective-permute-start | bytes 196616 | tf_op jit(solution)/shard_map/ppermute | solution.py:378
  11.4 4.5 %collective-permute-start.1 = (bf16[128,256]{1,0:T(8,128)(2,1)S(1)}, bf16[128,256]{1,0:T(8,128)(2,1)S(1)}, u32[]{:S(2)}, u32[]{:S(2)}) collective-permute-start(bf16[128,256]{1,0:T(8,128)(2,1)S(1)} %get-tuple-element.39), channel_id=1, source_target_pairs={{0,2},{1,3},{2,0},{3,1},{4,6},{5,7},{6,4},{7,5},{8,10},{9,11},{10,... | collective-permute-start | bytes 196616 | tf_op jit(solution)/shard_map/ppermute | solution.py:378
  13.0 4.0 %collective-permute-start.2 = (bf16[128,256]{1,0:T(8,128)(2,1)S(1)}, bf16[128,256]{1,0:T(8,128)(2,1)S(1)}, u32[]{:S(2)}, u32[]{:S(2)}) collective-permute-start(bf16[128,256]{1,0:T(8,128)(2,1)S(1)} %get-tuple-element.40), channel_id=1, source_target_pairs={{0,3},{1,2},{2,1},{3,0},{4,7},{5,6},{6,5},{7,4},{8,11},{9,10},{10,... | collective-permute-start | bytes 196616 | tf_op jit(solution)/shard_map/ppermute | solution.py:378
  42.2 12.8 %collective-permute-start.6 = (bf16[64,1024]{1,0:T(8,128)(2,1)S(1)}, bf16[64,1024]{1,0:T(8,128)(2,1)S(1)}, u32[]{:S(2)}, u32[]{:S(2)}) collective-permute-start(bf16[64,1024]{1,0:T(8,128)(2,1)S(1)} %get-tuple-element.56), channel_id=1, source_target_pairs={{0,16},{4,20},{8,24},{12,28},{16,0},{20,4},{24,8},{28,12},{1,17},{... | collective-permute-start | bytes 393224 | tf_op jit(solution)/shard_map/ppermute | solution.py:378
  42.6 14.1 %collective-permute-start.7 = (bf16[64,1024]{1,0:T(8,128)(2,1)S(1)}, bf16[64,1024]{1,0:T(8,128)(2,1)S(1)}, u32[]{:S(2)}, u32[]{:S(2)}) collective-permute-start(bf16[64,1024]{1,0:T(8,128)(2,1)S(1)} %get-tuple-element.57), channel_id=1, source_target_pairs={{0,20},{4,16},{8,28},{12,24},{16,4},{20,0},{24,12},{28,8},{1,21},{... | collective-permute-start | bytes 393224 | tf_op jit(solution)/shard_map/ppermute | solution.py:378
  45.5 14.0 %collective-permute-start.8 = (bf16[64,1024]{1,0:T(8,128)(2,1)S(1)}, bf16[64,1024]{1,0:T(8,128)(2,1)S(1)}, u32[]{:S(2)}, u32[]{:S(2)}) collective-permute-start(bf16[64,1024]{1,0:T(8,128)(2,1)S(1)} %get-tuple-element.58), channel_id=1, source_target_pairs={{0,12},{4,8},{8,4},{12,0},{16,28},{20,24},{24,20},{28,16},{1,13},{... | collective-permute-start | bytes 393224 | tf_op jit(solution)/shard_map/ppermute | solution.py:378
  47.0 13.5 %collective-permute-start.9 = (bf16[64,1024]{1,0:T(8,128)(2,1)S(1)}, bf16[64,1024]{1,0:T(8,128)(2,1)S(1)}, u32[]{:S(2)}, u32[]{:S(2)}) collective-permute-start(bf16[64,1024]{1,0:T(8,128)(2,1)S(1)} %get-tuple-element.59), channel_id=1, source_target_pairs={{0,8},{4,12},{8,0},{12,4},{16,24},{20,28},{24,16},{28,20},{1,9},{5... | collective-permute-start | bytes 393224 | tf_op jit(solution)/shard_map/ppermute | solution.py:378
  48.1 12.4 %collective-permute-start.10 = (bf16[64,1024]{1,0:T(8,128)(2,1)S(1)}, bf16[64,1024]{1,0:T(8,128)(2,1)S(1)}, u32[]{:S(2)}, u32[]{:S(2)}) collective-permute-start(bf16[64,1024]{1,0:T(8,128)(2,1)S(1)} %get-tuple-element.60), channel_id=1, source_target_pairs={{0,4},{4,0},{8,12},{12,8},{16,20},{20,16},{24,28},{28,24},{1,5},{5... | collective-permute-start | bytes 393224 | tf_op jit(solution)/shard_map/ppermute | solution.py:378
  55.0 11.1 %collective-permute-start.16 = (bf16[64,1024]{1,0:T(8,128)(2,1)S(1)}, bf16[64,1024]{1,0:T(8,128)(2,1)S(1)}, u32[]{:S(2)}, u32[]{:S(2)}) collective-permute-start(bf16[64,1024]{1,0:T(8,128)(2,1)S(1)} %get-tuple-element.66), channel_id=1, source_target_pairs={{0,24},{4,28},{8,16},{12,20},{16,8},{20,12},{24,0},{28,4},{1,25},{... | collective-permute-start | bytes 393224 | tf_op jit(solution)/shard_map/ppermute | solution.py:378
  56.6 10.3 %collective-permute-start.17 = (bf16[64,1024]{1,0:T(8,128)(2,1)S(1)}, bf16[64,1024]{1,0:T(8,128)(2,1)S(1)}, u32[]{:S(2)}, u32[]{:S(2)}) collective-permute-start(bf16[64,1024]{1,0:T(8,128)(2,1)S(1)} %get-tuple-element.67), channel_id=1, source_target_pairs={{0,28},{4,24},{8,20},{12,16},{16,12},{20,8},{24,4},{28,0},{1,29},{... | collective-permute-start | bytes 393224 | tf_op jit(solution)/shard_map/ppermute | solution.py:378
  62.6 9.5 %collective-permute-start.11 = (bf16[64,1024]{1,0:T(8,128)(2,1)S(1)}, bf16[64,1024]{1,0:T(8,128)(2,1)S(1)}, u32[]{:S(2)}, u32[]{:S(2)}) collective-permute-start(bf16[64,1024]{1,0:T(8,128)(2,1)S(1)} %get-tuple-element.61), channel_id=1, source_target_pairs={{0,4},{4,0},{8,12},{12,8},{16,20},{20,16},{24,28},{28,24},{1,5},{5... | collective-permute-start | bytes 393224 | tf_op jit(solution)/shard_map/ppermute | solution.py:378
  62.6 12.2 %collective-permute-start.12 = (bf16[64,1024]{1,0:T(8,128)(2,1)S(1)}, bf16[64,1024]{1,0:T(8,128)(2,1)S(1)}, u32[]{:S(2)}, u32[]{:S(2)}) collective-permute-start(bf16[64,1024]{1,0:T(8,128)(2,1)S(1)} %get-tuple-element.62), channel_id=1, source_target_pairs={{0,8},{4,12},{8,0},{12,4},{16,24},{20,28},{24,16},{28,20},{1,9},{5... | collective-permute-start | bytes 393224 | tf_op jit(solution)/shard_map/ppermute | solution.py:378
  62.7 14.7 %collective-permute-start.13 = (bf16[64,1024]{1,0:T(8,128)(2,1)S(1)}, bf16[64,1024]{1,0:T(8,128)(2,1)S(1)}, u32[]{:S(2)}, u32[]{:S(2)}) collective-permute-start(bf16[64,1024]{1,0:T(8,128)(2,1)S(1)} %get-tuple-element.63), channel_id=1, source_target_pairs={{0,12},{4,8},{8,4},{12,0},{16,28},{20,24},{24,20},{28,16},{1,13},{... | collective-permute-start | bytes 393224 | tf_op jit(solution)/shard_map/ppermute | solution.py:378
  66.1 18.1 %collective-permute-start.14 = (bf16[64,1024]{1,0:T(8,128)(2,1)S(1)}, bf16[64,1024]{1,0:T(8,128)(2,1)S(1)}, u32[]{:S(2)}, u32[]{:S(2)}) collective-permute-start(bf16[64,1024]{1,0:T(8,128)(2,1)S(1)} %get-tuple-element.64.refs_2_), channel_id=1, source_target_pairs={{0,16},{4,20},{8,24},{12,28},{16,0},{20,4},{24,8},{28,12},{1,17},{... | collective-permute-start | bytes 393224 | tf_op jit(solution)/shard_map/ppermute | solution.py:378
  67.0 19.7 %collective-permute-start.15 = (bf16[64,1024]{1,0:T(8,128)(2,1)S(1)}, bf16[64,1024]{1,0:T(8,128)(2,1)S(1)}, u32[]{:S(2)}, u32[]{:S(2)}) collective-permute-start(bf16[64,1024]{1,0:T(8,128)(2,1)S(1)} %get-tuple-element.65), channel_id=1, source_target_pairs={{0,20},{4,16},{8,28},{12,24},{16,4},{20,0},{24,12},{28,8},{1,21},{... | collective-permute-start | bytes 393224 | tf_op jit(solution)/shard_map/ppermute | solution.py:378
  72.0 14.7 %collective-permute-start.18 = (bf16[64,1024]{1,0:T(8,128)(2,1)S(1)}, bf16[64,1024]{1,0:T(8,128)(2,1)S(1)}, u32[]{:S(2)}, u32[]{:S(2)}) collective-permute-start(bf16[64,1024]{1,0:T(8,128)(2,1)S(1)} %get-tuple-element.68), channel_id=1, source_target_pairs={{0,24},{4,28},{8,16},{12,20},{16,8},{20,12},{24,0},{28,4},{1,25},{... | collective-permute-start | bytes 393224 | tf_op jit(solution)/shard_map/ppermute | solution.py:378
  74.8 11.9 %collective-permute-start.19 = (bf16[64,1024]{1,0:T(8,128)(2,1)S(1)}, bf16[64,1024]{1,0:T(8,128)(2,1)S(1)}, u32[]{:S(2)}, u32[]{:S(2)}) collective-permute-start(bf16[64,1024]{1,0:T(8,128)(2,1)S(1)} %get-tuple-element.69), channel_id=1, source_target_pairs={{0,28},{4,24},{8,20},{12,16},{16,12},{20,8},{24,4},{28,0},{1,29},{... | collective-permute-start | bytes 393224 | tf_op jit(solution)/shard_map/ppermute | solution.py:378
  77.4 12.2 %collective-permute-start.3 = (bf16[128,256]{1,0:T(8,128)(2,1)S(1)}, bf16[128,256]{1,0:T(8,128)(2,1)S(1)}, u32[]{:S(2)}, u32[]{:S(2)}) collective-permute-start(bf16[128,256]{1,0:T(8,128)(2,1)S(1)} %get-tuple-element.51), channel_id=1, source_target_pairs={{0,1},{1,0},{2,3},{3,2},{4,5},{5,4},{6,7},{7,6},{8,9},{9,8},{10,11... | collective-permute-start | bytes 196616 | tf_op jit(solution)/shard_map/ppermute | solution.py:378
  84.2 6.4 %collective-permute-start.4 = (bf16[128,256]{1,0:T(8,128)(2,1)S(1)}, bf16[128,256]{1,0:T(8,128)(2,1)S(1)}, u32[]{:S(2)}, u32[]{:S(2)}) collective-permute-start(bf16[128,256]{1,0:T(8,128)(2,1)S(1)} %get-tuple-element.52), channel_id=1, source_target_pairs={{0,2},{1,3},{2,0},{3,1},{4,6},{5,7},{6,4},{7,5},{8,10},{9,11},{10,... | collective-permute-start | bytes 196616 | tf_op jit(solution)/shard_map/ppermute | solution.py:378
  86.7 4.3 %collective-permute-start.5 = (bf16[128,256]{1,0:T(8,128)(2,1)S(1)}, bf16[128,256]{1,0:T(8,128)(2,1)S(1)}, u32[]{:S(2)}, u32[]{:S(2)}) collective-permute-start(bf16[128,256]{1,0:T(8,128)(2,1)S(1)} %get-tuple-element.53), channel_id=1, source_target_pairs={{0,3},{1,2},{2,1},{3,0},{4,7},{5,6},{6,5},{7,4},{8,11},{9,10},{10,... | collective-permute-start | bytes 196616 | tf_op jit(solution)/shard_map/ppermute | solution.py:378
  87.4 4.3 %collective-permute-start.20 = (bf16[128,256]{1,0:T(8,128)(2,1)S(1)}, bf16[128,256]{1,0:T(8,128)(2,1)S(1)}, u32[]{:S(2)}, u32[]{:S(2)}) collective-permute-start(bf16[128,256]{1,0:T(8,128)(2,1)S(1)} %get-tuple-element.71), channel_id=1, source_target_pairs={{0,1},{1,0},{2,3},{3,2},{4,5},{5,4},{6,7},{7,6},{8,9},{9,8},{10,11... | collective-permute-start | bytes 196616 | tf_op jit(solution)/shard_map/ppermute | solution.py:378
  89.1 4.8 %collective-permute-start.21 = (bf16[128,256]{1,0:T(8,128)(2,1)S(1)}, bf16[128,256]{1,0:T(8,128)(2,1)S(1)}, u32[]{:S(2)}, u32[]{:S(2)}) collective-permute-start(bf16[128,256]{1,0:T(8,128)(2,1)S(1)} %get-tuple-element.72), channel_id=1, source_target_pairs={{0,2},{1,3},{2,0},{3,1},{4,6},{5,7},{6,4},{7,5},{8,10},{9,11},{10,... | collective-permute-start | bytes 196616 | tf_op jit(solution)/shard_map/ppermute | solution.py:378
  89.6 4.4 %collective-permute-start.22 = (bf16[128,256]{1,0:T(8,128)(2,1)S(1)}, bf16[128,256]{1,0:T(8,128)(2,1)S(1)}, u32[]{:S(2)}, u32[]{:S(2)}) collective-permute-start(bf16[128,256]{1,0:T(8,128)(2,1)S(1)} %get-tuple-element.73), channel_id=1, source_target_pairs={{0,3},{1,2},{2,1},{3,0},{4,7},{5,6},{6,5},{7,4},{8,11},{9,10},{10,... | collective-permute-start | bytes 196616 | tf_op jit(solution)/shard_map/ppermute | solution.py:378
  (8 other events, 111.6 us)

commit v5 on v4

--- a/solution.py
+++ b/solution.py
@@ -204,7 +204,12 @@
     return picks
 
 
-def rows_kernel(experts, blocks, me, at, routes_t, gain, conv, *refs):
+def picks_kernel(experts, routes_t, *out):
+    for pick, ref in zip(slots(routes_t[...], experts), out):
+        ref[...] = pick.astype(bf16).reshape(ref.shape)
+
+
+def rows_kernel(experts, blocks, me, at, first, second, gain, conv, *refs):
     pieces, refs = refs[:blocks], refs[blocks:]
     mixed_out, refs = refs[:blocks], refs[blocks:]
     send, (normed_out, mixed, sent) = refs[:-3], refs[-3:]
@@ -224,8 +229,7 @@
     for h in range(blocks):
         lanes = slice(h * chans, (h + 1) * chans)
         normed_out[:, lanes] = (mixed[h].astype(f32) * scale * gain[:, lanes]).astype(bf16)
-    first, second = slots(routes_t[...], experts)
-    pick = (first + second).astype(bf16).reshape(experts * CAP, rows)
+    pick = first[...] + second[...]
     values = jnp.dot(pick, normed_out[...], preferred_element_type=f32).astype(bf16)
     _, size, _ = sent.shape
     copies = shards * size // (experts * CAP)
@@ -300,10 +304,10 @@
     )(w_up, w_down, *got, *after)
 
 
-def combine_kernel(experts, blocks, shards, me, at, routes_t, gates, *refs):
+def combine_kernel(experts, blocks, shards, me, at, first, second, gates, *refs):
     back, out, home = refs[: -blocks - 1], refs[-blocks - 1 : -1], refs[-1]
     _, size, width = home.shape
-    rows = routes_t.shape[1]
+    rows = first.shape[1]
     chans = width // blocks
     copies = shards * size // (experts * CAP)
     if len(back) == 1:
@@ -311,10 +315,10 @@
     else:
         for o in range(shards):
             home[at[0] ^ o] = back[o][...]
-    picks = slots(routes_t[...], experts)
+    picks = (first, second)
     total = jnp.zeros((rows, width), f32)
     for k in range(2):
-        pick = picks[k].astype(bf16).reshape(experts * CAP, rows)
+        pick = picks[k][...]
         for c in range(copies):
             if copies == 1:
                 values = home[...].reshape(experts * CAP, width)
@@ -427,7 +431,14 @@
     )
     got = spread_out(spread, "ctx")
     own, *pieces = swap(pieces, "ch", around, blocks)
-    got, pieces = lax.optimization_barrier((got, pieces))
+    picks = call(
+        functools.partial(picks_kernel, experts),
+        [shape((experts * CAP, rows), bf16)] * 2,
+        [],
+        [routes.T],
+        "picks",
+    )
+    got, pieces, picks = lax.optimization_barrier((got, pieces, picks))
     pieces = [own, *pieces]
     conv = call(
         functools.partial(conv_kernel, blocks),
@@ -439,7 +450,6 @@
     )
     conv = spread_out(conv.reshape(shards * blocks, per, rows), ("ctx", "ch"))
     conv = conv.reshape(shards, blocks, per, rows)
-    routes_t = routes.T
     if direct:
         send_shape = [shape((size, width), bf16)] * shards
     else:
@@ -448,7 +458,7 @@
         functools.partial(rows_kernel, experts, blocks),
         [shape((rows, chans), bf16)] * blocks + send_shape + [shape((rows, width), bf16)],
         [me, at],
-        [routes_t, norm_gain.reshape(1, width), conv, *pieces],
+        [*picks, norm_gain.reshape(1, width), conv, *pieces],
         "rows",
         [pltpu.VMEM((blocks, rows, chans), bf16), pltpu.VMEM((shards, size, width), bf16)],
     )
@@ -476,7 +486,7 @@
         functools.partial(combine_kernel, experts, blocks, shards),
         [shape((rows, chans), bf16)] * blocks,
         [me, at],
-        [routes_t, gates, *back],
+        [*picks, gates, *back],
         "combine",
         [pltpu.VMEM((shards, size, width), bf16)],
     )

time: 95.5 us -> 95.4 us (level)
    unnamed x18 -> x20, local copies, waits for them, and re-layouts: 5.65 us -> 6.32 us
    pallas_call x5 -> x6, Pallas kernels: 5.35 us -> 5.41 us  [call(): pl.pallas_call(kernel, out_shape=out_shape, in_specs=[smem] * len(scalars...]
where the time goes in v5:
time: 95.4 us; the launch traced here: 94.6 us
  starting transfers between devices  37.5 us (39%)
  waiting for transfers between devices  21 us (22%)
  Pallas kernels  14.8 us (16%)
  blocking collectives  14.1 us (15%)
  local copies, waits for them, and re-layouts  6.32 us (7%)
    ppermute x23, starting transfers between devices, swap(): lax.ppermute(piece, axis, [(i, i ^ o) for i in range(total)])  30.3 us
    all_to_all x1, blocking collectives, spread_out(): return lax.all_to_all(block, axis, split_axis=0, concat_axis=0, tiled=True)  14.1 us
    ppermute x23, waiting for transfers between devices, swap(): lax.ppermute(piece, axis, [(i, i ^ o) for i in range(total)])  13.5 us
    all_to_all x1, waiting for transfers between devices, spread_out(): return lax.all_to_all(block, axis, split_axis=0, concat_axis=0, tiled=True)  7.47 us
    all_to_all x1, starting transfers between devices, spread_out(): return lax.all_to_all(block, axis, split_axis=0, concat_axis=0, tiled=True)  7.26 us
    unnamed x20, local copies, waits for them, and re-layouts  6.32 us
    pallas_call x3, Pallas kernels, run_experts(): pl.pallas_call(functools.partial(expert_kernel, len(got), owned), out_sha...  5.49 us
    pallas_call x6, Pallas kernels, call(): pl.pallas_call(kernel, out_shape=out_shape, in_specs=[smem] * len(scalars...  5.41 us
  transfers between devices with their start and end apart: 24, of which 9 were waited for; matrix products, arithmetic and copies ran while one was open for 0% of the time, Pallas kernels for 9%

profile of v5, /device:TPU:0, one launch (start us, length us, event | category | flops | bytes accessed | tf_op | source)
XLA Modules:
  0.0 94.6 jit_solution(1041952048475402835)
XLA Ops:
  0.6 2.1 %prep.1 = bf16[8,64,512]{2,1,0:T(8,128)(2,1)} custom-call(s32[1]{0:T(128)} %bitcast.1.at, bf16[512,256]{1,0:T(8,128)(2,1)} %far_sig.1, f32[512,256]{1,0:T(8,128)} %far_taps.1, f32[1,256]{1,0:T(1,128)} %bitcast.11), custom_call_target="tpu_custom_call" | custom-call | tf_op jit(solution)/shard_map/prep/pallas_call | solution.py:407
  2.8 7.3 %all-to-all-start = ((bf16[8,64,512]{2,1,0:T(8,128)(2,1)}), bf16[8,64,512]{2,1,0:T(8,128)(2,1)S(1)}, u32[]{:S(2)}, u32[]{:S(2)}) async-start(bf16[8,64,512]{2,1,0:T(8,128)(2,1)} %prep.1), calls=%async_computation | async-start | bytes 1048576 | tf_op jit(solution)/shard_map/all_to_all | solution.py:388
  11.4 1.6 %collective-permute-start.1 = (bf16[128,256]{1,0:T(8,128)(2,1)S(1)}, bf16[128,256]{1,0:T(8,128)(2,1)S(1)}, u32[]{:S(2)}, u32[]{:S(2)}) collective-permute-start(bf16[128,256]{1,0:T(8,128)(2,1)S(1)} %get-tuple-element.43), channel_id=1, source_target_pairs={{0,2},{1,3},{2,0},{3,1},{4,6},{5,7},{6,4},{7,5},{8,10},{9,11},{10,... | collective-permute-start | bytes 196616 | tf_op jit(solution)/shard_map/ppermute | solution.py:382
  14.7 1.3 %collective-permute-done.1.refs_2_ = bf16[128,256]{1,0:T(8,128)(2,1)S(1)} collective-permute-done((bf16[128,256]{1,0:T(8,128)(2,1)S(1)}, bf16[128,256]{1,0:T(8,128)(2,1)S(1)}, u32[]{:S(2)}, u32[]{:S(2)}) %collective-permute-start.1) | collective-permute-done | bytes 65568 | tf_op jit(solution)/shard_map/ppermute | solution.py:382
  17.1 7.5 %all-to-all-done.got = bf16[8,64,512]{2,1,0:T(8,128)(2,1)S(1)} async-done(((bf16[8,64,512]{2,1,0:T(8,128)(2,1)}), bf16[8,64,512]{2,1,0:T(8,128)(2,1)S(1)}, u32[]{:S(2)}, u32[]{:S(2)}) %all-to-all-start) | async-done | bytes 524320 | tf_op jit(solution)/shard_map/all_to_all | solution.py:388
  24.5 2.8 %conv.1 = bf16[8,4,32,128]{3,2,1,0:T(8,128)(2,1)S(1)} custom-call(bf16[8,64,512]{2,1,0:T(8,128)(2,1)S(1)} %all-to-all-done.got, f32[8,512]{1,0:T(8,128)S(1)} %get-tuple-element.50.turn_cos, f32[8,512]{1,0:T(8,128)S(1)} %get-tuple-element.51.turn_sin, bf16[512,512]{1,0:T(8,128)(2,1)S(1)} %get-tuple-element.52.cos, bf16[512,512]{1,0:T(8,128)(2,1)S(1)} %get-tuple-element.53.sin), custom_call_target="tpu_custom_call" | custom-call | tf_op jit(solution)/shard_map/conv/pallas_call | solution.py:27
  27.3 14.1 %all_to_all.10 = bf16[32,32,128]{2,1,0:T(8,128)(2,1)S(1)} all-to-all(bf16[32,32,128]{2,1,0:T(8,128)(2,1)S(1)} %bitcast.7), channel_id=1, replica_groups=mesh['ctx'=8,'ch'=4] {'ctx','ch'}, dimensions={0} | all-to-all | bytes 524288 | tf_op jit(solution)/shard_map/all_to_all | solution.py:388
  42.5 3.0 %collective-permute-start.7 = (bf16[64,1024]{1,0:T(8,128)(2,1)S(1)}, bf16[64,1024]{1,0:T(8,128)(2,1)S(1)}, u32[]{:S(2)}, u32[]{:S(2)}) collective-permute-start(bf16[64,1024]{1,0:T(8,128)(2,1)S(1)} %get-tuple-element.65), channel_id=1, source_target_pairs={{0,20},{4,16},{8,28},{12,24},{16,4},{20,0},{24,12},{28,8},{1,21},{... | collective-permute-start | bytes 393224 | tf_op jit(solution)/shard_map/ppermute | solution.py:382
  45.5 1.5 %collective-permute-start.8 = (bf16[64,1024]{1,0:T(8,128)(2,1)S(1)}, bf16[64,1024]{1,0:T(8,128)(2,1)S(1)}, u32[]{:S(2)}, u32[]{:S(2)}) collective-permute-start(bf16[64,1024]{1,0:T(8,128)(2,1)S(1)} %get-tuple-element.66), channel_id=1, source_target_pairs={{0,12},{4,8},{8,4},{12,0},{16,28},{20,24},{24,20},{28,16},{1,13},{... | collective-permute-start | bytes 393224 | tf_op jit(solution)/shard_map/ppermute | solution.py:382
  49.0 2.2 %copy-done = bf16[8,1024,256]{2,1,0:T(8,128)(2,1)S(1)} copy-done((bf16[8,1024,256]{2,1,0:T(8,128)(2,1)S(1)}, bf16[8,1024,256]{2,1,0:T(8,128)(2,1)}, u32[]{:S(2)}) %copy-start) | copy-done | bytes 4194328
  51.2 2.2 %copy-done.2 = bf16[8,256,1024]{2,1,0:T(8,128)(2,1)S(1)} copy-done((bf16[8,256,1024]{2,1,0:T(8,128)(2,1)S(1)}, bf16[8,256,1024]{2,1,0:T(8,128)(2,1)}, u32[]{:S(2)}) %copy-start.2) | copy-done | bytes 4194328
  53.4 1.6 %experts.3.refs_5_.refs_0_ = bf16[64,1024]{1,0:T(8,128)(2,1)S(1)} custom-call(bf16[8,1024,256]{2,1,0:T(8,128)(2,1)S(1)} %copy-done, bf16[8,256,1024]{2,1,0:T(8,128)(2,1)S(1)} %copy-done.2, bf16[64,1024]{1,0:T(8,128)(2,1)S(1)} %get-tuple-element.63.refs_0_), custom_call_target="tpu_custom_call" | custom-call | flops 1 | bytes 1 | tf_op jit(solution)/shard_map/experts/pallas_call | solution.py:295
  56.6 2.9 %collective-permute-start.17 = (bf16[64,1024]{1,0:T(8,128)(2,1)S(1)}, bf16[64,1024]{1,0:T(8,128)(2,1)S(1)}, u32[]{:S(2)}, u32[]{:S(2)}) collective-permute-start(bf16[64,1024]{1,0:T(8,128)(2,1)S(1)} %get-tuple-element.75), channel_id=1, source_target_pairs={{0,28},{4,24},{8,20},{12,16},{16,12},{20,8},{24,4},{28,0},{1,29},{... | collective-permute-start | bytes 393224 | tf_op jit(solution)/shard_map/ppermute | solution.py:382
  60.5 2.0 %experts.4 = (bf16[64,1024]{1,0:T(8,128)(2,1)S(1)}, bf16[64,1024]{1,0:T(8,128)(2,1)S(1)}, bf16[64,1024]{1,0:T(8,128)(2,1)S(1)}, bf16[64,1024]{1,0:T(8,128)(2,1)S(1)}, bf16[64,1024]{1,0:T(8,128)(2,1)S(1)}) custom-call(bf16[8,1024,256]{2,1,0:T(8,128)(2,1)S(1)} %copy-done.1, bf16[8,256,1024]{2,1,0:T(8,128)(2,1)S(1)} %copy-done.3, ...), custom_call_target="tpu_custom_call" | custom-call | flops 1 | bytes 1 | tf_op jit(solution)/shard_map/experts/pallas_call | solution.py:295
  62.7 3.4 %collective-permute-start.13 = (bf16[64,1024]{1,0:T(8,128)(2,1)S(1)}, bf16[64,1024]{1,0:T(8,128)(2,1)S(1)}, u32[]{:S(2)}, u32[]{:S(2)}) collective-permute-start(bf16[64,1024]{1,0:T(8,128)(2,1)S(1)} %get-tuple-element.71), channel_id=1, source_target_pairs={{0,12},{4,8},{8,4},{12,0},{16,28},{20,24},{24,20},{28,16},{1,13},{... | collective-permute-start | bytes 393224 | tf_op jit(solution)/shard_map/ppermute | solution.py:382
  66.9 3.2 %collective-permute-start.15 = (bf16[64,1024]{1,0:T(8,128)(2,1)S(1)}, bf16[64,1024]{1,0:T(8,128)(2,1)S(1)}, u32[]{:S(2)}, u32[]{:S(2)}) collective-permute-start(bf16[64,1024]{1,0:T(8,128)(2,1)S(1)} %get-tuple-element.73), channel_id=1, source_target_pairs={{0,20},{4,16},{8,28},{12,24},{16,4},{20,0},{24,12},{28,8},{1,21},{... | collective-permute-start | bytes 393224 | tf_op jit(solution)/shard_map/ppermute | solution.py:382
  70.1 1.9 %experts.5 = (bf16[64,1024]{1,0:T(8,128)(2,1)S(1)}, bf16[64,1024]{1,0:T(8,128)(2,1)S(1)}) custom-call(bf16[8,1024,256]{2,1,0:T(8,128)(2,1)S(1)} %copy-done.1, bf16[8,256,1024]{2,1,0:T(8,128)(2,1)S(1)} %copy-done.3, bf16[64,1024]{1,0:T(8,128)(2,1)S(1)} %collective-permute-done.16.refs_0_, bf16[64,1024]{1,0:T(8,128)(2,1)S(1)} %collective-permute-done.17.refs_1_, ...), custom_call_target="tpu_custom_call" | custom-call | flops 1 | bytes 1 | tf_op jit(solution)/shard_map/experts/pallas_call | solution.py:295
  72.0 2.8 %collective-permute-start.18 = (bf16[64,1024]{1,0:T(8,128)(2,1)S(1)}, bf16[64,1024]{1,0:T(8,128)(2,1)S(1)}, u32[]{:S(2)}, u32[]{:S(2)}) collective-permute-start(bf16[64,1024]{1,0:T(8,128)(2,1)S(1)} %get-tuple-element.76), channel_id=1, source_target_pairs={{0,24},{4,28},{8,16},{12,20},{16,8},{20,12},{24,0},{28,4},{1,25},{... | collective-permute-start | bytes 393224 | tf_op jit(solution)/shard_map/ppermute | solution.py:382
  74.8 2.7 %collective-permute-start.19 = (bf16[64,1024]{1,0:T(8,128)(2,1)S(1)}, bf16[64,1024]{1,0:T(8,128)(2,1)S(1)}, u32[]{:S(2)}, u32[]{:S(2)}) collective-permute-start(bf16[64,1024]{1,0:T(8,128)(2,1)S(1)} %get-tuple-element.77), channel_id=1, source_target_pairs={{0,28},{4,24},{8,20},{12,16},{16,12},{20,8},{24,4},{28,0},{1,29},{... | collective-permute-start | bytes 393224 | tf_op jit(solution)/shard_map/ppermute | solution.py:382
  78.5 5.7 %collective-permute-done.14.refs_4_ = bf16[64,1024]{1,0:T(8,128)(2,1)S(1)} collective-permute-done((bf16[64,1024]{1,0:T(8,128)(2,1)S(1)}, bf16[64,1024]{1,0:T(8,128)(2,1)S(1)}, u32[]{:S(2)}, u32[]{:S(2)}) %collective-permute-start.14) | collective-permute-done | bytes 131104 | tf_op jit(solution)/shard_map/ppermute | solution.py:382
  84.2 1.3 %collective-permute-start.4 = (bf16[128,256]{1,0:T(8,128)(2,1)S(1)}, bf16[128,256]{1,0:T(8,128)(2,1)S(1)}, u32[]{:S(2)}, u32[]{:S(2)}) collective-permute-start(bf16[128,256]{1,0:T(8,128)(2,1)S(1)} %get-tuple-element.60), channel_id=1, source_target_pairs={{0,2},{1,3},{2,0},{3,1},{4,6},{5,7},{6,4},{7,5},{8,10},{9,11},{10,... | collective-permute-start | bytes 196616 | tf_op jit(solution)/shard_map/ppermute | solution.py:382
  85.4 1.3 %collective-permute-done.15.refs_5_ = bf16[64,1024]{1,0:T(8,128)(2,1)S(1)} collective-permute-done((bf16[64,1024]{1,0:T(8,128)(2,1)S(1)}, bf16[64,1024]{1,0:T(8,128)(2,1)S(1)}, u32[]{:S(2)}, u32[]{:S(2)}) %collective-permute-start.15) | collective-permute-done | bytes 131104 | tf_op jit(solution)/shard_map/ppermute | solution.py:382
  87.3 1.7 %collective-permute-start.20 = (bf16[128,256]{1,0:T(8,128)(2,1)S(1)}, bf16[128,256]{1,0:T(8,128)(2,1)S(1)}, u32[]{:S(2)}, u32[]{:S(2)}) collective-permute-start(bf16[128,256]{1,0:T(8,128)(2,1)S(1)} %get-tuple-element.79), channel_id=1, source_target_pairs={{0,1},{1,0},{2,3},{3,2},{4,5},{5,4},{6,7},{7,6},{8,9},{9,8},{10,11... | collective-permute-start | bytes 196616 | tf_op jit(solution)/shard_map/ppermute | solution.py:382
  91.8 2.1 %collective-permute-done.21.refs_2_ = bf16[128,256]{1,0:T(8,128)(2,1)S(1)} collective-permute-done((bf16[128,256]{1,0:T(8,128)(2,1)S(1)}, bf16[128,256]{1,0:T(8,128)(2,1)S(1)}, u32[]{:S(2)}, u32[]{:S(2)}) %collective-permute-start.21) | collective-permute-done | bytes 65568 | tf_op jit(solution)/shard_map/ppermute | solution.py:382
  (58 shorter events, 15.9 us)
Async XLA Ops:
  2.8 21.8 %all-to-all-start = ((bf16[8,64,512]{2,1,0:T(8,128)(2,1)}), bf16[8,64,512]{2,1,0:T(8,128)(2,1)S(1)}, u32[]{:S(2)}, u32[]{:S(2)}) async-start(bf16[8,64,512]{2,1,0:T(8,128)(2,1)} %prep.1), calls=%async_computation | async-start | bytes 1048576 | tf_op jit(solution)/shard_map/all_to_all | solution.py:388
  11.4 3.3 %collective-permute-start = (bf16[128,256]{1,0:T(8,128)(2,1)S(1)}, bf16[128,256]{1,0:T(8,128)(2,1)S(1)}, u32[]{:S(2)}, u32[]{:S(2)}) collective-permute-start(bf16[128,256]{1,0:T(8,128)(2,1)S(1)} %get-tuple-element.42), channel_id=1, source_target_pairs={{0,1},{1,0},{2,3},{3,2},{4,5},{5,4},{6,7},{7,6},{8,9},{9,8},{10,11... | collective-permute-start | bytes 196616 | tf_op jit(solution)/shard_map/ppermute | solution.py:382
  11.4 4.5 %collective-permute-start.1 = (bf16[128,256]{1,0:T(8,128)(2,1)S(1)}, bf16[128,256]{1,0:T(8,128)(2,1)S(1)}, u32[]{:S(2)}, u32[]{:S(2)}) collective-permute-start(bf16[128,256]{1,0:T(8,128)(2,1)S(1)} %get-tuple-element.43), channel_id=1, source_target_pairs={{0,2},{1,3},{2,0},{3,1},{4,6},{5,7},{6,4},{7,5},{8,10},{9,11},{10,... | collective-permute-start | bytes 196616 | tf_op jit(solution)/shard_map/ppermute | solution.py:382
  13.0 4.0 %collective-permute-start.2 = (bf16[128,256]{1,0:T(8,128)(2,1)S(1)}, bf16[128,256]{1,0:T(8,128)(2,1)S(1)}, u32[]{:S(2)}, u32[]{:S(2)}) collective-permute-start(bf16[128,256]{1,0:T(8,128)(2,1)S(1)} %get-tuple-element.44), channel_id=1, source_target_pairs={{0,3},{1,2},{2,1},{3,0},{4,7},{5,6},{6,5},{7,4},{8,11},{9,10},{10,... | collective-permute-start | bytes 196616 | tf_op jit(solution)/shard_map/ppermute | solution.py:382
  42.2 12.8 %collective-permute-start.6 = (bf16[64,1024]{1,0:T(8,128)(2,1)S(1)}, bf16[64,1024]{1,0:T(8,128)(2,1)S(1)}, u32[]{:S(2)}, u32[]{:S(2)}) collective-permute-start(bf16[64,1024]{1,0:T(8,128)(2,1)S(1)} %get-tuple-element.64), channel_id=1, source_target_pairs={{0,16},{4,20},{8,24},{12,28},{16,0},{20,4},{24,8},{28,12},{1,17},{... | collective-permute-start | bytes 393224 | tf_op jit(solution)/shard_map/ppermute | solution.py:382
  42.5 14.1 %collective-permute-start.7 = (bf16[64,1024]{1,0:T(8,128)(2,1)S(1)}, bf16[64,1024]{1,0:T(8,128)(2,1)S(1)}, u32[]{:S(2)}, u32[]{:S(2)}) collective-permute-start(bf16[64,1024]{1,0:T(8,128)(2,1)S(1)} %get-tuple-element.65), channel_id=1, source_target_pairs={{0,20},{4,16},{8,28},{12,24},{16,4},{20,0},{24,12},{28,8},{1,21},{... | collective-permute-start | bytes 393224 | tf_op jit(solution)/shard_map/ppermute | solution.py:382
  45.5 14.0 %collective-permute-start.8 = (bf16[64,1024]{1,0:T(8,128)(2,1)S(1)}, bf16[64,1024]{1,0:T(8,128)(2,1)S(1)}, u32[]{:S(2)}, u32[]{:S(2)}) collective-permute-start(bf16[64,1024]{1,0:T(8,128)(2,1)S(1)} %get-tuple-element.66), channel_id=1, source_target_pairs={{0,12},{4,8},{8,4},{12,0},{16,28},{20,24},{24,20},{28,16},{1,13},{... | collective-permute-start | bytes 393224 | tf_op jit(solution)/shard_map/ppermute | solution.py:382
  47.0 13.6 %collective-permute-start.9 = (bf16[64,1024]{1,0:T(8,128)(2,1)S(1)}, bf16[64,1024]{1,0:T(8,128)(2,1)S(1)}, u32[]{:S(2)}, u32[]{:S(2)}) collective-permute-start(bf16[64,1024]{1,0:T(8,128)(2,1)S(1)} %get-tuple-element.67), channel_id=1, source_target_pairs={{0,8},{4,12},{8,0},{12,4},{16,24},{20,28},{24,16},{28,20},{1,9},{5... | collective-permute-start | bytes 393224 | tf_op jit(solution)/shard_map/ppermute | solution.py:382
  48.1 12.4 %collective-permute-start.10 = (bf16[64,1024]{1,0:T(8,128)(2,1)S(1)}, bf16[64,1024]{1,0:T(8,128)(2,1)S(1)}, u32[]{:S(2)}, u32[]{:S(2)}) collective-permute-start(bf16[64,1024]{1,0:T(8,128)(2,1)S(1)} %get-tuple-element.68), channel_id=1, source_target_pairs={{0,4},{4,0},{8,12},{12,8},{16,20},{20,16},{24,28},{28,24},{1,5},{5... | collective-permute-start | bytes 393224 | tf_op jit(solution)/shard_map/ppermute | solution.py:382
  54.9 11.2 %collective-permute-start.16 = (bf16[64,1024]{1,0:T(8,128)(2,1)S(1)}, bf16[64,1024]{1,0:T(8,128)(2,1)S(1)}, u32[]{:S(2)}, u32[]{:S(2)}) collective-permute-start(bf16[64,1024]{1,0:T(8,128)(2,1)S(1)} %get-tuple-element.74), channel_id=1, source_target_pairs={{0,24},{4,28},{8,16},{12,20},{16,8},{20,12},{24,0},{28,4},{1,25},{... | collective-permute-start | bytes 393224 | tf_op jit(solution)/shard_map/ppermute | solution.py:382
  56.6 10.3 %collective-permute-start.17 = (bf16[64,1024]{1,0:T(8,128)(2,1)S(1)}, bf16[64,1024]{1,0:T(8,128)(2,1)S(1)}, u32[]{:S(2)}, u32[]{:S(2)}) collective-permute-start(bf16[64,1024]{1,0:T(8,128)(2,1)S(1)} %get-tuple-element.75), channel_id=1, source_target_pairs={{0,28},{4,24},{8,20},{12,16},{16,12},{20,8},{24,4},{28,0},{1,29},{... | collective-permute-start | bytes 393224 | tf_op jit(solution)/shard_map/ppermute | solution.py:382
  62.6 9.4 %collective-permute-start.11 = (bf16[64,1024]{1,0:T(8,128)(2,1)S(1)}, bf16[64,1024]{1,0:T(8,128)(2,1)S(1)}, u32[]{:S(2)}, u32[]{:S(2)}) collective-permute-start(bf16[64,1024]{1,0:T(8,128)(2,1)S(1)} %get-tuple-element.69), channel_id=1, source_target_pairs={{0,4},{4,0},{8,12},{12,8},{16,20},{20,16},{24,28},{28,24},{1,5},{5... | collective-permute-start | bytes 393224 | tf_op jit(solution)/shard_map/ppermute | solution.py:382
  62.6 12.2 %collective-permute-start.12 = (bf16[64,1024]{1,0:T(8,128)(2,1)S(1)}, bf16[64,1024]{1,0:T(8,128)(2,1)S(1)}, u32[]{:S(2)}, u32[]{:S(2)}) collective-permute-start(bf16[64,1024]{1,0:T(8,128)(2,1)S(1)} %get-tuple-element.70), channel_id=1, source_target_pairs={{0,8},{4,12},{8,0},{12,4},{16,24},{20,28},{24,16},{28,20},{1,9},{5... | collective-permute-start | bytes 393224 | tf_op jit(solution)/shard_map/ppermute | solution.py:382
  62.7 14.7 %collective-permute-start.13 = (bf16[64,1024]{1,0:T(8,128)(2,1)S(1)}, bf16[64,1024]{1,0:T(8,128)(2,1)S(1)}, u32[]{:S(2)}, u32[]{:S(2)}) collective-permute-start(bf16[64,1024]{1,0:T(8,128)(2,1)S(1)} %get-tuple-element.71), channel_id=1, source_target_pairs={{0,12},{4,8},{8,4},{12,0},{16,28},{20,24},{24,20},{28,16},{1,13},{... | collective-permute-start | bytes 393224 | tf_op jit(solution)/shard_map/ppermute | solution.py:382
  66.1 18.0 %collective-permute-start.14 = (bf16[64,1024]{1,0:T(8,128)(2,1)S(1)}, bf16[64,1024]{1,0:T(8,128)(2,1)S(1)}, u32[]{:S(2)}, u32[]{:S(2)}) collective-permute-start(bf16[64,1024]{1,0:T(8,128)(2,1)S(1)} %get-tuple-element.72.refs_2_), channel_id=1, source_target_pairs={{0,16},{4,20},{8,24},{12,28},{16,0},{20,4},{24,8},{28,12},{1,17},{... | collective-permute-start | bytes 393224 | tf_op jit(solution)/shard_map/ppermute | solution.py:382
  66.9 19.8 %collective-permute-start.15 = (bf16[64,1024]{1,0:T(8,128)(2,1)S(1)}, bf16[64,1024]{1,0:T(8,128)(2,1)S(1)}, u32[]{:S(2)}, u32[]{:S(2)}) collective-permute-start(bf16[64,1024]{1,0:T(8,128)(2,1)S(1)} %get-tuple-element.73), channel_id=1, source_target_pairs={{0,20},{4,16},{8,28},{12,24},{16,4},{20,0},{24,12},{28,8},{1,21},{... | collective-permute-start | bytes 393224 | tf_op jit(solution)/shard_map/ppermute | solution.py:382
  72.0 14.7 %collective-permute-start.18 = (bf16[64,1024]{1,0:T(8,128)(2,1)S(1)}, bf16[64,1024]{1,0:T(8,128)(2,1)S(1)}, u32[]{:S(2)}, u32[]{:S(2)}) collective-permute-start(bf16[64,1024]{1,0:T(8,128)(2,1)S(1)} %get-tuple-element.76), channel_id=1, source_target_pairs={{0,24},{4,28},{8,16},{12,20},{16,8},{20,12},{24,0},{28,4},{1,25},{... | collective-permute-start | bytes 393224 | tf_op jit(solution)/shard_map/ppermute | solution.py:382
  74.8 11.9 %collective-permute-start.19 = (bf16[64,1024]{1,0:T(8,128)(2,1)S(1)}, bf16[64,1024]{1,0:T(8,128)(2,1)S(1)}, u32[]{:S(2)}, u32[]{:S(2)}) collective-permute-start(bf16[64,1024]{1,0:T(8,128)(2,1)S(1)} %get-tuple-element.77), channel_id=1, source_target_pairs={{0,28},{4,24},{8,20},{12,16},{16,12},{20,8},{24,4},{28,0},{1,29},{... | collective-permute-start | bytes 393224 | tf_op jit(solution)/shard_map/ppermute | solution.py:382
  77.5 12.0 %collective-permute-start.3 = (bf16[128,256]{1,0:T(8,128)(2,1)S(1)}, bf16[128,256]{1,0:T(8,128)(2,1)S(1)}, u32[]{:S(2)}, u32[]{:S(2)}) collective-permute-start(bf16[128,256]{1,0:T(8,128)(2,1)S(1)} %get-tuple-element.59), channel_id=1, source_target_pairs={{0,1},{1,0},{2,3},{3,2},{4,5},{5,4},{6,7},{7,6},{8,9},{9,8},{10,11... | collective-permute-start | bytes 196616 | tf_op jit(solution)/shard_map/ppermute | solution.py:382
  84.2 6.2 %collective-permute-start.4 = (bf16[128,256]{1,0:T(8,128)(2,1)S(1)}, bf16[128,256]{1,0:T(8,128)(2,1)S(1)}, u32[]{:S(2)}, u32[]{:S(2)}) collective-permute-start(bf16[128,256]{1,0:T(8,128)(2,1)S(1)} %get-tuple-element.60), channel_id=1, source_target_pairs={{0,2},{1,3},{2,0},{3,1},{4,6},{5,7},{6,4},{7,5},{8,10},{9,11},{10,... | collective-permute-start | bytes 196616 | tf_op jit(solution)/shard_map/ppermute | solution.py:382
  86.7 4.3 %collective-permute-start.5 = (bf16[128,256]{1,0:T(8,128)(2,1)S(1)}, bf16[128,256]{1,0:T(8,128)(2,1)S(1)}, u32[]{:S(2)}, u32[]{:S(2)}) collective-permute-start(bf16[128,256]{1,0:T(8,128)(2,1)S(1)} %get-tuple-element.61), channel_id=1, source_target_pairs={{0,3},{1,2},{2,1},{3,0},{4,7},{5,6},{6,5},{7,4},{8,11},{9,10},{10,... | collective-permute-start | bytes 196616 | tf_op jit(solution)/shard_map/ppermute | solution.py:382
  87.3 4.5 %collective-permute-start.20 = (bf16[128,256]{1,0:T(8,128)(2,1)S(1)}, bf16[128,256]{1,0:T(8,128)(2,1)S(1)}, u32[]{:S(2)}, u32[]{:S(2)}) collective-permute-start(bf16[128,256]{1,0:T(8,128)(2,1)S(1)} %get-tuple-element.79), channel_id=1, source_target_pairs={{0,1},{1,0},{2,3},{3,2},{4,5},{5,4},{6,7},{7,6},{8,9},{9,8},{10,11... | collective-permute-start | bytes 196616 | tf_op jit(solution)/shard_map/ppermute | solution.py:382
  89.0 4.9 %collective-permute-start.21 = (bf16[128,256]{1,0:T(8,128)(2,1)S(1)}, bf16[128,256]{1,0:T(8,128)(2,1)S(1)}, u32[]{:S(2)}, u32[]{:S(2)}) collective-permute-start(bf16[128,256]{1,0:T(8,128)(2,1)S(1)} %get-tuple-element.80), channel_id=1, source_target_pairs={{0,2},{1,3},{2,0},{3,1},{4,6},{5,7},{6,4},{7,5},{8,10},{9,11},{10,... | collective-permute-start | bytes 196616 | tf_op jit(solution)/shard_map/ppermute | solution.py:382
  89.5 4.4 %collective-permute-start.22 = (bf16[128,256]{1,0:T(8,128)(2,1)S(1)}, bf16[128,256]{1,0:T(8,128)(2,1)S(1)}, u32[]{:S(2)}, u32[]{:S(2)}) collective-permute-start(bf16[128,256]{1,0:T(8,128)(2,1)S(1)} %get-tuple-element.81), channel_id=1, source_target_pairs={{0,3},{1,2},{2,1},{3,0},{4,7},{5,6},{6,5},{7,4},{8,11},{9,10},{10,... | collective-permute-start | bytes 196616 | tf_op jit(solution)/shard_map/ppermute | solution.py:382
  (9 other events, 82.4 us)

commit v6 on v4

--- a/solution.py
+++ b/solution.py
@@ -465,6 +465,7 @@
             done = run_experts(there[i], w_up, w_down, owned, done[:1])
             home.update(zip(group, swap(done, "ctx", group, shards)))
         back = [home[o] for o in range(shards)]
+        mixed, done = lax.optimization_barrier((mixed, done))
         mixed = swap(mixed, "ch", around, blocks)
     else:
         there = spread_out(send[0], "ctx")

time: 95.5 us -> 95.5 us (level)
  no operation moved by 1% of the time
where the time goes in v6:
time: 95.5 us; the launch traced here: 94.7 us
  starting transfers between devices  37.6 us (39%)
  waiting for transfers between devices  21.8 us (23%)
  Pallas kernels  14.8 us (15%)
  blocking collectives  14.1 us (15%)
  local copies, waits for them, and re-layouts  5.65 us (6%)
    ppermute x23, starting transfers between devices, swap(): lax.ppermute(piece, axis, [(i, i ^ o) for i in range(total)])  30.3 us
    ppermute x23, waiting for transfers between devices, swap(): lax.ppermute(piece, axis, [(i, i ^ o) for i in range(total)])  14.3 us
    all_to_all x1, blocking collectives, spread_out(): return lax.all_to_all(block, axis, split_axis=0, concat_axis=0, tiled=True)  14.1 us
    all_to_all x1, waiting for transfers between devices, spread_out(): return lax.all_to_all(block, axis, split_axis=0, concat_axis=0, tiled=True)  7.47 us
    all_to_all x1, starting transfers between devices, spread_out(): return lax.all_to_all(block, axis, split_axis=0, concat_axis=0, tiled=True)  7.26 us
    unnamed x18, local copies, waits for them, and re-layouts  5.65 us
    pallas_call x3, Pallas kernels, run_experts(): pl.pallas_call(functools.partial(expert_kernel, len(got), owned), out_sha...  5.51 us
    pallas_call x5, Pallas kernels, call(): pl.pallas_call(kernel, out_shape=out_shape, in_specs=[smem] * len(scalars...  5.35 us
  transfers between devices with their start and end apart: 24, of which 9 were waited for; matrix products, arithmetic and copies ran while one was open for 0% of the time, Pallas kernels for 9%

profile of v6, /device:TPU:0, one launch (start us, length us, event | category | flops | bytes accessed | tf_op | source)
XLA Modules:
  0.0 94.7 jit_solution(14166931035350787396)
XLA Ops:
  0.7 2.1 %prep.1 = bf16[8,64,512]{2,1,0:T(8,128)(2,1)} custom-call(s32[1]{0:T(128)} %bitcast.1.at, bf16[512,256]{1,0:T(8,128)(2,1)} %far_sig.1, f32[512,256]{1,0:T(8,128)} %far_taps.1, f32[1,256]{1,0:T(1,128)} %bitcast.12), custom_call_target="tpu_custom_call" | custom-call | tf_op jit(solution)/shard_map/prep/pallas_call | solution.py:403
  2.8 7.3 %all-to-all-start = ((bf16[8,64,512]{2,1,0:T(8,128)(2,1)}), bf16[8,64,512]{2,1,0:T(8,128)(2,1)S(1)}, u32[]{:S(2)}, u32[]{:S(2)}) async-start(bf16[8,64,512]{2,1,0:T(8,128)(2,1)} %prep.1), calls=%async_computation | async-start | bytes 1048576 | tf_op jit(solution)/shard_map/all_to_all | solution.py:384
  11.4 1.6 %collective-permute-start.1 = (bf16[128,256]{1,0:T(8,128)(2,1)S(1)}, bf16[128,256]{1,0:T(8,128)(2,1)S(1)}, u32[]{:S(2)}, u32[]{:S(2)}) collective-permute-start(bf16[128,256]{1,0:T(8,128)(2,1)S(1)} %get-tuple-element.43), channel_id=1, source_target_pairs={{0,2},{1,3},{2,0},{3,1},{4,6},{5,7},{6,4},{7,5},{8,10},{9,11},{10,... | collective-permute-start | bytes 196616 | tf_op jit(solution)/shard_map/ppermute | solution.py:378
  13.8 2.2 %collective-permute-done.1.refs_2_ = bf16[128,256]{1,0:T(8,128)(2,1)S(1)} collective-permute-done((bf16[128,256]{1,0:T(8,128)(2,1)S(1)}, bf16[128,256]{1,0:T(8,128)(2,1)S(1)}, u32[]{:S(2)}, u32[]{:S(2)}) %collective-permute-start.1) | collective-permute-done | bytes 65568 | tf_op jit(solution)/shard_map/ppermute | solution.py:378
  17.1 7.5 %all-to-all-done.got = bf16[8,64,512]{2,1,0:T(8,128)(2,1)S(1)} async-done(((bf16[8,64,512]{2,1,0:T(8,128)(2,1)}), bf16[8,64,512]{2,1,0:T(8,128)(2,1)S(1)}, u32[]{:S(2)}, u32[]{:S(2)}) %all-to-all-start) | async-done | bytes 524320 | tf_op jit(solution)/shard_map/all_to_all | solution.py:384
  24.5 2.7 %conv.1 = bf16[8,4,32,128]{3,2,1,0:T(8,128)(2,1)S(1)} custom-call(bf16[8,64,512]{2,1,0:T(8,128)(2,1)S(1)} %all-to-all-done.got, f32[8,512]{1,0:T(8,128)S(1)} %get-tuple-element.46.turn_cos, f32[8,512]{1,0:T(8,128)S(1)} %get-tuple-element.47.turn_sin, bf16[512,512]{1,0:T(8,128)(2,1)S(1)} %get-tuple-element.48.cos, bf16[512,512]{1,0:T(8,128)(2,1)S(1)} %get-tuple-element.49.sin), custom_call_target="tpu_custom_call" | custom-call | tf_op jit(solution)/shard_map/conv/pallas_call | solution.py:27
  27.3 14.1 %all_to_all.10 = bf16[32,32,128]{2,1,0:T(8,128)(2,1)S(1)} all-to-all(bf16[32,32,128]{2,1,0:T(8,128)(2,1)S(1)} %bitcast.7), channel_id=1, replica_groups=mesh['ctx'=8,'ch'=4] {'ctx','ch'}, dimensions={0} | all-to-all | bytes 524288 | tf_op jit(solution)/shard_map/all_to_all | solution.py:384
  42.6 3.0 %collective-permute-start.6 = (bf16[64,1024]{1,0:T(8,128)(2,1)S(1)}, bf16[64,1024]{1,0:T(8,128)(2,1)S(1)}, u32[]{:S(2)}, u32[]{:S(2)}) collective-permute-start(bf16[64,1024]{1,0:T(8,128)(2,1)S(1)} %get-tuple-element.61), channel_id=1, source_target_pairs={{0,20},{4,16},{8,28},{12,24},{16,4},{20,0},{24,12},{28,8},{1,21},{... | collective-permute-start | bytes 393224 | tf_op jit(solution)/shard_map/ppermute | solution.py:378
  45.5 1.5 %collective-permute-start.7 = (bf16[64,1024]{1,0:T(8,128)(2,1)S(1)}, bf16[64,1024]{1,0:T(8,128)(2,1)S(1)}, u32[]{:S(2)}, u32[]{:S(2)}) collective-permute-start(bf16[64,1024]{1,0:T(8,128)(2,1)S(1)} %get-tuple-element.62), channel_id=1, source_target_pairs={{0,12},{4,8},{8,4},{12,0},{16,28},{20,24},{24,20},{28,16},{1,13},{... | collective-permute-start | bytes 393224 | tf_op jit(solution)/shard_map/ppermute | solution.py:378
  49.0 2.2 %copy-done = bf16[8,1024,256]{2,1,0:T(8,128)(2,1)S(1)} copy-done((bf16[8,1024,256]{2,1,0:T(8,128)(2,1)S(1)}, bf16[8,1024,256]{2,1,0:T(8,128)(2,1)}, u32[]{:S(2)}) %copy-start) | copy-done | bytes 4194328
  51.2 2.2 %copy-done.2 = bf16[8,256,1024]{2,1,0:T(8,128)(2,1)S(1)} copy-done((bf16[8,256,1024]{2,1,0:T(8,128)(2,1)S(1)}, bf16[8,256,1024]{2,1,0:T(8,128)(2,1)}, u32[]{:S(2)}) %copy-start.2) | copy-done | bytes 4194328
  53.4 1.6 %experts.3.refs_5_.refs_0_ = bf16[64,1024]{1,0:T(8,128)(2,1)S(1)} custom-call(bf16[8,1024,256]{2,1,0:T(8,128)(2,1)S(1)} %copy-done, bf16[8,256,1024]{2,1,0:T(8,128)(2,1)S(1)} %copy-done.2, bf16[64,1024]{1,0:T(8,128)(2,1)S(1)} %get-tuple-element.65.refs_0_), custom_call_target="tpu_custom_call" | custom-call | flops 1 | bytes 1 | tf_op jit(solution)/shard_map/experts/pallas_call | solution.py:291
  55.0 1.2 %collective-permute-start.3 = (bf16[64,1024]{1,0:T(8,128)(2,1)S(1)}, bf16[64,1024]{1,0:T(8,128)(2,1)S(1)}, u32[]{:S(2)}, u32[]{:S(2)}) collective-permute-start(bf16[64,1024]{1,0:T(8,128)(2,1)S(1)} %get-tuple-element.58), channel_id=1, source_target_pairs={{0,24},{4,28},{8,16},{12,20},{16,8},{20,12},{24,0},{28,4},{1,25},{... | collective-permute-start | bytes 393224 | tf_op jit(solution)/shard_map/ppermute | solution.py:378
  56.6 2.9 %collective-permute-start.4 = (bf16[64,1024]{1,0:T(8,128)(2,1)S(1)}, bf16[64,1024]{1,0:T(8,128)(2,1)S(1)}, u32[]{:S(2)}, u32[]{:S(2)}) collective-permute-start(bf16[64,1024]{1,0:T(8,128)(2,1)S(1)} %get-tuple-element.59), channel_id=1, source_target_pairs={{0,28},{4,24},{8,20},{12,16},{16,12},{20,8},{24,4},{28,0},{1,29},{... | collective-permute-start | bytes 393224 | tf_op jit(solution)/shard_map/ppermute | solution.py:378
  60.5 2.1 %experts.4 = (bf16[64,1024]{1,0:T(8,128)(2,1)S(1)}, bf16[64,1024]{1,0:T(8,128)(2,1)S(1)}, bf16[64,1024]{1,0:T(8,128)(2,1)S(1)}, bf16[64,1024]{1,0:T(8,128)(2,1)S(1)}, bf16[64,1024]{1,0:T(8,128)(2,1)S(1)}) custom-call(bf16[8,1024,256]{2,1,0:T(8,128)(2,1)S(1)} %copy-done.1, bf16[8,256,1024]{2,1,0:T(8,128)(2,1)S(1)} %copy-done.3, ...), custom_call_target="tpu_custom_call" | custom-call | flops 1 | bytes 1 | tf_op jit(solution)/shard_map/experts/pallas_call | solution.py:291
  62.7 3.4 %collective-permute-start.15 = (bf16[64,1024]{1,0:T(8,128)(2,1)S(1)}, bf16[64,1024]{1,0:T(8,128)(2,1)S(1)}, u32[]{:S(2)}, u32[]{:S(2)}) collective-permute-start(bf16[64,1024]{1,0:T(8,128)(2,1)S(1)} %get-tuple-element.76), channel_id=1, source_target_pairs={{0,12},{4,8},{8,4},{12,0},{16,28},{20,24},{24,20},{28,16},{1,13},{... | collective-permute-start | bytes 393224 | tf_op jit(solution)/shard_map/ppermute | solution.py:378
  67.0 3.2 %collective-permute-start.17 = (bf16[64,1024]{1,0:T(8,128)(2,1)S(1)}, bf16[64,1024]{1,0:T(8,128)(2,1)S(1)}, u32[]{:S(2)}, u32[]{:S(2)}) collective-permute-start(bf16[64,1024]{1,0:T(8,128)(2,1)S(1)} %get-tuple-element.77), channel_id=1, source_target_pairs={{0,20},{4,16},{8,28},{12,24},{16,4},{20,0},{24,12},{28,8},{1,21},{... | collective-permute-start | bytes 393224 | tf_op jit(solution)/shard_map/ppermute | solution.py:378
  70.1 1.9 %experts.5 = (bf16[64,1024]{1,0:T(8,128)(2,1)S(1)}, bf16[64,1024]{1,0:T(8,128)(2,1)S(1)}) custom-call(bf16[8,1024,256]{2,1,0:T(8,128)(2,1)S(1)} %copy-done.1, bf16[8,256,1024]{2,1,0:T(8,128)(2,1)S(1)} %copy-done.3, bf16[64,1024]{1,0:T(8,128)(2,1)S(1)} %collective-permute-done.3.refs_0_, bf16[64,1024]{1,0:T(8,128)(2,1)S(1)} %collective-permute-done.4.refs_1_, ...), custom_call_target="tpu_custom_call" | custom-call | flops 1 | bytes 1 | tf_op jit(solution)/shard_map/experts/pallas_call | solution.py:291
  72.0 2.8 %collective-permute-start.18 = (bf16[64,1024]{1,0:T(8,128)(2,1)S(1)}, bf16[64,1024]{1,0:T(8,128)(2,1)S(1)}, u32[]{:S(2)}, u32[]{:S(2)}) collective-permute-start(bf16[64,1024]{1,0:T(8,128)(2,1)S(1)} %get-tuple-element.67), channel_id=1, source_target_pairs={{0,24},{4,28},{8,16},{12,20},{16,8},{20,12},{24,0},{28,4},{1,25},{... | collective-permute-start | bytes 393224 | tf_op jit(solution)/shard_map/ppermute | solution.py:378
  74.8 2.6 %collective-permute-start.19 = (bf16[64,1024]{1,0:T(8,128)(2,1)S(1)}, bf16[64,1024]{1,0:T(8,128)(2,1)S(1)}, u32[]{:S(2)}, u32[]{:S(2)}) collective-permute-start(bf16[64,1024]{1,0:T(8,128)(2,1)S(1)} %get-tuple-element.68), channel_id=1, source_target_pairs={{0,28},{4,24},{8,20},{12,16},{16,12},{20,8},{24,4},{28,0},{1,29},{... | collective-permute-start | bytes 393224 | tf_op jit(solution)/shard_map/ppermute | solution.py:378
  78.4 5.7 %collective-permute-done.16.refs_4_ = bf16[64,1024]{1,0:T(8,128)(2,1)S(1)} collective-permute-done((bf16[64,1024]{1,0:T(8,128)(2,1)S(1)}, bf16[64,1024]{1,0:T(8,128)(2,1)S(1)}, u32[]{:S(2)}, u32[]{:S(2)}) %collective-permute-start.16) | collective-permute-done | bytes 131104 | tf_op jit(solution)/shard_map/ppermute | solution.py:378
  84.2 1.3 %collective-permute-start.11 = (bf16[128,256]{1,0:T(8,128)(2,1)S(1)}, bf16[128,256]{1,0:T(8,128)(2,1)S(1)}, u32[]{:S(2)}, u32[]{:S(2)}) collective-permute-start(bf16[128,256]{1,0:T(8,128)(2,1)S(1)} %get-tuple-element.71), channel_id=1, source_target_pairs={{0,2},{1,3},{2,0},{3,1},{4,6},{5,7},{6,4},{7,5},{8,10},{9,11},{10,... | collective-permute-start | bytes 196616 | tf_op jit(solution)/shard_map/ppermute | solution.py:378
  87.4 1.8 %collective-permute-start.20 = (bf16[128,256]{1,0:T(8,128)(2,1)S(1)}, bf16[128,256]{1,0:T(8,128)(2,1)S(1)}, u32[]{:S(2)}, u32[]{:S(2)}) collective-permute-start(bf16[128,256]{1,0:T(8,128)(2,1)S(1)} %get-tuple-element.79), channel_id=1, source_target_pairs={{0,1},{1,0},{2,3},{3,2},{4,5},{5,4},{6,7},{7,6},{8,9},{9,8},{10,11... | collective-permute-start | bytes 196616 | tf_op jit(solution)/shard_map/ppermute | solution.py:378
  91.7 2.3 %collective-permute-done.21.refs_2_ = bf16[128,256]{1,0:T(8,128)(2,1)S(1)} collective-permute-done((bf16[128,256]{1,0:T(8,128)(2,1)S(1)}, bf16[128,256]{1,0:T(8,128)(2,1)S(1)}, u32[]{:S(2)}, u32[]{:S(2)}) %collective-permute-start.21) | collective-permute-done | bytes 65568 | tf_op jit(solution)/shard_map/ppermute | solution.py:378
  (55 shorter events, 14.9 us)
Async XLA Ops:
  2.8 21.8 %all-to-all-start = ((bf16[8,64,512]{2,1,0:T(8,128)(2,1)}), bf16[8,64,512]{2,1,0:T(8,128)(2,1)S(1)}, u32[]{:S(2)}, u32[]{:S(2)}) async-start(bf16[8,64,512]{2,1,0:T(8,128)(2,1)} %prep.1), calls=%async_computation | async-start | bytes 1048576 | tf_op jit(solution)/shard_map/all_to_all | solution.py:384
  11.4 2.4 %collective-permute-start = (bf16[128,256]{1,0:T(8,128)(2,1)S(1)}, bf16[128,256]{1,0:T(8,128)(2,1)S(1)}, u32[]{:S(2)}, u32[]{:S(2)}) collective-permute-start(bf16[128,256]{1,0:T(8,128)(2,1)S(1)} %get-tuple-element.42), channel_id=1, source_target_pairs={{0,1},{1,0},{2,3},{3,2},{4,5},{5,4},{6,7},{7,6},{8,9},{9,8},{10,11... | collective-permute-start | bytes 196616 | tf_op jit(solution)/shard_map/ppermute | solution.py:378
  11.4 4.5 %collective-permute-start.1 = (bf16[128,256]{1,0:T(8,128)(2,1)S(1)}, bf16[128,256]{1,0:T(8,128)(2,1)S(1)}, u32[]{:S(2)}, u32[]{:S(2)}) collective-permute-start(bf16[128,256]{1,0:T(8,128)(2,1)S(1)} %get-tuple-element.43), channel_id=1, source_target_pairs={{0,2},{1,3},{2,0},{3,1},{4,6},{5,7},{6,4},{7,5},{8,10},{9,11},{10,... | collective-permute-start | bytes 196616 | tf_op jit(solution)/shard_map/ppermute | solution.py:378
  13.0 4.0 %collective-permute-start.2 = (bf16[128,256]{1,0:T(8,128)(2,1)S(1)}, bf16[128,256]{1,0:T(8,128)(2,1)S(1)}, u32[]{:S(2)}, u32[]{:S(2)}) collective-permute-start(bf16[128,256]{1,0:T(8,128)(2,1)S(1)} %get-tuple-element.44), channel_id=1, source_target_pairs={{0,3},{1,2},{2,1},{3,0},{4,7},{5,6},{6,5},{7,4},{8,11},{9,10},{10,... | collective-permute-start | bytes 196616 | tf_op jit(solution)/shard_map/ppermute | solution.py:378
  42.2 12.8 %collective-permute-start.5 = (bf16[64,1024]{1,0:T(8,128)(2,1)S(1)}, bf16[64,1024]{1,0:T(8,128)(2,1)S(1)}, u32[]{:S(2)}, u32[]{:S(2)}) collective-permute-start(bf16[64,1024]{1,0:T(8,128)(2,1)S(1)} %get-tuple-element.60), channel_id=1, source_target_pairs={{0,16},{4,20},{8,24},{12,28},{16,0},{20,4},{24,8},{28,12},{1,17},{... | collective-permute-start | bytes 393224 | tf_op jit(solution)/shard_map/ppermute | solution.py:378
  42.6 14.1 %collective-permute-start.6 = (bf16[64,1024]{1,0:T(8,128)(2,1)S(1)}, bf16[64,1024]{1,0:T(8,128)(2,1)S(1)}, u32[]{:S(2)}, u32[]{:S(2)}) collective-permute-start(bf16[64,1024]{1,0:T(8,128)(2,1)S(1)} %get-tuple-element.61), channel_id=1, source_target_pairs={{0,20},{4,16},{8,28},{12,24},{16,4},{20,0},{24,12},{28,8},{1,21},{... | collective-permute-start | bytes 393224 | tf_op jit(solution)/shard_map/ppermute | solution.py:378
  45.5 14.0 %collective-permute-start.7 = (bf16[64,1024]{1,0:T(8,128)(2,1)S(1)}, bf16[64,1024]{1,0:T(8,128)(2,1)S(1)}, u32[]{:S(2)}, u32[]{:S(2)}) collective-permute-start(bf16[64,1024]{1,0:T(8,128)(2,1)S(1)} %get-tuple-element.62), channel_id=1, source_target_pairs={{0,12},{4,8},{8,4},{12,0},{16,28},{20,24},{24,20},{28,16},{1,13},{... | collective-permute-start | bytes 393224 | tf_op jit(solution)/shard_map/ppermute | solution.py:378
  47.0 13.5 %collective-permute-start.8 = (bf16[64,1024]{1,0:T(8,128)(2,1)S(1)}, bf16[64,1024]{1,0:T(8,128)(2,1)S(1)}, u32[]{:S(2)}, u32[]{:S(2)}) collective-permute-start(bf16[64,1024]{1,0:T(8,128)(2,1)S(1)} %get-tuple-element.63), channel_id=1, source_target_pairs={{0,8},{4,12},{8,0},{12,4},{16,24},{20,28},{24,16},{28,20},{1,9},{5... | collective-permute-start | bytes 393224 | tf_op jit(solution)/shard_map/ppermute | solution.py:378
  48.1 12.4 %collective-permute-start.9 = (bf16[64,1024]{1,0:T(8,128)(2,1)S(1)}, bf16[64,1024]{1,0:T(8,128)(2,1)S(1)}, u32[]{:S(2)}, u32[]{:S(2)}) collective-permute-start(bf16[64,1024]{1,0:T(8,128)(2,1)S(1)} %get-tuple-element.64), channel_id=1, source_target_pairs={{0,4},{4,0},{8,12},{12,8},{16,20},{20,16},{24,28},{28,24},{1,5},{5... | collective-permute-start | bytes 393224 | tf_op jit(solution)/shard_map/ppermute | solution.py:378
  55.0 11.1 %collective-permute-start.3 = (bf16[64,1024]{1,0:T(8,128)(2,1)S(1)}, bf16[64,1024]{1,0:T(8,128)(2,1)S(1)}, u32[]{:S(2)}, u32[]{:S(2)}) collective-permute-start(bf16[64,1024]{1,0:T(8,128)(2,1)S(1)} %get-tuple-element.58), channel_id=1, source_target_pairs={{0,24},{4,28},{8,16},{12,20},{16,8},{20,12},{24,0},{28,4},{1,25},{... | collective-permute-start | bytes 393224 | tf_op jit(solution)/shard_map/ppermute | solution.py:378
  56.6 10.3 %collective-permute-start.4 = (bf16[64,1024]{1,0:T(8,128)(2,1)S(1)}, bf16[64,1024]{1,0:T(8,128)(2,1)S(1)}, u32[]{:S(2)}, u32[]{:S(2)}) collective-permute-start(bf16[64,1024]{1,0:T(8,128)(2,1)S(1)} %get-tuple-element.59), channel_id=1, source_target_pairs={{0,28},{4,24},{8,20},{12,16},{16,12},{20,8},{24,4},{28,0},{1,29},{... | collective-permute-start | bytes 393224 | tf_op jit(solution)/shard_map/ppermute | solution.py:378
  62.6 9.5 %collective-permute-start.13 = (bf16[64,1024]{1,0:T(8,128)(2,1)S(1)}, bf16[64,1024]{1,0:T(8,128)(2,1)S(1)}, u32[]{:S(2)}, u32[]{:S(2)}) collective-permute-start(bf16[64,1024]{1,0:T(8,128)(2,1)S(1)} %get-tuple-element.74), channel_id=1, source_target_pairs={{0,4},{4,0},{8,12},{12,8},{16,20},{20,16},{24,28},{28,24},{1,5},{5... | collective-permute-start | bytes 393224 | tf_op jit(solution)/shard_map/ppermute | solution.py:378
  62.6 12.2 %collective-permute-start.14 = (bf16[64,1024]{1,0:T(8,128)(2,1)S(1)}, bf16[64,1024]{1,0:T(8,128)(2,1)S(1)}, u32[]{:S(2)}, u32[]{:S(2)}) collective-permute-start(bf16[64,1024]{1,0:T(8,128)(2,1)S(1)} %get-tuple-element.75), channel_id=1, source_target_pairs={{0,8},{4,12},{8,0},{12,4},{16,24},{20,28},{24,16},{28,20},{1,9},{5... | collective-permute-start | bytes 393224 | tf_op jit(solution)/shard_map/ppermute | solution.py:378
  62.7 14.7 %collective-permute-start.15 = (bf16[64,1024]{1,0:T(8,128)(2,1)S(1)}, bf16[64,1024]{1,0:T(8,128)(2,1)S(1)}, u32[]{:S(2)}, u32[]{:S(2)}) collective-permute-start(bf16[64,1024]{1,0:T(8,128)(2,1)S(1)} %get-tuple-element.76), channel_id=1, source_target_pairs={{0,12},{4,8},{8,4},{12,0},{16,28},{20,24},{24,20},{28,16},{1,13},{... | collective-permute-start | bytes 393224 | tf_op jit(solution)/shard_map/ppermute | solution.py:378
  66.1 18.1 %collective-permute-start.16 = (bf16[64,1024]{1,0:T(8,128)(2,1)S(1)}, bf16[64,1024]{1,0:T(8,128)(2,1)S(1)}, u32[]{:S(2)}, u32[]{:S(2)}) collective-permute-start(bf16[64,1024]{1,0:T(8,128)(2,1)S(1)} %get-tuple-element.66.refs_2_), channel_id=1, source_target_pairs={{0,16},{4,20},{8,24},{12,28},{16,0},{20,4},{24,8},{28,12},{1,17},{... | collective-permute-start | bytes 393224 | tf_op jit(solution)/shard_map/ppermute | solution.py:378
  67.0 19.7 %collective-permute-start.17 = (bf16[64,1024]{1,0:T(8,128)(2,1)S(1)}, bf16[64,1024]{1,0:T(8,128)(2,1)S(1)}, u32[]{:S(2)}, u32[]{:S(2)}) collective-permute-start(bf16[64,1024]{1,0:T(8,128)(2,1)S(1)} %get-tuple-element.77), channel_id=1, source_target_pairs={{0,20},{4,16},{8,28},{12,24},{16,4},{20,0},{24,12},{28,8},{1,21},{... | collective-permute-start | bytes 393224 | tf_op jit(solution)/shard_map/ppermute | solution.py:378
  72.0 14.7 %collective-permute-start.18 = (bf16[64,1024]{1,0:T(8,128)(2,1)S(1)}, bf16[64,1024]{1,0:T(8,128)(2,1)S(1)}, u32[]{:S(2)}, u32[]{:S(2)}) collective-permute-start(bf16[64,1024]{1,0:T(8,128)(2,1)S(1)} %get-tuple-element.67), channel_id=1, source_target_pairs={{0,24},{4,28},{8,16},{12,20},{16,8},{20,12},{24,0},{28,4},{1,25},{... | collective-permute-start | bytes 393224 | tf_op jit(solution)/shard_map/ppermute | solution.py:378
  74.8 11.9 %collective-permute-start.19 = (bf16[64,1024]{1,0:T(8,128)(2,1)S(1)}, bf16[64,1024]{1,0:T(8,128)(2,1)S(1)}, u32[]{:S(2)}, u32[]{:S(2)}) collective-permute-start(bf16[64,1024]{1,0:T(8,128)(2,1)S(1)} %get-tuple-element.68), channel_id=1, source_target_pairs={{0,28},{4,24},{8,20},{12,16},{16,12},{20,8},{24,4},{28,0},{1,29},{... | collective-permute-start | bytes 393224 | tf_op jit(solution)/shard_map/ppermute | solution.py:378
  77.4 12.2 %collective-permute-start.10 = (bf16[128,256]{1,0:T(8,128)(2,1)S(1)}, bf16[128,256]{1,0:T(8,128)(2,1)S(1)}, u32[]{:S(2)}, u32[]{:S(2)}) collective-permute-start(bf16[128,256]{1,0:T(8,128)(2,1)S(1)} %get-tuple-element.70), channel_id=1, source_target_pairs={{0,1},{1,0},{2,3},{3,2},{4,5},{5,4},{6,7},{7,6},{8,9},{9,8},{10,11... | collective-permute-start | bytes 196616 | tf_op jit(solution)/shard_map/ppermute | solution.py:378
  84.2 6.4 %collective-permute-start.11 = (bf16[128,256]{1,0:T(8,128)(2,1)S(1)}, bf16[128,256]{1,0:T(8,128)(2,1)S(1)}, u32[]{:S(2)}, u32[]{:S(2)}) collective-permute-start(bf16[128,256]{1,0:T(8,128)(2,1)S(1)} %get-tuple-element.71), channel_id=1, source_target_pairs={{0,2},{1,3},{2,0},{3,1},{4,6},{5,7},{6,4},{7,5},{8,10},{9,11},{10,... | collective-permute-start | bytes 196616 | tf_op jit(solution)/shard_map/ppermute | solution.py:378
  86.7 4.3 %collective-permute-start.12 = (bf16[128,256]{1,0:T(8,128)(2,1)S(1)}, bf16[128,256]{1,0:T(8,128)(2,1)S(1)}, u32[]{:S(2)}, u32[]{:S(2)}) collective-permute-start(bf16[128,256]{1,0:T(8,128)(2,1)S(1)} %get-tuple-element.72), channel_id=1, source_target_pairs={{0,3},{1,2},{2,1},{3,0},{4,7},{5,6},{6,5},{7,4},{8,11},{9,10},{10,... | collective-permute-start | bytes 196616 | tf_op jit(solution)/shard_map/ppermute | solution.py:378
  87.4 4.3 %collective-permute-start.20 = (bf16[128,256]{1,0:T(8,128)(2,1)S(1)}, bf16[128,256]{1,0:T(8,128)(2,1)S(1)}, u32[]{:S(2)}, u32[]{:S(2)}) collective-permute-start(bf16[128,256]{1,0:T(8,128)(2,1)S(1)} %get-tuple-element.79), channel_id=1, source_target_pairs={{0,1},{1,0},{2,3},{3,2},{4,5},{5,4},{6,7},{7,6},{8,9},{9,8},{10,11... | collective-permute-start | bytes 196616 | tf_op jit(solution)/shard_map/ppermute | solution.py:378
  89.1 4.8 %collective-permute-start.21 = (bf16[128,256]{1,0:T(8,128)(2,1)S(1)}, bf16[128,256]{1,0:T(8,128)(2,1)S(1)}, u32[]{:S(2)}, u32[]{:S(2)}) collective-permute-start(bf16[128,256]{1,0:T(8,128)(2,1)S(1)} %get-tuple-element.80), channel_id=1, source_target_pairs={{0,2},{1,3},{2,0},{3,1},{4,6},{5,7},{6,4},{7,5},{8,10},{9,11},{10,... | collective-permute-start | bytes 196616 | tf_op jit(solution)/shard_map/ppermute | solution.py:378
  89.6 4.4 %collective-permute-start.22 = (bf16[128,256]{1,0:T(8,128)(2,1)S(1)}, bf16[128,256]{1,0:T(8,128)(2,1)S(1)}, u32[]{:S(2)}, u32[]{:S(2)}) collective-permute-start(bf16[128,256]{1,0:T(8,128)(2,1)S(1)} %get-tuple-element.81), channel_id=1, source_target_pairs={{0,3},{1,2},{2,1},{3,0},{4,7},{5,6},{6,5},{7,4},{8,11},{9,10},{10,... | collective-permute-start | bytes 196616 | tf_op jit(solution)/shard_map/ppermute | solution.py:378
  (8 other events, 111.6 us)
